TPU v7x, 256 devices: a whole 4x4x8 slice. The times are simulated.
256 devices in a mesh: sample: 8 (over x, core), space: 32 (over y, z).
Axes of the slice: x: 4, y: 4, z: 8, core: 2. Of those that a mesh axis runs over, the one named last changes fastest.
Arguments:
- load_field: float32 [3, 128, 64, 128], P(None, 'space'), may hold values from -6 to 6
- density: float32 [128, 64, 128], P('space'), may hold values from 0.3 to 1
- mode_panels: bfloat16 [256, 32, 512], P('sample', 'space'), may hold values from -5 to 5
- mode_weight: float32 [256], replicated, may hold values from 0.01 to 0.12
- mode_germs: float32 [8, 256], replicated, may hold values from -5 to 5
Outputs:
- displacement: float32 [8, 3, 128, 64, 128], P('sample', None, 'space')
- gradient: float32 [128, 64, 128], P('space', 'sample')
- compliance: float32 [8], P('sample')
All inputs are finite; a program needn't handle non-finite values.
Results may differ from a plain program's by a relative error of at most 0.00068.
Values sent between devices are 32-bit elements; how exact they have to be, the bound alone decides.
No kernel may reach another device: no remote copies, remote signals or barrier semaphores. Data moves between devices by JAX's collectives and lax.ppermute only.
A program may use at most 64 MiB of HBM per device.

v0:
```python
import math

import jax
import jax.numpy as jnp
import numpy as np
from jax import lax
from jax.sharding import PartitionSpec as P

ITERS = 2


highest_precision = lax.Precision.HIGHEST


def padded_2(block, sides, width):
    for axis, dim in sides:
        count = lax.axis_size(axis)
        forward = [(i, i + 1) for i in range(count - 1)]
        backward = [(target, source) for source, target in forward]
        low = lax.ppermute(
            lax.slice_in_dim(block, block.shape[dim] - width, None, axis=dim), axis, forward
        )
        high = lax.ppermute(lax.slice_in_dim(block, 0, width, axis=dim), axis, backward)
        block = jnp.concatenate([low, block, high], axis=dim)
    return block


def passed_along(value, axis, steps):
    count = lax.axis_size(axis)
    initial, last = (max(0, -steps), min(count, count - steps))
    return lax.ppermute(value, axis, [(source, source + steps) for source in range(initial, last)])


def stiffness_table():
    poisson = 0.3
    lame_first = poisson / ((1.0 + poisson) * (1.0 - 2.0 * poisson))
    shear_modulus = 1.0 / (2.0 * (1.0 + poisson))
    moduli = np.zeros((6, 6))
    moduli[:3, :3] = lame_first
    for direction in range(3):
        moduli[direction, direction] += 2.0 * shear_modulus
        moduli[3 + direction, 3 + direction] = shear_modulus
    points = (0.5 - 0.5 / math.sqrt(3.0), 0.5 + 0.5 / math.sqrt(3.0))
    shear_pairs = ((0, 1), (1, 2), (0, 2))
    matrix = np.zeros((24, 24))
    for gauss_one in points:
        for gauss_two in points:
            for gauss_three in points:
                location = (gauss_one, gauss_two, gauss_three)
                strain = np.zeros((6, 24))
                for corner in range(8):
                    corner_bits = (corner >> 2 & 1, corner >> 1 & 1, corner & 1)
                    values = [
                        location[direction] if corner_bits[direction] else 1.0 - location[direction]
                        for direction in range(3)
                    ]
                    slopes = []
                    for direction in range(3):
                        slope_value = 1.0 if corner_bits[direction] else -1.0
                        for others in range(3):
                            if others != direction:
                                slope_value = slope_value * values[others]
                        slopes.append(slope_value)
                    for direction in range(3):
                        strain[direction, 3 * corner + direction] = slopes[direction]
                    for pair_index in range(3):
                        left_axis, right_axis = shear_pairs[pair_index]
                        strain[3 + pair_index, 3 * corner + left_axis] = slopes[right_axis]
                        strain[3 + pair_index, 3 * corner + right_axis] = slopes[left_axis]
                matrix = matrix + strain.T @ moduli @ strain / 8.0
    return matrix


def corner_offsets():
    return [(corner >> 2 & 1, corner >> 1 & 1, corner & 1) for corner in range(8)]


def hat_weights(fine_count, coarse_count, offset):
    fine_pos = (jnp.arange(fine_count).astype(jnp.float32) + 0.5) / 4.0 - 0.5 + offset
    coarse_pos = jnp.arange(coarse_count).astype(jnp.float32)
    return jnp.maximum(0.0, 1.0 - jnp.abs(fine_pos[:, None] - coarse_pos[None, :]))


def upsample(coarse_grid, weight_z, weight_x, weight_y):
    along_y = jnp.einsum("cde,ye->cdy", coarse_grid, weight_y, precision=highest_precision)
    along_x = jnp.einsum("cdy,xd->cxy", along_y, weight_x, precision=highest_precision)
    return jnp.einsum("cxy,zc->zxy", along_x, weight_z, precision=highest_precision)


def diagonal_of(elastic_ext, matrix_diag, depth_count):
    rows_x = elastic_ext.shape[1]
    cols_y = elastic_ext.shape[2]
    padded = jnp.pad(elastic_ext, ((0, 0), (1, 0), (1, 0)))
    summed = jnp.zeros((3, depth_count, rows_x, cols_y), jnp.float32)
    for corner, (shift_z, shift_x, shift_y) in enumerate(corner_offsets()):
        window = padded[
            1 - shift_z : 1 - shift_z + depth_count,
            1 - shift_x : 1 - shift_x + rows_x,
            1 - shift_y : 1 - shift_y + cols_y,
        ]
        summed = summed + matrix_diag[corner][:, None, None, None] * window[None]
    return summed


def corner_stack(extended, depth_count):
    rows_x = extended.shape[2]
    cols_y = extended.shape[3]
    padded = jnp.pad(extended, ((0, 0), (0, 0), (0, 1), (0, 1)))
    pieces = [
        padded[
            :,
            shift_z : shift_z + depth_count + 1,
            shift_x : shift_x + rows_x,
            shift_y : shift_y + cols_y,
        ]
        for shift_z, shift_x, shift_y in corner_offsets()
    ]
    return jnp.stack(pieces).reshape(24, depth_count + 1, rows_x, cols_y)


def apply_operator(extended, elastic_ext, matrix, depth_count):
    rows_x = extended.shape[2]
    cols_y = extended.shape[3]
    stacked = corner_stack(extended, depth_count)
    forces = jnp.dot(matrix, stacked.reshape(24, -1), precision=highest_precision)
    forces = forces.reshape(8, 3, depth_count + 1, rows_x, cols_y) * elastic_ext[None, None]
    padded = jnp.pad(forces, ((0, 0), (0, 0), (0, 0), (1, 0), (1, 0)))
    summed = jnp.zeros((3, depth_count, rows_x, cols_y), jnp.float32)
    for corner, (shift_z, shift_x, shift_y) in enumerate(corner_offsets()):
        summed = (
            summed
            + padded[
                corner,
                :,
                1 - shift_z : 1 - shift_z + depth_count,
                1 - shift_x : 1 - shift_x + rows_x,
                1 - shift_y : 1 - shift_y + cols_y,
            ]
        )
    return summed


def element_energy(extended, matrix, depth_count):
    rows_x = extended.shape[2]
    cols_y = extended.shape[3]
    stacked = corner_stack(extended, depth_count)[:, 1:]
    flat_stack = stacked.reshape(24, -1)
    forces = jnp.dot(matrix, flat_stack, precision=highest_precision)
    return jnp.sum(flat_stack * forces, axis=0).reshape(depth_count, rows_x, cols_y)


def per_device(load_field, density, mode_panels, mode_weight, mode_germs):
    matrix = jnp.asarray(stiffness_table(), jnp.float32)
    matrix_diag = jnp.diagonal(matrix).reshape(8, 3)
    depth_count = density.shape[0]
    rows_x = density.shape[1]
    cols_y = density.shape[2]
    own_modes = mode_panels.shape[0]
    coarse_planes = mode_panels.shape[1]
    coefficients = (mode_weight[None, :] * mode_germs).astype(jnp.bfloat16)
    local_coeff = lax.dynamic_slice_in_dim(
        coefficients, lax.axis_index("sample") * own_modes, own_modes, 1
    )
    partial_field = jnp.dot(
        local_coeff, mode_panels.reshape(own_modes, -1), preferred_element_type=jnp.float32
    )
    coarse_field = lax.psum_scatter(partial_field, "sample", scatter_dimension=0, tiled=True)
    coarse_ext = padded_2(coarse_field, (("space", 0),), 1)
    coarse_grid = coarse_ext.reshape(coarse_planes + 2, rows_x // 4, cols_y // 4)
    log_field = upsample(
        coarse_grid,
        hat_weights(depth_count, coarse_planes + 2, 1.0),
        hat_weights(rows_x, rows_x // 4, 0.0),
        hat_weights(cols_y, cols_y // 4, 0.0),
    )
    elastic = jnp.exp(log_field) * (0.001 + density**3)
    below = passed_along(elastic[depth_count - 1 :], "space", 1)
    elastic_ext = jnp.concatenate([below, elastic], axis=0)
    jacobi_diag = diagonal_of(elastic_ext, matrix_diag, depth_count)

    def node_rim(nodal):
        return padded_2(nodal, (("space", 1),), 1)

    def dot_residual(left_vec, right_vec):
        return lax.psum(jnp.sum(left_vec * right_vec), "space")

    displacement = jnp.zeros_like(load_field)
    work_terms = []
    residual = load_field
    precond_res = residual / jacobi_diag
    direction = precond_res
    precond_dot = dot_residual(residual, precond_res)
    for iteration in range(ITERS):
        direction_ext = node_rim(direction)
        image_vec = apply_operator(direction_ext, elastic_ext, matrix, depth_count)
        step_length = precond_dot / lax.psum(jnp.sum(direction * image_vec), "space")
        displacement = displacement + step_length * direction
        work_terms.append(step_length * precond_dot)
        if iteration + 1 < ITERS:
            residual = residual - step_length * image_vec
            precond_res = residual / jacobi_diag
            next_dot = dot_residual(residual, precond_res)
            direction = precond_res + next_dot / precond_dot * direction
            precond_dot = next_dot
    final_ext = node_rim(displacement)
    energy = element_energy(final_ext, matrix, depth_count)
    compliance = lax.psum(jnp.sum(load_field * displacement), "space")
    partial_grad = -(3.0 / lax.axis_size("sample")) * density**2 * jnp.exp(log_field) * energy
    gradient = lax.psum_scatter(partial_grad, "sample", scatter_dimension=1, tiled=True)
    return (displacement[None], gradient, jnp.reshape(compliance, (1,)))


def solution(mesh):
    placed = (
        P(None, "space", None, None),
        P("space", None, None),
        P("sample", "space", None),
        P(),
        P(),
    )
    return jax.shard_map(
        per_device,
        mesh=mesh,
        in_specs=placed,
        out_specs=(P("sample", None, "space", None, None), P("space", "sample", None), P("sample")),
        check_vma=False,
    )
```

profile of v0, /device:TPU:32, one launch (start us, length us, event | category | flops | bytes accessed | tf_op | source)
XLA Modules:
  0.0 436.3 jit_solution(7911127369032044501)
XLA Ops:
  8.0 0.9 fusion.56
  8.9 25.6 %all-reduce.6 = f32[8,512]{1,0:T(8,128)S(1)} all-reduce(f32[8,512]{1,0:T(8,128)S(1)} %fusion.56), channel_id=2, replica_groups=mesh['sample'=8,'space'=32] {'sample'}, use_global_device_ids=true, to_apply=%region_0.1.clone | all-reduce | flops 4096 | bytes 32768
  34.5 1.3 dynamic-slice
  36.4 2.0 collective-permute-start.1
  38.4 3.8 collective-permute-start
  42.3 1.5 gather_fusion
  45.0 0.9 fusion.51
  46.0 3.8 collective-permute-start.2
  49.9 1.9 collective-permute-done.2
  52.0 1.3 fusion.48
  53.3 4.6 %collective-permute-start.3 = (f32[3,1,64,128]{3,2,1,0:T(8,128)S(1)}, f32[3,1,64,128]{3,2,1,0:T(8,128)S(1)}, u32[]{:S(2)}, u32[]{:S(2)}) collective-permute-start(f32[3,1,64,128]{3,2,1,0:T(8,128)S(1)} %get-tuple-element.29), channel_id=1, source_target_pairs={{0,1},{1,2},{2,3},{3,4},{4,5},{5,6},{6,7},{7,8},{8,9},{9,10},{10,1... | collective-permute-start | bytes 294920 | tf_op jit(solution)/shard_map/ppermute | solution.py:20
  58.0 1.9 collective-permute-start.4
  60.1 0.8 fusion.24
  61.0 4.6 %collective-permute-done.4 = f32[3,1,64,128]{3,2,1,0:T(8,128)S(1)} collective-permute-done((f32[3,1,64,128]{3,2,1,0:T(8,128)S(1)}, f32[3,1,64,128]{3,2,1,0:T(8,128)S(1)}, u32[]{:S(2)}, u32[]{:S(2)}) %collective-permute-start.4) | collective-permute-done | bytes 98336 | tf_op jit(solution)/shard_map/ppermute | solution.py:23
  65.7 1.0 fusion.23
  66.7 0.8 fusion.22
  67.5 1.0 fusion.21
  68.5 0.8 fusion.25
  69.4 1.0 fusion.20
  70.3 0.8 fusion.19
  71.2 1.0 fusion.18
  72.2 5.2 %reshape_reshape.6 = f32[24,40960]{1,0:T(8,128)} reshape(f32[8,3,5,64,128]{4,3,2,1,0:T(8,128)} %fusion.18) | data formatting | bytes 7864320 | tf_op jit(solution)/shard_map/reshape;reshape | solution.py:125
  77.3 5.5 %convolution_bitcast_fusion.1 = f32[3,8,320,128]{3,1,2,0:T(8,128)S(1)} fusion(f32[24,24]{1,0:T(8,128)S(1)} %copy-done.1, f32[24,40960]{1,0:T(8,128)} %reshape_reshape.6), kind=kOutput, calls=%fused_computation.17 | convolution fusion | flops 283115520 | bytes 7866624 | tf_op jit(solution)/shard_map/dot_general | solution.py:125
  84.5 1.2 fusion.45
  85.7 72.4 %all-reduce.8 = (f32[]{:T(128)}, f32[]{:T(128)}) all-reduce(f32[]{:T(128)} %get-tuple-element.16, f32[]{:T(128)} %get-tuple-element.15), channel_id=1, replica_groups=mesh['sample'=8,'space'=32] {'space'}, use_global_device_ids=true, to_apply=%region_2.3 | all-reduce | flops 2 | bytes 16 | tf_op jit(solution)/shard_map/psum | solution.py:185
  159.5 1.0 multiply_reduce_fusion.1
  160.4 73.2 %psum.37 = f32[]{:T(128)} all-reduce(f32[]{:T(128)} %get-tuple-element.21), channel_id=1, replica_groups=mesh['sample'=8,'space'=32] {'space'}, use_global_device_ids=true, to_apply=%region_6.7 | all-reduce | flops 1 | bytes 8 | tf_op jit(solution)/shard_map/psum | solution.py:185
  235.3 1.9 collective-permute-start.5
  237.2 4.1 collective-permute-start.6
  241.8 0.8 fusion.26
  242.6 1.1 collective-permute-done.6
  243.9 1.0 fusion.17
  244.8 0.8 fusion.16
  245.7 1.0 fusion.15
  246.7 0.9 fusion.27
  247.5 1.0 fusion.14
  248.5 0.8 fusion.13
  249.4 1.0 fusion.12
  250.3 5.2 %reshape_reshape.7 = f32[24,40960]{1,0:T(8,128)} reshape(f32[8,3,5,64,128]{4,3,2,1,0:T(8,128)} %fusion.12) | data formatting | bytes 7864320 | tf_op jit(solution)/shard_map/reshape;reshape | solution.py:125
  255.5 5.5 %convolution_bitcast_fusion = f32[3,8,320,128]{3,1,2,0:T(8,128)S(1)} fusion(f32[24,24]{1,0:T(8,128)S(1)} %copy-done.1, f32[24,40960]{1,0:T(8,128)} %reshape_reshape.7), kind=kOutput, calls=%fused_computation.16 | convolution fusion | flops 283115520 | bytes 7866624 | tf_op jit(solution)/shard_map/dot_general | solution.py:125
  262.4 1.1 fusion.44
  263.5 72.2 %psum.38 = f32[]{:T(128)} all-reduce(f32[]{:T(128)} %fusion.44), channel_id=1, replica_groups=mesh['sample'=8,'space'=32] {'space'}, use_global_device_ids=true, to_apply=%region_8.9 | all-reduce | flops 1 | bytes 8 | tf_op jit(solution)/shard_map/psum | solution.py:196
  337.1 1.0 multiply_reduce_fusion
  338.1 1.9 collective-permute-start.7
  340.0 4.1 collective-permute-start.8
  344.6 1.9 collective-permute-done.8
  348.1 6.4 %fusion.2 = f32[32768]{0:T(1024)S(1)} fusion(f32[24,24]{1,0:T(8,128)S(1)} %copy-done.1, f32[3,8,256,128]{3,2,1,0:T(8,128)S(1)} %bitcast.161), kind=kOutput, calls=%fused_computation.20 | convolution fusion | flops 228032512 | bytes 3279104 | tf_op jit(solution)/shard_map/dot_general | solution.py:148
  355.9 72.2 %psum.39 = f32[1]{0:T(128)} all-reduce(f32[1]{0:T(128)} %bitcast.35), channel_id=1, replica_groups=mesh['sample'=8,'space'=32] {'space'}, use_global_device_ids=true, to_apply=%region_12.13 | all-reduce | flops 1 | bytes 8 | tf_op jit(solution)/shard_map/psum | solution.py:207
  (60 shorter events, 11.4 us)
Async XLA Ops:
  7.2 0.8 copy-start
  7.2 421.0 %all-reduce.11.cloned.1.call-start = ((), (), s32[]{:S(2)}) async-start(), calls=%async_computation | async-start | bytes 262144
  36.4 7.5 %collective-permute-start.1 = (f32[1,512]{1,0:T(1,128)S(1)}, f32[1,512]{1,0:T(1,128)S(1)}, u32[]{:S(2)}, u32[]{:S(2)}) collective-permute-start(f32[1,512]{1,0:T(1,128)S(1)} %constant_dynamic-slice_fusion.1), channel_id=1, source_target_pairs={{1,0},{2,1},{3,2},{4,3},{5,4},{6,5},{7,6},{8,7},{9,8},{10,9},{11,1... | collective-permute-start | bytes 6152 | tf_op jit(solution)/shard_map/ppermute | solution.py:23
  38.4 5.5 %collective-permute-start = (f32[1,512]{1,0:T(1,128)S(1)}, f32[1,512]{1,0:T(1,128)S(1)}, u32[]{:S(2)}, u32[]{:S(2)}) collective-permute-start(f32[1,512]{1,0:T(1,128)S(1)} %constant_dynamic-slice_fusion.1), channel_id=1, source_target_pairs={{0,1},{1,2},{2,3},{3,4},{4,5},{5,6},{6,7},{7,8},{8,9},{9,10},{10,1... | collective-permute-start | bytes 6152 | tf_op jit(solution)/shard_map/ppermute | solution.py:20
  46.0 5.8 %collective-permute-start.2 = (f32[1,64,128]{2,1,0:T(8,128)S(1)}, f32[1,64,128]{2,1,0:T(8,128)S(1)}, u32[]{:S(2)}, u32[]{:S(2)}) collective-permute-start(f32[1,64,128]{2,1,0:T(8,128)S(1)} %slice.263), channel_id=1, source_target_pairs={{0,1},{1,2},{2,3},{3,4},{4,5},{5,6},{6,7},{7,8},{8,9},{9,10},{10,1... | collective-permute-start | bytes 98312 | tf_op jit(solution)/shard_map/ppermute | solution.py:31
  53.3 6.8 %collective-permute-start.3 = (f32[3,1,64,128]{3,2,1,0:T(8,128)S(1)}, f32[3,1,64,128]{3,2,1,0:T(8,128)S(1)}, u32[]{:S(2)}, u32[]{:S(2)}) collective-permute-start(f32[3,1,64,128]{3,2,1,0:T(8,128)S(1)} %get-tuple-element.29), channel_id=1, source_target_pairs={{0,1},{1,2},{2,3},{3,4},{4,5},{5,6},{6,7},{7,8},{8,9},{9,10},{10,1... | collective-permute-start | bytes 294920 | tf_op jit(solution)/shard_map/ppermute | solution.py:20
  58.0 7.6 %collective-permute-start.4 = (f32[3,1,64,128]{3,2,1,0:T(8,128)S(1)}, f32[3,1,64,128]{3,2,1,0:T(8,128)S(1)}, u32[]{:S(2)}, u32[]{:S(2)}) collective-permute-start(f32[3,1,64,128]{3,2,1,0:T(8,128)S(1)} %get-tuple-element.28), channel_id=1, source_target_pairs={{1,0},{2,1},{3,2},{4,3},{5,4},{6,5},{7,6},{8,7},{9,8},{10,9},{11,1... | collective-permute-start | bytes 294920 | tf_op jit(solution)/shard_map/ppermute | solution.py:23
  72.2 5.2 %copy-start.1 = (f32[24,24]{1,0:T(8,128)S(1)}, f32[24,24]{1,0:T(8,128)}, u32[]{:S(2)}) copy-start(f32[24,24]{1,0:T(8,128)} %constant.50.clone) | copy-start | bytes 6916
  83.5 1.0 copy-start.2
  235.3 6.5 %collective-permute-start.5 = (f32[3,1,64,128]{3,2,1,0:T(8,128)S(1)}, f32[3,1,64,128]{3,2,1,0:T(8,128)S(1)}, u32[]{:S(2)}, u32[]{:S(2)}) collective-permute-start(f32[3,1,64,128]{3,2,1,0:T(8,128)S(1)} %get-tuple-element.27), channel_id=1, source_target_pairs={{0,1},{1,2},{2,3},{3,4},{4,5},{5,6},{6,7},{7,8},{8,9},{9,10},{10,1... | collective-permute-start | bytes 294920 | tf_op jit(solution)/shard_map/ppermute | solution.py:20
  237.2 6.5 %collective-permute-start.6 = (f32[3,1,64,128]{3,2,1,0:T(8,128)S(1)}, f32[3,1,64,128]{3,2,1,0:T(8,128)S(1)}, u32[]{:S(2)}, u32[]{:S(2)}) collective-permute-start(f32[3,1,64,128]{3,2,1,0:T(8,128)S(1)} %get-tuple-element.26), channel_id=1, source_target_pairs={{1,0},{2,1},{3,2},{4,3},{5,4},{6,5},{7,6},{8,7},{9,8},{10,9},{11,1... | collective-permute-start | bytes 294920 | tf_op jit(solution)/shard_map/ppermute | solution.py:23
  338.1 9.3 %copy-start.3 = (f32[3,4,64,128]{3,2,1,0:T(8,128)}, f32[3,4,64,128]{3,2,1,0:T(8,128)S(1)}, u32[]{:S(2)}) copy-start(f32[3,4,64,128]{3,2,1,0:T(8,128)S(1)} %get-tuple-element.20) | copy-start | bytes 1179652
  338.1 6.5 %collective-permute-start.7 = (f32[3,1,64,128]{3,2,1,0:T(8,128)S(1)}, f32[3,1,64,128]{3,2,1,0:T(8,128)S(1)}, u32[]{:S(2)}, u32[]{:S(2)}) collective-permute-start(f32[3,1,64,128]{3,2,1,0:T(8,128)S(1)} %get-tuple-element.25), channel_id=1, source_target_pairs={{0,1},{1,2},{2,3},{3,4},{4,5},{5,6},{6,7},{7,8},{8,9},{9,10},{10,1... | collective-permute-start | bytes 294920 | tf_op jit(solution)/shard_map/ppermute | solution.py:20
  340.0 6.6 %collective-permute-start.8 = (f32[3,1,64,128]{3,2,1,0:T(8,128)S(1)}, f32[3,1,64,128]{3,2,1,0:T(8,128)S(1)}, u32[]{:S(2)}, u32[]{:S(2)}) collective-permute-start(f32[3,1,64,128]{3,2,1,0:T(8,128)S(1)} %get-tuple-element.24), channel_id=1, source_target_pairs={{1,0},{2,1},{3,2},{4,3},{5,4},{6,5},{7,6},{8,7},{9,8},{10,9},{11,1... | collective-permute-start | bytes 294920 | tf_op jit(solution)/shard_map/ppermute | solution.py:23
  347.6 6.8 %copy-start.4 = (f32[4,64,128]{2,1,0:T(8,128)S(1)}, f32[4,64,128]{2,1,0:T(8,128)}, u32[]{:S(2)}) copy-start(f32[4,64,128]{2,1,0:T(8,128)} %param.7) | copy-start | bytes 393220
Sparse Core Ops, SparseCore 0:
  355.4 58.0 all-reduce.10
where the time goes:
time: 437 us; the launch traced here: 436 us
  blocking collectives  316 us (72%)
  local copies, waits for them, and re-layouts  30.9 us (7%)
  starting transfers between devices  28.3 us (6%)
  matrix products  19.2 us (4%)
  between operations  19.1 us (4%)
  other arithmetic  12.4 us (3%)
  waiting for transfers between devices  10.8 us (2%)
    psum x2, blocking collectives, dot_residual(): return lax.psum(jnp.sum(left_vec * right_vec), 'space')  146 us
    psum x1, blocking collectives, per_device(): lax.psum(jnp.sum(direction * image_vec), 'space')  72.2 us
    psum x1, blocking collectives, per_device(): compliance = lax.psum(jnp.sum(load_field * displacement), 'space')  72.2 us
    unnamed x1, blocking collectives  25.6 us
    unnamed x31, local copies, waits for them, and re-layouts  14.8 us
    ppermute x4, starting transfers between devices, padded_2(): lax.ppermute(lax.slice_in_dim(block, block.shape[dim] - width, None, axis...  12.3 us
    ppermute x4, starting transfers between devices, padded_2(): lax.ppermute(lax.slice_in_dim(block, 0, width, axis=dim), axis, backward)  12.2 us
    dot_general x2, matrix products, apply_operator(): jnp.dot(matrix, stacked.reshape(24, -1), precision=highest_precision)  10.9 us
  transfers between devices with their start and end apart: 10, of which 7 were waited for; matrix products, arithmetic and copies ran while one was open for 1% of the time, Pallas kernels for 0%

commit v1 on v0

v1 whole, which is shorter than its diff:
```python
import itertools

import jax
import jax.numpy as jnp
import numpy as np
from jax import lax
from jax.experimental import pallas as pl
from jax.experimental.pallas import tpu as pltpu
from jax.sharding import PartitionSpec as P

BOTH = ("sample", "space")
POISSON = 0.3
LAME = POISSON / ((1.0 + POISSON) * (1.0 - 2.0 * POISSON))
SHEAR = 1.0 / (2.0 * (1.0 + POISSON))
DIAGONAL = (LAME + 2.0 * SHEAR) / 9.0 + 2.0 * SHEAR / 9.0
MODES = tuple(itertools.product((0, 1), repeat=3))
VMEM_LIMIT = 48 * 1024 * 1024


def vmem_spec():
    return pl.BlockSpec(memory_space=pltpu.VMEM)


def f32(*shape):
    return jax.ShapeDtypeStruct(shape, jnp.float32)


def split3(value):
    high = value.astype(jnp.bfloat16)
    rest = value - high.astype(jnp.float32)
    mid = rest.astype(jnp.bfloat16)
    low = (rest - mid.astype(jnp.float32)).astype(jnp.bfloat16)
    return high, mid, low


def dot32(left, right):
    return jnp.dot(left, right, preferred_element_type=jnp.float32)


def weight_tables(depth, rows, cols):
    def hat(positions, cells):
        return np.maximum(0.0, 1.0 - np.abs(positions[:, None] - cells[None, :]))

    along_x = hat((np.arange(rows) + 0.5) / 4.0 - 0.5, np.arange(rows // 4))
    along_y = hat((np.arange(cols) + 0.5) / 4.0 - 0.5, np.arange(cols // 4))
    along_z = hat((np.arange(depth + 4) - 2 + 0.5) / 4.0 - 0.5, np.arange(-1, 2))
    spread_y = np.tile(along_y.T, (rows // 4, 1))
    spread_zx = np.einsum("pc,xd->pxcd", along_z, along_x).reshape((depth + 4) * rows, -1)
    return spread_y.astype(jnp.bfloat16), spread_zx.astype(jnp.bfloat16)


def first_kernel(
    weight_ref, germs_ref, panels_ref, density_ref, load_ref,
    keep_ref, send1_ref, send2_ref, send3_ref, up_ref, down_ref,
):
    sample = lax.axis_index("sample")
    chip, core = sample // 2, sample % 2
    own_modes = panels_ref.shape[0]
    modes = germs_ref.shape[1]
    coefficients = (weight_ref[...] * germs_ref[...]).astype(jnp.bfloat16)
    mode_at = lax.broadcasted_iota(jnp.int32, (modes, own_modes), 0)
    slot_at = lax.broadcasted_iota(jnp.int32, (modes, own_modes), 1)
    pick = jnp.where(mode_at == slot_at + sample * own_modes, 1.0, 0.0).astype(jnp.bfloat16)
    own_coeff = dot32(coefficients, pick).astype(jnp.bfloat16)
    partial = dot32(own_coeff, panels_ref[...])
    row_at = lax.broadcasted_iota(jnp.int32, partial.shape, 0)
    for step, out_ref in enumerate((keep_ref, send1_ref, send2_ref, send3_ref)):
        target = (chip + step) % 4
        for place in range(2):
            row = 2 * target + (core if place == 0 else 1 - core)
            out_ref[place : place + 1] = jnp.sum(
                jnp.where(row_at == row, partial, 0.0), axis=0, keepdims=True
            )
    up_ref[0:2] = density_ref[2:4]
    down_ref[0:2] = density_ref[0:2]
    for comp in range(3):
        up_ref[2 + comp] = load_ref[comp, 3]
        down_ref[2 + 2 * comp : 4 + 2 * comp] = load_ref[comp, 0:2]


def shift_ahead(value, axis, mask):
    return jnp.where(mask, 0.0, pltpu.roll(value, value.shape[axis] - 1, axis))


def shift_back(value, axis, mask):
    return jnp.where(mask, 0.0, pltpu.roll(value, 1, axis))


def spread_plane(value, last_row, last_col):
    ahead = shift_ahead(value, 1, last_col)
    by_y = (value + ahead, ahead - value)
    aheads = [shift_ahead(part, 0, last_row) for part in by_y]
    sums = [part + other for part, other in zip(by_y, aheads)]
    diffs = [other - part for part, other in zip(by_y, aheads)]
    return sums + diffs


def element_modes(lower, upper):
    hat = {}
    for comp in range(3):
        for mode_x, mode_y in itertools.product((0, 1), repeat=2):
            at = 4 * comp + 2 * mode_x + mode_y
            if mode_x or mode_y:
                hat[comp, (0, mode_x, mode_y)] = lower[at] + upper[at]
            hat[comp, (1, mode_x, mode_y)] = upper[at] - lower[at]
    return hat


def modal_forces(hat):
    forces = {}
    for comp in range(3):
        for mode in MODES:
            count = sum(mode)
            if not count:
                continue
            own = (LAME + 2.0 * SHEAR) * mode[comp] + SHEAR * (count - mode[comp])
            value = (own / (16.0 * 3.0 ** (count - 1))) * hat[comp, mode]
            for other in range(3):
                if other == comp or mode[comp] + mode[other] != 1:
                    continue
                third = 3 - comp - other
                swapped = list(mode)
                swapped[comp], swapped[other] = mode[other], mode[comp]
                factor = (LAME if mode[comp] else SHEAR) / (16.0 * 3.0 ** mode[third])
                value = value + factor * hat[other, tuple(swapped)]
            forces[comp, mode] = value
    return forces


def modal_product(left, right):
    total = None
    for key, value in right.items():
        term = left[key] * value
        total = term if total is None else total + term
    return total


def fold(plane):
    return jnp.sum(plane.reshape(-1, 8, plane.shape[-1]), axis=0)


def middle_kernel(
    sums_ref, here_ref, low_other_ref, high_other_ref, low_same_ref, high_same_ref,
    density_ref, load_ref, below_ref, above_ref, spread_y_ref, spread_zx_ref,
    z_ref, y_ref, quad_ref, dots_ref,
    elastic, fields, fields_y, forces_at, inverse,
):
    slab = lax.axis_index("space")
    slabs = lax.axis_size("space")
    depth, rows, cols = density_ref.shape
    row_at = lax.broadcasted_iota(jnp.int32, (rows, cols), 0)
    col_at = lax.broadcasted_iota(jnp.int32, (rows, cols), 1)
    first_row, last_row = row_at == 0, row_at == rows - 1
    first_col, last_col = col_at == 0, col_at == cols - 1

    planes = (
        low_other_ref[...] + low_same_ref[...],
        sums_ref[0:1] + here_ref[...],
        high_other_ref[...] + high_same_ref[...],
    )
    cells = planes[0].shape[1]
    coarse_x, coarse_y = rows // 4, cols // 4
    cell_at = lax.broadcasted_iota(jnp.int32, (coarse_x, cells), 1)
    line_at = lax.broadcasted_iota(jnp.int32, (coarse_x, cells), 0)
    on_line = cell_at // coarse_y == line_at
    lines = jnp.concatenate(
        [jnp.where(on_line, jnp.broadcast_to(plane, on_line.shape), 0.0) for plane in planes], axis=0
    )
    spread_y = spread_y_ref[...]
    high, mid, low = (dot32(part, spread_y) for part in split3(lines))
    along_y = high + (mid + low)
    spread_zx = spread_zx_ref[...]
    high, mid, low = (dot32(spread_zx, part) for part in split3(along_y))
    growth = jnp.exp(high + (mid + low)).reshape(depth + 4, rows, cols)

    for place in range(depth + 4):
        if place < 2:
            dense = below_ref[place]
        elif place < depth + 2:
            dense = density_ref[place - 2]
        else:
            dense = above_ref[place - depth - 2]
        modulus = growth[place] * (0.001 + dense * dense * dense)
        if place < 2:
            modulus = jnp.where(slab > 0, modulus, 0.0)
        if place >= depth + 2:
            modulus = jnp.where(slab < slabs - 1, modulus, 0.0)
        elastic[place] = modulus

    before = None
    dot_load = jnp.zeros((8, cols), jnp.float32)
    for place in range(depth + 4):
        modulus = elastic[place]
        along = modulus + shift_back(modulus, 1, first_col)
        along = along + shift_back(along, 0, first_row)
        if place:
            diagonal = DIAGONAL * (along + before)
            if place == 1:
                diagonal = jnp.where(slab > 0, diagonal, 1.0)
            if place == depth + 3:
                diagonal = jnp.where(slab < slabs - 1, diagonal, 1.0)
            inverse_here = 1.0 / diagonal
            if 2 <= place <= depth + 2:
                inverse[place - 2] = inverse_here
            for comp in range(3):
                if place < 2:
                    load = below_ref[2 + comp]
                elif place < depth + 2:
                    load = load_ref[comp, place - 2]
                else:
                    load = above_ref[2 + 2 * comp + place - depth - 2]
                start = load * inverse_here
                if 2 <= place < depth + 2:
                    z_ref[comp, place - 2] = start
                    dot_load = dot_load + fold(load * start)
                for at, part in enumerate(spread_plane(start, last_row, last_col)):
                    fields[place - 1, 4 * comp + at] = part
        before = along

    def first_product(chunk, dot_zz):
        span = pl.ds(pl.multiple_of(chunk * 8, 8), 8)
        lower = [fields[0, at, span] for at in range(12)]
        carried = None
        for place in range(1, depth + 3):
            upper = [fields[place, at, span] for at in range(12)]
            hat = element_modes(lower, upper)
            forces = modal_forces(hat)
            modulus = elastic[place, span]
            if 2 <= place < depth + 2:
                energy = modal_product(hat, forces)
                quad_ref[0, place - 2, span] = energy
                dot_zz = dot_zz + modulus * energy
            forces = {key: value * modulus for key, value in forces.items()}
            passed = []
            for comp in range(3):
                for mode_x, mode_y in itertools.product((0, 1), repeat=2):
                    at = 4 * comp + 2 * mode_x + mode_y
                    rise = forces[comp, (1, mode_x, mode_y)]
                    if mode_x or mode_y:
                        level = forces[comp, (0, mode_x, mode_y)]
                        near, far = level - rise, level + rise
                    else:
                        near, far = -rise, rise
                    if carried is not None:
                        forces_at[place - 2, at, span] = near + carried[at]
                    passed.append(far)
            carried = passed
            lower = upper
        return dot_zz

    zeros = jnp.zeros((8, cols), jnp.float32)
    dot_zz = lax.fori_loop(0, rows // 8, first_product, zeros)

    for place in range(depth + 1):
        scale = inverse[place]
        if place == depth:
            scale = jnp.where(slab < slabs - 1, scale, 0.0)
        for comp in range(3):
            along = []
            for mode_y in range(2):
                level = forces_at[place, 4 * comp + mode_y]
                rise = forces_at[place, 4 * comp + 2 + mode_y]
                along.append((level - rise) + shift_back(level + rise, 0, first_row))
            image = (along[0] - along[1]) + shift_back(along[0] + along[1], 1, first_col)
            image = image * scale
            if place < depth:
                y_ref[comp, place] = image
            for at, part in enumerate(spread_plane(image, last_row, last_col)):
                fields_y[place, 4 * comp + at] = part

    def second_product(chunk, dots):
        dot_zy, dot_yy = dots
        span = pl.ds(pl.multiple_of(chunk * 8, 8), 8)
        lower = [fields_y[0, at, span] for at in range(12)]
        lower_z = [fields[1, at, span] for at in range(12)]
        for place in range(depth):
            upper = [fields_y[place + 1, at, span] for at in range(12)]
            upper_z = [fields[place + 2, at, span] for at in range(12)]
            hat = element_modes(lower, upper)
            forces = modal_forces(hat)
            modulus = elastic[place + 2, span]
            energy_yy = modal_product(hat, forces)
            energy_zy = modal_product(element_modes(lower_z, upper_z), forces)
            dot_zy = dot_zy + modulus * energy_zy
            dot_yy = dot_yy + modulus * energy_yy
            dense = density_ref[place, span]
            factor = -(3.0 / 8.0) * dense * dense
            factor = factor * modulus / (0.001 + dense * dense * dense)
            quad_ref[0, place, span] = factor * quad_ref[0, place, span]
            quad_ref[1, place, span] = (2.0 * factor) * energy_zy
            quad_ref[2, place, span] = factor * energy_yy
            lower, lower_z = upper, upper_z
        return dot_zy, dot_yy

    dot_zy, dot_yy = lax.fori_loop(0, rows // 8, second_product, (zeros, zeros))
    for at, part in enumerate((dot_load, dot_zz, dot_zy, dot_yy)):
        dots_ref[at : at + 1] = jnp.sum(part, axis=0, keepdims=True)


def last_kernel(
    dots_ref, other_dots_ref, z_ref, y_ref, quad_ref,
    displacement_ref, compliance_ref, keep_ref, send1_ref, send2_ref, send3_ref,
):
    chip = lax.axis_index("sample") // 2
    dots = jnp.sum(dots_ref[...] + other_dots_ref[...], axis=1, keepdims=True)
    dot_load, dot_zz, dot_zy, dot_yy = (dots[at : at + 1] for at in range(4))
    first = dot_zz / dot_load
    second = dot_zy / dot_load
    third = dot_yy / dot_load
    under = third * first - second * second
    along_z = (third - first * second) / under
    along_y = (first * first - second) / under
    compliance_ref[0] = (dot_load * (along_z + along_y * first))[0, 0]
    for comp in range(3):
        for place in range(z_ref.shape[1]):
            displacement_ref[0, comp, place] = along_z * z_ref[comp, place] + along_y * y_ref[comp, place]
    squares = (along_z * along_z, along_z * along_y, along_y * along_y)
    share = quad_ref.shape[2] // 4
    for step, out_ref in enumerate((keep_ref, send1_ref, send2_ref, send3_ref)):
        span = pl.ds(pl.multiple_of((chip + step) % 4 * share, share), share)
        for place in range(z_ref.shape[1]):
            out_ref[place] = sum(squares[at] * quad_ref[at, place, span] for at in range(3))


def call(kernel, outs, scratch=(), out_specs=None):
    return pl.pallas_call(
        kernel,
        out_shape=outs,
        out_specs=out_specs if out_specs is not None else [vmem_spec()] * len(outs),
        scratch_shapes=scratch,
        compiler_params=pltpu.CompilerParams(vmem_limit_bytes=VMEM_LIMIT),
    )


def ring_sum(value, offsets, period, base):
    total = value
    parts = []
    for offset in offsets:
        pairs = []
        for source in range(lax.axis_size("space")):
            block = source // period * period
            pairs.append((source, block + (source - block + offset) % period))
        parts.append(lax.ppermute(value, "space", pairs))
    for part in parts:
        total = total + part
    return total


def per_device(load_field, density, mode_panels, mode_weight, mode_germs):
    depth, rows, cols = density.shape
    slabs = lax.axis_size("space")
    samples = lax.axis_size("sample")
    own_modes = mode_panels.shape[0]
    cells = mode_panels.shape[2]
    spread_y, spread_zx = weight_tables(depth, rows, cols)

    keep, send1, send2, send3, going_up, going_down = call(
        first_kernel,
        [f32(2, cells)] * 4 + [f32(5, rows, cols), f32(8, rows, cols)],
    )(
        mode_weight.reshape(1, -1),
        mode_germs,
        mode_panels.reshape(own_modes, cells),
        density,
        load_field,
    )

    def along_chips(value, offset):
        return lax.ppermute(
            value, "sample", [(at, (at + 2 * offset) % samples) for at in range(samples)]
        )

    def neighbour(value, flip, step):
        pairs = []
        for sample in range(samples):
            for slab in range(slabs):
                if 0 <= slab + step < slabs:
                    target = sample ^ 1 if flip else sample
                    pairs.append((sample * slabs + slab, target * slabs + slab + step))
        return lax.ppermute(value, BOTH, pairs)

    got = [along_chips(value, step + 1) for step, value in enumerate((send1, send2, send3))]
    below = neighbour(going_up, False, 1)
    above = neighbour(going_down, False, -1)
    sums = keep + got[0] + got[1] + got[2]
    same, other = sums[0:1], sums[1:2]
    here = neighbour(other, True, 0)
    low_other, high_other = neighbour(other, True, 1), neighbour(other, True, -1)
    low_same, high_same = neighbour(same, False, 1), neighbour(same, False, -1)

    z_vec, y_vec, quads, dots = call(
        middle_kernel,
        [
            f32(3, depth, rows, cols),
            f32(3, depth, rows, cols),
            f32(3, depth, rows, cols),
            f32(4, cols),
        ],
        scratch=[
            pltpu.VMEM((depth + 4, rows, cols), jnp.float32),
            pltpu.VMEM((depth + 3, 12, rows, cols), jnp.float32),
            pltpu.VMEM((depth + 1, 12, rows, cols), jnp.float32),
            pltpu.VMEM((depth + 1, 12, rows, cols), jnp.float32),
            pltpu.VMEM((depth + 1, rows, cols), jnp.float32),
        ],
    )(
        sums, here, low_other, high_other, low_same, high_same,
        density, load_field, below, above, spread_y, spread_zx,
    )

    dots = ring_sum(dots, (8, 16, 24), 32, 0)
    dots = ring_sum(dots, (2, 4, 6), 8, 0)
    other_dots = lax.ppermute(dots, "space", [(at, at ^ 1) for at in range(slabs)])

    share = rows // 4
    displacement, compliance, keep, send1, send2, send3 = call(
        last_kernel,
        [f32(1, 3, depth, rows, cols), f32(1)] + [f32(depth, share, cols)] * 4,
        out_specs=[vmem_spec(), pl.BlockSpec(memory_space=pltpu.SMEM)] + [vmem_spec()] * 4,
    )(dots, other_dots, z_vec, y_vec, quads)

    got = [along_chips(value, step + 1) for step, value in enumerate((send1, send2, send3))]
    total = keep + got[0] + got[1] + got[2]
    halves = total.reshape(depth, 2, share // 2, cols)
    core = lax.axis_index("sample") % 2
    own = lax.dynamic_index_in_dim(halves, core, 1, keepdims=False)
    away = lax.dynamic_index_in_dim(halves, 1 - core, 1, keepdims=False)
    gradient = own + neighbour(away, True, 0)
    return displacement, gradient, compliance


def solution(mesh):
    placed = (
        P(None, "space", None, None),
        P("space", None, None),
        P("sample", "space", None),
        P(),
        P(),
    )
    return jax.shard_map(
        per_device,
        mesh=mesh,
        in_specs=placed,
        out_specs=(P("sample", None, "space", None, None), P("space", "sample", None), P("sample")),
        check_vma=False,
    )
```

time: 437 us -> 75.1 us (0.17)
  the two profiles are of different devices: /device:TPU:32 before, /device:TPU:1 now
where the time goes in v1:
time: 75.1 us; the launch traced here: 74.7 us
  starting transfers between devices  50.7 us (68%)
  waiting for transfers between devices  12.4 us (17%)
  Pallas kernels  5.16 us (7%)
  local copies, waits for them, and re-layouts  4.95 us (7%)
  between operations  0.83 us (1%)
    ppermute x8, starting transfers between devices, neighbour(): return lax.ppermute(value, BOTH, pairs)  24.8 us
    ppermute x6, starting transfers between devices, ring_sum(): parts.append(lax.ppermute(value, 'space', pairs))  14.6 us
    ppermute x6, starting transfers between devices, along_chips(): lax.ppermute(value, 'sample', [(at, (at + 2 * offset) % samples) for at i...  8.6 us
    ppermute x8, waiting for transfers between devices, neighbour(): return lax.ppermute(value, BOTH, pairs)  5.08 us
    unnamed x16, local copies, waits for them, and re-layouts  4.93 us
    ppermute x6, waiting for transfers between devices, ring_sum(): parts.append(lax.ppermute(value, 'space', pairs))  3.96 us
    pallas_call x1, Pallas kernels, per_device(): call(middle_kernel, [f32(3, depth, rows, cols), f32(3, depth, rows, cols)...  3.9 us
    ppermute x1, starting transfers between devices, per_device(): lax.ppermute(dots, 'space', [(at, at ^ 1) for at in range(slabs)])  2.69 us
  transfers between devices with their start and end apart: 21, of which 10 were waited for; matrix products, arithmetic and copies ran while one was open for 0% of the time, Pallas kernels for 0%

profile of v1, /device:TPU:1, one launch (start us, length us, event | category | flops | bytes accessed | tf_op | source)
XLA Modules:
  0.0 74.7 jit_solution(16919494440407054654)
XLA Ops:
  0.6 0.7 copy-done.7
  1.3 1.0 %copy-done = f32[3,4,64,128]{3,2,1,0:T(8,128)S(1)} copy-done((f32[3,4,64,128]{3,2,1,0:T(8,128)S(1)}, f32[3,4,64,128]{3,2,1,0:T(8,128)}, u32[]{:S(2)}) %copy-start) | copy-done | bytes 393240
  2.3 0.9 %copy-done.2 = f32[4,64,128]{2,1,0:T(8,128)S(1)} copy-done((f32[4,64,128]{2,1,0:T(8,128)S(1)}, f32[4,64,128]{2,1,0:T(8,128)}, u32[]{:S(2)}) %copy-start.2) | copy-done | bytes 131096
  3.2 0.8 %copy-done.5 = bf16[32,1,512]{2,0,1:T(8,128)(2,1)S(1)} copy-done((bf16[32,1,512]{2,0,1:T(8,128)(2,1)S(1)}, bf16[32,1,512]{2,0,1:T(8,128)(2,1)}, u32[]{:S(2)}) %copy-start.5) | copy-done | bytes 32792
  4.0 0.7 copy-done.6
  4.7 0.3 shard_map.94
  5.0 2.1 %collective-permute-start = (f32[2,512]{1,0:T(2,128)S(1)}, f32[2,512]{1,0:T(2,128)S(1)}, u32[]{:S(2)}, u32[]{:S(2)}) collective-permute-start(f32[2,512]{1,0:T(2,128)S(1)} %get-tuple-element.20), channel_id=1, source_target_pairs={{0,64},{32,96},{64,128},{96,160},{128,192},{160,224},{192,0},{224,... | collective-permute-start | bytes 12296 | tf_op jit(solution)/shard_map/ppermute | solution.py:369
  7.1 2.5 %collective-permute-start.1 = (f32[2,512]{1,0:T(2,128)S(1)}, f32[2,512]{1,0:T(2,128)S(1)}, u32[]{:S(2)}, u32[]{:S(2)}) collective-permute-start(f32[2,512]{1,0:T(2,128)S(1)} %get-tuple-element.21), channel_id=1, source_target_pairs={{0,128},{32,160},{64,192},{96,224},{128,0},{160,32},{192,64},{224,... | collective-permute-start | bytes 12296 | tf_op jit(solution)/shard_map/ppermute | solution.py:369
  9.5 1.2 %collective-permute-start.2 = (f32[2,512]{1,0:T(2,128)S(1)}, f32[2,512]{1,0:T(2,128)S(1)}, u32[]{:S(2)}, u32[]{:S(2)}) collective-permute-start(f32[2,512]{1,0:T(2,128)S(1)} %get-tuple-element.22), channel_id=1, source_target_pairs={{0,192},{32,224},{64,0},{96,32},{128,64},{160,96},{192,128},{224,1... | collective-permute-start | bytes 12296 | tf_op jit(solution)/shard_map/ppermute | solution.py:369
  10.7 1.3 %collective-permute-start.9 = (f32[8,64,128]{2,1,0:T(8,128)S(1)}, f32[8,64,128]{2,1,0:T(8,128)S(1)}, u32[]{:S(2)}, u32[]{:S(2)}) collective-permute-start(f32[8,64,128]{2,1,0:T(8,128)S(1)} %get-tuple-element.24), channel_id=1, source_target_pairs={{1,0},{2,1},{3,2},{4,3},{5,4},{6,5},{7,6},{8,7},{9,8},{10,9},{11,1... | collective-permute-start | bytes 786440 | tf_op jit(solution)/shard_map/ppermute | solution.py:380
  12.0 4.2 %collective-permute-start.8 = (f32[5,64,128]{2,1,0:T(8,128)S(1)}, f32[5,64,128]{2,1,0:T(8,128)S(1)}, u32[]{:S(2)}, u32[]{:S(2)}) collective-permute-start(f32[5,64,128]{2,1,0:T(8,128)S(1)} %get-tuple-element.23), channel_id=1, source_target_pairs={{0,1},{1,2},{2,3},{3,4},{4,5},{5,6},{6,7},{7,8},{8,9},{9,10},{10,1... | collective-permute-start | bytes 491528 | tf_op jit(solution)/shard_map/ppermute | solution.py:380
  16.2 0.0 collective-permute-done.1
  16.2 0.0 collective-permute-done.2
  16.2 2.0 %collective-permute-start.3 = (f32[1,512]{1,0:T(1,128)S(1)}, f32[1,512]{1,0:T(1,128)S(1)}, u32[]{:S(2)}, u32[]{:S(2)}) collective-permute-start(f32[1,512]{1,0:T(1,128)S(1)} %get-tuple-element.36), channel_id=1, source_target_pairs={{0,32},{1,33},{2,34},{3,35},{4,36},{5,37},{6,38},{7,39},{8,40},{9,... | collective-permute-start | bytes 6152 | tf_op jit(solution)/shard_map/ppermute | solution.py:380
  18.2 3.4 %collective-permute-start.4 = (f32[1,512]{1,0:T(1,128)S(1)}, f32[1,512]{1,0:T(1,128)S(1)}, u32[]{:S(2)}, u32[]{:S(2)}) collective-permute-start(f32[1,512]{1,0:T(1,128)S(1)} %get-tuple-element.36), channel_id=1, source_target_pairs={{0,33},{1,34},{2,35},{3,36},{4,37},{5,38},{6,39},{7,40},{8,41},{9,... | collective-permute-start | bytes 6152 | tf_op jit(solution)/shard_map/ppermute | solution.py:380
  21.7 1.3 %collective-permute-start.5 = (f32[1,512]{1,0:T(1,128)S(1)}, f32[1,512]{1,0:T(1,128)S(1)}, u32[]{:S(2)}, u32[]{:S(2)}) collective-permute-start(f32[1,512]{1,0:T(1,128)S(1)} %get-tuple-element.36), channel_id=1, source_target_pairs={{1,32},{2,33},{3,34},{4,35},{5,36},{6,37},{7,38},{8,39},{9,40},{10... | collective-permute-start | bytes 6152 | tf_op jit(solution)/shard_map/ppermute | solution.py:380
  23.0 4.4 %collective-permute-start.6 = (f32[1,512]{1,0:T(1,128)S(1)}, f32[1,512]{1,0:T(1,128)S(1)}, u32[]{:S(2)}, u32[]{:S(2)}) collective-permute-start(f32[1,512]{1,0:T(1,128)S(1)} %get-tuple-element.35), channel_id=1, source_target_pairs={{0,1},{1,2},{2,3},{3,4},{4,5},{5,6},{6,7},{7,8},{8,9},{9,10},{10,1... | collective-permute-start | bytes 6152 | tf_op jit(solution)/shard_map/ppermute | solution.py:380
  27.3 0.0 collective-permute-done.4.low_other_ref
  27.3 1.3 %collective-permute-start.7 = (f32[1,512]{1,0:T(1,128)S(1)}, f32[1,512]{1,0:T(1,128)S(1)}, u32[]{:S(2)}, u32[]{:S(2)}) collective-permute-start(f32[1,512]{1,0:T(1,128)S(1)} %get-tuple-element.35), channel_id=1, source_target_pairs={{1,0},{2,1},{3,2},{4,3},{5,4},{6,5},{7,6},{8,7},{9,8},{10,9},{11,1... | collective-permute-start | bytes 6152 | tf_op jit(solution)/shard_map/ppermute | solution.py:380
  28.7 4.2 %collective-permute-done.7.high_same_ref = f32[1,512]{1,0:T(1,128)S(1)} collective-permute-done((f32[1,512]{1,0:T(1,128)S(1)}, f32[1,512]{1,0:T(1,128)S(1)}, u32[]{:S(2)}, u32[]{:S(2)}) %collective-permute-start.7) | collective-permute-done | bytes 2080 | tf_op jit(solution)/shard_map/ppermute | solution.py:380
  32.9 0.0 collective-permute-done.8.below_ref
  32.9 0.0 collective-permute-done.9.above_ref
  32.9 0.0 copy-start.4
  32.9 0.9 %copy-done.4 = bf16[512,48]{1,0:T(8,128)(2,1)S(1)} copy-done((bf16[512,48]{1,0:T(8,128)(2,1)S(1)}, bf16[512,48]{1,0:T(8,128)(2,1)}, u32[]{:S(2)}) %copy-start.4) | copy-done | bytes 49176
  33.8 3.9 %shard_map.95 = (f32[3,4,64,128]{3,2,1,0:T(8,128)S(1)}, f32[3,4,64,128]{3,2,1,0:T(8,128)S(1)}, f32[3,4,64,128]{3,2,1,0:T(8,128)S(1)}, f32[4,128]{1,0:T(4,128)S(1)}) custom-call(f32[2,512]{1,0:T(2,128)S(1)} %add_add_fusion.sums_ref, f32[1,512]{1,0:T(1,128)S(1)} %collective-permute-done.3.here_ref, f32[1,512]{1,0:T(1,128)S(1)} %collective-permute-done.4.low_other_ref, ...), custom_call_target="tpu_custom_call" | custom-call | tf_op jit(solution)/shard_map/pallas_call | solution.py:391
  37.7 6.3 %collective-permute-start.10 = (f32[4,128]{1,0:T(4,128)S(1)}, f32[4,128]{1,0:T(4,128)S(1)}, u32[]{:S(2)}, u32[]{:S(2)}) collective-permute-start(f32[4,128]{1,0:T(4,128)S(1)} %get-tuple-element.25), channel_id=1, source_target_pairs={{0,8},{1,9},{2,10},{3,11},{4,12},{5,13},{6,14},{7,15},{8,16},{9,17... | collective-permute-start | bytes 6152 | tf_op jit(solution)/shard_map/ppermute | solution.py:343
  44.0 2.9 %collective-permute-start.11 = (f32[4,128]{1,0:T(4,128)S(1)}, f32[4,128]{1,0:T(4,128)S(1)}, u32[]{:S(2)}, u32[]{:S(2)}) collective-permute-start(f32[4,128]{1,0:T(4,128)S(1)} %get-tuple-element.25), channel_id=1, source_target_pairs={{0,16},{1,17},{2,18},{3,19},{4,20},{5,21},{6,22},{7,23},{8,24},{9,... | collective-permute-start | bytes 6152 | tf_op jit(solution)/shard_map/ppermute | solution.py:343
  46.9 0.8 %collective-permute-start.12 = (f32[4,128]{1,0:T(4,128)S(1)}, f32[4,128]{1,0:T(4,128)S(1)}, u32[]{:S(2)}, u32[]{:S(2)}) collective-permute-start(f32[4,128]{1,0:T(4,128)S(1)} %get-tuple-element.25), channel_id=1, source_target_pairs={{0,24},{1,25},{2,26},{3,27},{4,28},{5,29},{6,30},{7,31},{8,0},{9,1... | collective-permute-start | bytes 6152 | tf_op jit(solution)/shard_map/ppermute | solution.py:343
  47.7 0.2 collective-permute-done.11
  47.9 1.7 %collective-permute-done.12 = f32[4,128]{1,0:T(4,128)S(1)} collective-permute-done((f32[4,128]{1,0:T(4,128)S(1)}, f32[4,128]{1,0:T(4,128)S(1)}, u32[]{:S(2)}, u32[]{:S(2)}) %collective-permute-start.12) | collective-permute-done | bytes 2080 | tf_op jit(solution)/shard_map/ppermute | solution.py:343
  49.6 0.0 collective-permute-start.13
  49.7 2.4 %collective-permute-start.14 = (f32[4,128]{1,0:T(4,128)S(1)}, f32[4,128]{1,0:T(4,128)S(1)}, u32[]{:S(2)}, u32[]{:S(2)}) collective-permute-start(f32[4,128]{1,0:T(4,128)S(1)} %add_add_fusion.2), channel_id=1, source_target_pairs={{0,4},{1,5},{2,6},{3,7},{4,0},{5,1},{6,2},{7,3},{8,12},{9,13},{10,... | collective-permute-start | bytes 6152 | tf_op jit(solution)/shard_map/ppermute | solution.py:343
  52.1 2.2 %collective-permute-start.15 = (f32[4,128]{1,0:T(4,128)S(1)}, f32[4,128]{1,0:T(4,128)S(1)}, u32[]{:S(2)}, u32[]{:S(2)}) collective-permute-start(f32[4,128]{1,0:T(4,128)S(1)} %add_add_fusion.2), channel_id=1, source_target_pairs={{0,6},{1,7},{2,0},{3,1},{4,2},{5,3},{6,4},{7,5},{8,14},{9,15},{10,... | collective-permute-start | bytes 6152 | tf_op jit(solution)/shard_map/ppermute | solution.py:343
  54.3 0.0 collective-permute-done.13
  54.3 1.8 %collective-permute-done.14 = f32[4,128]{1,0:T(4,128)S(1)} collective-permute-done((f32[4,128]{1,0:T(4,128)S(1)}, f32[4,128]{1,0:T(4,128)S(1)}, u32[]{:S(2)}, u32[]{:S(2)}) %collective-permute-start.14) | collective-permute-done | bytes 2080 | tf_op jit(solution)/shard_map/ppermute | solution.py:343
  56.1 0.2 collective-permute-done.15
  56.3 2.7 %collective-permute-start.16 = (f32[4,128]{1,0:T(4,128)S(1)}, f32[4,128]{1,0:T(4,128)S(1)}, u32[]{:S(2)}, u32[]{:S(2)}) collective-permute-start(f32[4,128]{1,0:T(4,128)S(1)} %add_add_fusion.1.dots_ref), channel_id=1, source_target_pairs={{0,1},{1,0},{2,3},{3,2},{4,5},{5,4},{6,7},{7,6},{8,9},{9,8},{10,11... | collective-permute-start | bytes 6152 | tf_op jit(solution)/shard_map/ppermute | solution.py:413
  59.0 1.2 %collective-permute-done.16.other_dots_ref = f32[4,128]{1,0:T(4,128)S(1)} collective-permute-done((f32[4,128]{1,0:T(4,128)S(1)}, f32[4,128]{1,0:T(4,128)S(1)}, u32[]{:S(2)}, u32[]{:S(2)}) %collective-permute-start.16) | collective-permute-done | bytes 2080 | tf_op jit(solution)/shard_map/ppermute | solution.py:413
  60.2 1.0 %shard_map.96 = (f32[1,3,4,64,128]{4,3,2,1,0:T(8,128)}, f32[1]{0:T(128)}, f32[4,16,128]{2,1,0:T(8,128)S(1)}, f32[4,16,128]{2,1,0:T(8,128)S(1)}, f32[4,16,128]{2,1,0:T(8,128)S(1)}, /*index=5*/f32[4,16,128]{2,1,0:T(8,128)S(1)}) custom-call(f32[4,128]{1,0:T(4,128)S(1)} %add_add_fusion.1.dots_ref, f32[4,128]{1,0:T(4,128)S(1)} %collective-permute-done.16.other_dots_ref, ...), custom_call_target="tpu_custom_call" | custom-call | tf_op jit(solution)/shard_map/pallas_call | solution.py:416
  61.2 0.4 collective-permute-start.17
  61.6 0.6 collective-permute-start.18
  62.2 1.9 %collective-permute-start.19 = (f32[4,16,128]{2,1,0:T(8,128)S(1)}, f32[4,16,128]{2,1,0:T(8,128)S(1)}, u32[]{:S(2)}, u32[]{:S(2)}) collective-permute-start(f32[4,16,128]{2,1,0:T(8,128)S(1)} %get-tuple-element.33), channel_id=1, source_target_pairs={{0,192},{32,224},{64,0},{96,32},{128,64},{160,96},{192,128},{224,1... | collective-permute-start | bytes 98312 | tf_op jit(solution)/shard_map/ppermute | solution.py:369
  64.1 1.2 %collective-permute-done.17 = f32[4,16,128]{2,1,0:T(8,128)S(1)} collective-permute-done((f32[4,16,128]{2,1,0:T(8,128)S(1)}, f32[4,16,128]{2,1,0:T(8,128)S(1)}, u32[]{:S(2)}, u32[]{:S(2)}) %collective-permute-start.17) | collective-permute-done | bytes 32800 | tf_op jit(solution)/shard_map/ppermute | solution.py:369
  65.2 0.6 collective-permute-done.18
  65.8 0.3 collective-permute-done.19
  66.2 7.0 %collective-permute-start.20 = (f32[4,8,128]{2,1,0:T(8,128)S(1)}, f32[4,8,128]{2,1,0:T(8,128)S(1)}, u32[]{:S(2)}, u32[]{:S(2)}) collective-permute-start(f32[4,8,128]{2,1,0:T(8,128)S(1)} %dynamic-slice_bitcast_fusion), channel_id=1, source_target_pairs={{0,32},{1,33},{2,34},{3,35},{4,36},{5,37},{6,38},{7,39},{8,40},{9,... | collective-permute-start | bytes 49160 | tf_op jit(solution)/shard_map/ppermute | solution.py:380
  73.2 0.8 %collective-permute-done.20 = f32[4,8,128]{2,1,0:T(8,128)S(1)} collective-permute-done((f32[4,8,128]{2,1,0:T(8,128)S(1)}, f32[4,8,128]{2,1,0:T(8,128)S(1)}, u32[]{:S(2)}, u32[]{:S(2)}) %collective-permute-start.20) | collective-permute-done | bytes 16416 | tf_op jit(solution)/shard_map/ppermute | solution.py:380
  74.1 0.6 bitcast_add_fusion
  (20 shorter events, 0.1 us)
Async XLA Ops:
  0.6 0.7 copy-start.7
  1.3 1.0 %copy-start = (f32[3,4,64,128]{3,2,1,0:T(8,128)S(1)}, f32[3,4,64,128]{3,2,1,0:T(8,128)}, u32[]{:S(2)}) copy-start(f32[3,4,64,128]{3,2,1,0:T(8,128)} %load_ref.3) | copy-start | bytes 1179652
  2.3 0.9 %copy-start.2 = (f32[4,64,128]{2,1,0:T(8,128)S(1)}, f32[4,64,128]{2,1,0:T(8,128)}, u32[]{:S(2)}) copy-start(f32[4,64,128]{2,1,0:T(8,128)} %density_ref.3) | copy-start | bytes 393220
  3.2 0.8 %copy-start.5 = (bf16[32,1,512]{2,0,1:T(8,128)(2,1)S(1)}, bf16[32,1,512]{2,0,1:T(8,128)(2,1)}, u32[]{:S(2)}) copy-start(bf16[32,1,512]{2,0,1:T(8,128)(2,1)} %param.9) | copy-start | bytes 98308
  4.0 0.7 copy-start.6
  4.7 28.2 %copy-start.1 = (f32[3,4,64,128]{3,2,1,0:T(8,128)S(1)}, f32[3,4,64,128]{3,2,1,0:T(8,128)}, u32[]{:S(2)}) copy-start(f32[3,4,64,128]{3,2,1,0:T(8,128)} %load_ref.3) | copy-start | bytes 1179652
  4.7 28.2 %copy-start.3 = (bf16[512,128]{1,0:T(8,128)(2,1)S(1)}, bf16[512,128]{1,0:T(8,128)(2,1)}, u32[]{:S(2)}) copy-start(bf16[512,128]{1,0:T(8,128)(2,1)} %constant.32.clone.spread_y_ref) | copy-start | bytes 393220
  5.0 11.2 %collective-permute-start = (f32[2,512]{1,0:T(2,128)S(1)}, f32[2,512]{1,0:T(2,128)S(1)}, u32[]{:S(2)}, u32[]{:S(2)}) collective-permute-start(f32[2,512]{1,0:T(2,128)S(1)} %get-tuple-element.20), channel_id=1, source_target_pairs={{0,64},{32,96},{64,128},{96,160},{128,192},{160,224},{192,0},{224,... | collective-permute-start | bytes 12296 | tf_op jit(solution)/shard_map/ppermute | solution.py:369
  7.1 9.1 %collective-permute-start.1 = (f32[2,512]{1,0:T(2,128)S(1)}, f32[2,512]{1,0:T(2,128)S(1)}, u32[]{:S(2)}, u32[]{:S(2)}) collective-permute-start(f32[2,512]{1,0:T(2,128)S(1)} %get-tuple-element.21), channel_id=1, source_target_pairs={{0,128},{32,160},{64,192},{96,224},{128,0},{160,32},{192,64},{224,... | collective-permute-start | bytes 12296 | tf_op jit(solution)/shard_map/ppermute | solution.py:369
  9.5 6.7 %collective-permute-start.2 = (f32[2,512]{1,0:T(2,128)S(1)}, f32[2,512]{1,0:T(2,128)S(1)}, u32[]{:S(2)}, u32[]{:S(2)}) collective-permute-start(f32[2,512]{1,0:T(2,128)S(1)} %get-tuple-element.22), channel_id=1, source_target_pairs={{0,192},{32,224},{64,0},{96,32},{128,64},{160,96},{192,128},{224,1... | collective-permute-start | bytes 12296 | tf_op jit(solution)/shard_map/ppermute | solution.py:369
  10.7 22.2 %collective-permute-start.9 = (f32[8,64,128]{2,1,0:T(8,128)S(1)}, f32[8,64,128]{2,1,0:T(8,128)S(1)}, u32[]{:S(2)}, u32[]{:S(2)}) collective-permute-start(f32[8,64,128]{2,1,0:T(8,128)S(1)} %get-tuple-element.24), channel_id=1, source_target_pairs={{1,0},{2,1},{3,2},{4,3},{5,4},{6,5},{7,6},{8,7},{9,8},{10,9},{11,1... | collective-permute-start | bytes 786440 | tf_op jit(solution)/shard_map/ppermute | solution.py:380
  12.0 20.9 %collective-permute-start.8 = (f32[5,64,128]{2,1,0:T(8,128)S(1)}, f32[5,64,128]{2,1,0:T(8,128)S(1)}, u32[]{:S(2)}, u32[]{:S(2)}) collective-permute-start(f32[5,64,128]{2,1,0:T(8,128)S(1)} %get-tuple-element.23), channel_id=1, source_target_pairs={{0,1},{1,2},{2,3},{3,4},{4,5},{5,6},{6,7},{7,8},{8,9},{9,10},{10,1... | collective-permute-start | bytes 491528 | tf_op jit(solution)/shard_map/ppermute | solution.py:380
  16.2 6.7 %collective-permute-start.3 = (f32[1,512]{1,0:T(1,128)S(1)}, f32[1,512]{1,0:T(1,128)S(1)}, u32[]{:S(2)}, u32[]{:S(2)}) collective-permute-start(f32[1,512]{1,0:T(1,128)S(1)} %get-tuple-element.36), channel_id=1, source_target_pairs={{0,32},{1,33},{2,34},{3,35},{4,36},{5,37},{6,38},{7,39},{8,40},{9,... | collective-permute-start | bytes 6152 | tf_op jit(solution)/shard_map/ppermute | solution.py:380
  18.2 9.1 %collective-permute-start.4 = (f32[1,512]{1,0:T(1,128)S(1)}, f32[1,512]{1,0:T(1,128)S(1)}, u32[]{:S(2)}, u32[]{:S(2)}) collective-permute-start(f32[1,512]{1,0:T(1,128)S(1)} %get-tuple-element.36), channel_id=1, source_target_pairs={{0,33},{1,34},{2,35},{3,36},{4,37},{5,38},{6,39},{7,40},{8,41},{9,... | collective-permute-start | bytes 6152 | tf_op jit(solution)/shard_map/ppermute | solution.py:380
  21.7 7.0 %collective-permute-start.5 = (f32[1,512]{1,0:T(1,128)S(1)}, f32[1,512]{1,0:T(1,128)S(1)}, u32[]{:S(2)}, u32[]{:S(2)}) collective-permute-start(f32[1,512]{1,0:T(1,128)S(1)} %get-tuple-element.36), channel_id=1, source_target_pairs={{1,32},{2,33},{3,34},{4,35},{5,36},{6,37},{7,38},{8,39},{9,40},{10... | collective-permute-start | bytes 6152 | tf_op jit(solution)/shard_map/ppermute | solution.py:380
  23.0 5.7 %collective-permute-start.6 = (f32[1,512]{1,0:T(1,128)S(1)}, f32[1,512]{1,0:T(1,128)S(1)}, u32[]{:S(2)}, u32[]{:S(2)}) collective-permute-start(f32[1,512]{1,0:T(1,128)S(1)} %get-tuple-element.35), channel_id=1, source_target_pairs={{0,1},{1,2},{2,3},{3,4},{4,5},{5,6},{6,7},{7,8},{8,9},{9,10},{10,1... | collective-permute-start | bytes 6152 | tf_op jit(solution)/shard_map/ppermute | solution.py:380
  27.3 5.5 %collective-permute-start.7 = (f32[1,512]{1,0:T(1,128)S(1)}, f32[1,512]{1,0:T(1,128)S(1)}, u32[]{:S(2)}, u32[]{:S(2)}) collective-permute-start(f32[1,512]{1,0:T(1,128)S(1)} %get-tuple-element.35), channel_id=1, source_target_pairs={{1,0},{2,1},{3,2},{4,3},{5,4},{6,5},{7,6},{8,7},{9,8},{10,9},{11,1... | collective-permute-start | bytes 6152 | tf_op jit(solution)/shard_map/ppermute | solution.py:380
  32.9 0.9 %copy-start.4 = (bf16[512,48]{1,0:T(8,128)(2,1)S(1)}, bf16[512,48]{1,0:T(8,128)(2,1)}, u32[]{:S(2)}) copy-start(bf16[512,48]{1,0:T(8,128)(2,1)} %constant.33.clone.spread_zx_ref) | copy-start | bytes 147460
  37.7 10.0 %collective-permute-start.10 = (f32[4,128]{1,0:T(4,128)S(1)}, f32[4,128]{1,0:T(4,128)S(1)}, u32[]{:S(2)}, u32[]{:S(2)}) collective-permute-start(f32[4,128]{1,0:T(4,128)S(1)} %get-tuple-element.25), channel_id=1, source_target_pairs={{0,8},{1,9},{2,10},{3,11},{4,12},{5,13},{6,14},{7,15},{8,16},{9,17... | collective-permute-start | bytes 6152 | tf_op jit(solution)/shard_map/ppermute | solution.py:343
  44.0 3.9 %collective-permute-start.11 = (f32[4,128]{1,0:T(4,128)S(1)}, f32[4,128]{1,0:T(4,128)S(1)}, u32[]{:S(2)}, u32[]{:S(2)}) collective-permute-start(f32[4,128]{1,0:T(4,128)S(1)} %get-tuple-element.25), channel_id=1, source_target_pairs={{0,16},{1,17},{2,18},{3,19},{4,20},{5,21},{6,22},{7,23},{8,24},{9,... | collective-permute-start | bytes 6152 | tf_op jit(solution)/shard_map/ppermute | solution.py:343
  46.9 2.7 %collective-permute-start.12 = (f32[4,128]{1,0:T(4,128)S(1)}, f32[4,128]{1,0:T(4,128)S(1)}, u32[]{:S(2)}, u32[]{:S(2)}) collective-permute-start(f32[4,128]{1,0:T(4,128)S(1)} %get-tuple-element.25), channel_id=1, source_target_pairs={{0,24},{1,25},{2,26},{3,27},{4,28},{5,29},{6,30},{7,31},{8,0},{9,1... | collective-permute-start | bytes 6152 | tf_op jit(solution)/shard_map/ppermute | solution.py:343
  49.6 4.6 %collective-permute-start.13 = (f32[4,128]{1,0:T(4,128)S(1)}, f32[4,128]{1,0:T(4,128)S(1)}, u32[]{:S(2)}, u32[]{:S(2)}) collective-permute-start(f32[4,128]{1,0:T(4,128)S(1)} %add_add_fusion.2), channel_id=1, source_target_pairs={{0,2},{1,3},{2,4},{3,5},{4,6},{5,7},{6,0},{7,1},{8,10},{9,11},{10,... | collective-permute-start | bytes 6152 | tf_op jit(solution)/shard_map/ppermute | solution.py:343
  49.7 6.4 %collective-permute-start.14 = (f32[4,128]{1,0:T(4,128)S(1)}, f32[4,128]{1,0:T(4,128)S(1)}, u32[]{:S(2)}, u32[]{:S(2)}) collective-permute-start(f32[4,128]{1,0:T(4,128)S(1)} %add_add_fusion.2), channel_id=1, source_target_pairs={{0,4},{1,5},{2,6},{3,7},{4,0},{5,1},{6,2},{7,3},{8,12},{9,13},{10,... | collective-permute-start | bytes 6152 | tf_op jit(solution)/shard_map/ppermute | solution.py:343
  52.1 4.2 %collective-permute-start.15 = (f32[4,128]{1,0:T(4,128)S(1)}, f32[4,128]{1,0:T(4,128)S(1)}, u32[]{:S(2)}, u32[]{:S(2)}) collective-permute-start(f32[4,128]{1,0:T(4,128)S(1)} %add_add_fusion.2), channel_id=1, source_target_pairs={{0,6},{1,7},{2,0},{3,1},{4,2},{5,3},{6,4},{7,5},{8,14},{9,15},{10,... | collective-permute-start | bytes 6152 | tf_op jit(solution)/shard_map/ppermute | solution.py:343
  56.3 3.9 %collective-permute-start.16 = (f32[4,128]{1,0:T(4,128)S(1)}, f32[4,128]{1,0:T(4,128)S(1)}, u32[]{:S(2)}, u32[]{:S(2)}) collective-permute-start(f32[4,128]{1,0:T(4,128)S(1)} %add_add_fusion.1.dots_ref), channel_id=1, source_target_pairs={{0,1},{1,0},{2,3},{3,2},{4,5},{5,4},{6,7},{7,6},{8,9},{9,8},{10,11... | collective-permute-start | bytes 6152 | tf_op jit(solution)/shard_map/ppermute | solution.py:413
  61.2 4.1 %collective-permute-start.17 = (f32[4,16,128]{2,1,0:T(8,128)S(1)}, f32[4,16,128]{2,1,0:T(8,128)S(1)}, u32[]{:S(2)}, u32[]{:S(2)}) collective-permute-start(f32[4,16,128]{2,1,0:T(8,128)S(1)} %get-tuple-element.31), channel_id=1, source_target_pairs={{0,64},{32,96},{64,128},{96,160},{128,192},{160,224},{192,0},{224,... | collective-permute-start | bytes 98312 | tf_op jit(solution)/shard_map/ppermute | solution.py:369
  61.6 4.3 %collective-permute-start.18 = (f32[4,16,128]{2,1,0:T(8,128)S(1)}, f32[4,16,128]{2,1,0:T(8,128)S(1)}, u32[]{:S(2)}, u32[]{:S(2)}) collective-permute-start(f32[4,16,128]{2,1,0:T(8,128)S(1)} %get-tuple-element.32), channel_id=1, source_target_pairs={{0,128},{32,160},{64,192},{96,224},{128,0},{160,32},{192,64},{224,... | collective-permute-start | bytes 98312 | tf_op jit(solution)/shard_map/ppermute | solution.py:369
  62.2 4.0 %collective-permute-start.19 = (f32[4,16,128]{2,1,0:T(8,128)S(1)}, f32[4,16,128]{2,1,0:T(8,128)S(1)}, u32[]{:S(2)}, u32[]{:S(2)}) collective-permute-start(f32[4,16,128]{2,1,0:T(8,128)S(1)} %get-tuple-element.33), channel_id=1, source_target_pairs={{0,192},{32,224},{64,0},{96,32},{128,64},{160,96},{192,128},{224,1... | collective-permute-start | bytes 98312 | tf_op jit(solution)/shard_map/ppermute | solution.py:369
  66.2 7.8 %collective-permute-start.20 = (f32[4,8,128]{2,1,0:T(8,128)S(1)}, f32[4,8,128]{2,1,0:T(8,128)S(1)}, u32[]{:S(2)}, u32[]{:S(2)}) collective-permute-start(f32[4,8,128]{2,1,0:T(8,128)S(1)} %dynamic-slice_bitcast_fusion), channel_id=1, source_target_pairs={{0,32},{1,33},{2,34},{3,35},{4,36},{5,37},{6,38},{7,39},{8,40},{9,... | collective-permute-start | bytes 49160 | tf_op jit(solution)/shard_map/ppermute | solution.py:380

commit v2 on v1

--- a/solution.py
+++ b/solution.py
@@ -8,7 +8,6 @@
 from jax.experimental.pallas import tpu as pltpu
 from jax.sharding import PartitionSpec as P
 
-BOTH = ("sample", "space")
 POISSON = 0.3
 LAME = POISSON / ((1.0 + POISSON) * (1.0 - 2.0 * POISSON))
 SHEAR = 1.0 / (2.0 * (1.0 + POISSON))
@@ -44,38 +43,62 @@
     along_x = hat((np.arange(rows) + 0.5) / 4.0 - 0.5, np.arange(rows // 4))
     along_y = hat((np.arange(cols) + 0.5) / 4.0 - 0.5, np.arange(cols // 4))
     along_z = hat((np.arange(depth + 4) - 2 + 0.5) / 4.0 - 0.5, np.arange(-1, 2))
-    spread_y = np.tile(along_y.T, (rows // 4, 1))
+    spread_y = np.tile(along_y.T, (4, 1))
     spread_zx = np.einsum("pc,xd->pxcd", along_z, along_x).reshape((depth + 4) * rows, -1)
     return spread_y.astype(jnp.bfloat16), spread_zx.astype(jnp.bfloat16)
 
 
-def first_kernel(
-    weight_ref, germs_ref, panels_ref, density_ref, load_ref,
-    keep_ref, send1_ref, send2_ref, send3_ref, up_ref, down_ref,
-):
+def first_kernel(weight_hbm, germs_hbm, panels_hbm, partial_ref, weight, germs, panels, sems):
     sample = lax.axis_index("sample")
-    chip, core = sample // 2, sample % 2
-    own_modes = panels_ref.shape[0]
-    modes = germs_ref.shape[1]
-    coefficients = (weight_ref[...] * germs_ref[...]).astype(jnp.bfloat16)
+    copies = [
+        pltpu.make_async_copy(source, target, sems.at[at])
+        for at, (source, target) in enumerate(
+            ((weight_hbm, weight), (germs_hbm, germs), (panels_hbm, panels))
+        )
+    ]
+    for copy in copies:
+        copy.start()
+    own_modes = panels.shape[0]
+    modes = germs.shape[1]
     mode_at = lax.broadcasted_iota(jnp.int32, (modes, own_modes), 0)
     slot_at = lax.broadcasted_iota(jnp.int32, (modes, own_modes), 1)
     pick = jnp.where(mode_at == slot_at + sample * own_modes, 1.0, 0.0).astype(jnp.bfloat16)
+    for copy in copies:
+        copy.wait()
+    coefficients = (weight[...] * germs[...]).astype(jnp.bfloat16)
     own_coeff = dot32(coefficients, pick).astype(jnp.bfloat16)
-    partial = dot32(own_coeff, panels_ref[...])
-    row_at = lax.broadcasted_iota(jnp.int32, partial.shape, 0)
-    for step, out_ref in enumerate((keep_ref, send1_ref, send2_ref, send3_ref)):
-        target = (chip + step) % 4
-        for place in range(2):
-            row = 2 * target + (core if place == 0 else 1 - core)
-            out_ref[place : place + 1] = jnp.sum(
-                jnp.where(row_at == row, partial, 0.0), axis=0, keepdims=True
-            )
-    up_ref[0:2] = density_ref[2:4]
-    down_ref[0:2] = density_ref[0:2]
-    for comp in range(3):
-        up_ref[2 + comp] = load_ref[comp, 3]
-        down_ref[2 + 2 * comp : 4 + 2 * comp] = load_ref[comp, 0:2]
+    partial = dot32(own_coeff, panels[...])
+    for at in range(partial_ref.shape[1]):
+        partial_ref[:, at] = partial[:, at * 128 : (at + 1) * 128]
+
+
+def pack_kernel(parts_ref, density_ref, load_ref, sums_ref, pair_ref, next_ref):
+    slab = lax.axis_index("space")
+    planes = (pair_ref.shape[0] - 8) // density_ref.shape[1]
+    rows = density_ref.shape[1]
+    depth = density_ref.shape[0]
+    cells = parts_ref.shape[1]
+    sums = jnp.sum(parts_ref[...], axis=0)
+    sums_ref[...] = sums
+
+    def fill(up_ref, down_ref):
+        up = [density_ref[depth - 2], density_ref[depth - 1]]
+        up += [load_ref[comp, depth - 1] for comp in range(3)]
+        down = [density_ref[0], density_ref[1]]
+        down += [load_ref[comp, place] for comp in range(3) for place in range(2)]
+        for ref, parts in ((up_ref, up), (down_ref, down)):
+            for at in range(planes):
+                ref[at * rows : (at + 1) * rows] = parts[at] if at < len(parts) else jnp.zeros_like(up[0])
+            ref[planes * rows : planes * rows + cells] = sums
+            ref[planes * rows + cells :] = jnp.zeros((8 - cells, sums.shape[1]), jnp.float32)
+
+    @pl.when(slab % 2 == 0)
+    def _():
+        fill(pair_ref, next_ref)
+
+    @pl.when(slab % 2 == 1)
+    def _():
+        fill(next_ref, pair_ref)
 
 
 def shift_ahead(value, axis, mask):
@@ -140,32 +163,42 @@
 
 
 def middle_kernel(
-    sums_ref, here_ref, low_other_ref, high_other_ref, low_same_ref, high_same_ref,
-    density_ref, load_ref, below_ref, above_ref, spread_y_ref, spread_zx_ref,
+    sums_ref, density_ref, load_ref, pair_ref, next_ref, spread_y_ref, spread_zx_ref,
     z_ref, y_ref, quad_ref, dots_ref,
     elastic, fields, fields_y, forces_at, inverse,
 ):
     slab = lax.axis_index("space")
     slabs = lax.axis_size("space")
+    even = slab % 2 == 0
     depth, rows, cols = density_ref.shape
     row_at = lax.broadcasted_iota(jnp.int32, (rows, cols), 0)
     col_at = lax.broadcasted_iota(jnp.int32, (rows, cols), 1)
     first_row, last_row = row_at == 0, row_at == rows - 1
     first_col, last_col = col_at == 0, col_at == cols - 1
-
-    planes = (
-        low_other_ref[...] + low_same_ref[...],
-        sums_ref[0:1] + here_ref[...],
-        high_other_ref[...] + high_same_ref[...],
-    )
-    cells = planes[0].shape[1]
+    cells = sums_ref.shape[0]
+    extra = pl.ds(pair_ref.shape[0] - 8, cells)
+
+    def from_below(span):
+        return jnp.where(even, next_ref[span], pair_ref[span])
+
+    def from_above(span):
+        return jnp.where(even, pair_ref[span], next_ref[span])
+
+    def plane(place):
+        return pl.ds(place * rows, rows)
+
     coarse_x, coarse_y = rows // 4, cols // 4
-    cell_at = lax.broadcasted_iota(jnp.int32, (coarse_x, cells), 1)
-    line_at = lax.broadcasted_iota(jnp.int32, (coarse_x, cells), 0)
-    on_line = cell_at // coarse_y == line_at
-    lines = jnp.concatenate(
-        [jnp.where(on_line, jnp.broadcast_to(plane, on_line.shape), 0.0) for plane in planes], axis=0
-    )
+    fold_x = coarse_x // cells
+    line_at = lax.broadcasted_iota(jnp.int32, (coarse_x, cols), 0)
+    cell_at = lax.broadcasted_iota(jnp.int32, (coarse_x, cols), 1)
+    on_line = cell_at // coarse_y == line_at % fold_x
+    lines = []
+    for coarse in (from_below(extra), sums_ref[...], from_above(extra)):
+        tall = jnp.zeros((coarse_x, cols), jnp.float32)
+        for at in range(cells):
+            tall = jnp.where(line_at // fold_x == at, coarse[at : at + 1], tall)
+        lines.append(jnp.where(on_line, tall, 0.0))
+    lines = jnp.concatenate(lines, axis=0)
     spread_y = spread_y_ref[...]
     high, mid, low = (dot32(part, spread_y) for part in split3(lines))
     along_y = high + (mid + low)
@@ -175,11 +208,11 @@
 
     for place in range(depth + 4):
         if place < 2:
-            dense = below_ref[place]
+            dense = from_below(plane(place))
         elif place < depth + 2:
             dense = density_ref[place - 2]
         else:
-            dense = above_ref[place - depth - 2]
+            dense = from_above(plane(place - depth - 2))
         modulus = growth[place] * (0.001 + dense * dense * dense)
         if place < 2:
             modulus = jnp.where(slab > 0, modulus, 0.0)
@@ -204,11 +237,11 @@
                 inverse[place - 2] = inverse_here
             for comp in range(3):
                 if place < 2:
-                    load = below_ref[2 + comp]
+                    load = from_below(plane(2 + comp))
                 elif place < depth + 2:
                     load = load_ref[comp, place - 2]
                 else:
-                    load = above_ref[2 + 2 * comp + place - depth - 2]
+                    load = from_above(plane(2 + 2 * comp + place - depth - 2))
                 start = load * inverse_here
                 if 2 <= place < depth + 2:
                     z_ref[comp, place - 2] = start
@@ -293,17 +326,19 @@
         return dot_zy, dot_yy
 
     dot_zy, dot_yy = lax.fori_loop(0, rows // 8, second_product, (zeros, zeros))
+    lane_at = lax.broadcasted_iota(jnp.int32, (1, cols), 1)
+    packed = jnp.zeros((1, cols), jnp.float32)
     for at, part in enumerate((dot_load, dot_zz, dot_zy, dot_yy)):
-        dots_ref[at : at + 1] = jnp.sum(part, axis=0, keepdims=True)
-
-
-def last_kernel(
-    dots_ref, other_dots_ref, z_ref, y_ref, quad_ref,
-    displacement_ref, compliance_ref, keep_ref, send1_ref, send2_ref, send3_ref,
-):
-    chip = lax.axis_index("sample") // 2
-    dots = jnp.sum(dots_ref[...] + other_dots_ref[...], axis=1, keepdims=True)
-    dot_load, dot_zz, dot_zy, dot_yy = (dots[at : at + 1] for at in range(4))
+        packed = jnp.where(lane_at == at, jnp.sum(part, keepdims=True), packed)
+    dots_ref[...] = jnp.broadcast_to(packed, dots_ref.shape)
+
+
+def last_kernel(dots_ref, z_ref, y_ref, quad_ref, displacement_ref, compliance_ref, terms_ref):
+    dots = jnp.sum(dots_ref[...], axis=0, keepdims=True)
+    lane_at = lax.broadcasted_iota(jnp.int32, dots.shape, 1)
+    dot_load, dot_zz, dot_zy, dot_yy = (
+        jnp.sum(jnp.where(lane_at == at, dots, 0.0), axis=1, keepdims=True) for at in range(4)
+    )
     first = dot_zz / dot_load
     second = dot_zy / dot_load
     third = dot_yy / dot_load
@@ -315,87 +350,59 @@
         for place in range(z_ref.shape[1]):
             displacement_ref[0, comp, place] = along_z * z_ref[comp, place] + along_y * y_ref[comp, place]
     squares = (along_z * along_z, along_z * along_y, along_y * along_y)
-    share = quad_ref.shape[2] // 4
-    for step, out_ref in enumerate((keep_ref, send1_ref, send2_ref, send3_ref)):
-        span = pl.ds(pl.multiple_of((chip + step) % 4 * share, share), share)
-        for place in range(z_ref.shape[1]):
-            out_ref[place] = sum(squares[at] * quad_ref[at, place, span] for at in range(3))
-
-
-def call(kernel, outs, scratch=(), out_specs=None):
+    samples, depth, share = terms_ref.shape[:3]
+    for sample in range(samples):
+        span = pl.ds(sample * share, share)
+        for place in range(depth):
+            terms_ref[sample, place] = sum(squares[at] * quad_ref[at, place, span] for at in range(3))
+
+
+def call(kernel, outs, inputs, scratch=(), in_memory=pltpu.VMEM, out_specs=None):
     return pl.pallas_call(
         kernel,
         out_shape=outs,
+        in_specs=[pl.BlockSpec(memory_space=in_memory)] * inputs,
         out_specs=out_specs if out_specs is not None else [vmem_spec()] * len(outs),
         scratch_shapes=scratch,
         compiler_params=pltpu.CompilerParams(vmem_limit_bytes=VMEM_LIMIT),
     )
 
 
-def ring_sum(value, offsets, period, base):
-    total = value
-    parts = []
-    for offset in offsets:
-        pairs = []
-        for source in range(lax.axis_size("space")):
-            block = source // period * period
-            pairs.append((source, block + (source - block + offset) % period))
-        parts.append(lax.ppermute(value, "space", pairs))
-    for part in parts:
-        total = total + part
-    return total
-
-
 def per_device(load_field, density, mode_panels, mode_weight, mode_germs):
     depth, rows, cols = density.shape
     slabs = lax.axis_size("space")
     samples = lax.axis_size("sample")
-    own_modes = mode_panels.shape[0]
-    cells = mode_panels.shape[2]
+    own_modes, _, cells = mode_panels.shape
     spread_y, spread_zx = weight_tables(depth, rows, cols)
 
-    keep, send1, send2, send3, going_up, going_down = call(
+    (partial,) = call(
         first_kernel,
-        [f32(2, cells)] * 4 + [f32(5, rows, cols), f32(8, rows, cols)],
-    )(
-        mode_weight.reshape(1, -1),
-        mode_germs,
-        mode_panels.reshape(own_modes, cells),
-        density,
-        load_field,
+        [f32(samples, cells // 128, 128)],
+        inputs=3,
+        scratch=[
+            pltpu.VMEM((1, mode_weight.shape[0]), jnp.float32),
+            pltpu.VMEM(mode_germs.shape, jnp.float32),
+            pltpu.VMEM((own_modes, cells), jnp.bfloat16),
+            pltpu.SemaphoreType.DMA((3,)),
+        ],
+        in_memory=pl.ANY,
+    )(mode_weight.reshape(1, -1), mode_germs, mode_panels.reshape(own_modes, cells))
+    parts = lax.all_to_all(partial, "sample", 0, 0, tiled=True)
+
+    message = f32(8 * rows + 8, cols)
+    sums, pair_out, next_out = call(pack_kernel, [f32(cells // 128, 128), message, message], inputs=3)(
+        parts, density, load_field
     )
-
-    def along_chips(value, offset):
-        return lax.ppermute(
-            value, "sample", [(at, (at + 2 * offset) % samples) for at in range(samples)]
-        )
-
-    def neighbour(value, flip, step):
-        pairs = []
-        for sample in range(samples):
-            for slab in range(slabs):
-                if 0 <= slab + step < slabs:
-                    target = sample ^ 1 if flip else sample
-                    pairs.append((sample * slabs + slab, target * slabs + slab + step))
-        return lax.ppermute(value, BOTH, pairs)
-
-    got = [along_chips(value, step + 1) for step, value in enumerate((send1, send2, send3))]
-    below = neighbour(going_up, False, 1)
-    above = neighbour(going_down, False, -1)
-    sums = keep + got[0] + got[1] + got[2]
-    same, other = sums[0:1], sums[1:2]
-    here = neighbour(other, True, 0)
-    low_other, high_other = neighbour(other, True, 1), neighbour(other, True, -1)
-    low_same, high_same = neighbour(same, False, 1), neighbour(same, False, -1)
+    pairs = [(at, at ^ 1) for at in range(slabs)]
+    nexts = [(at, at + 1) for at in range(1, slabs - 1, 2)]
+    nexts += [(target, source) for source, target in nexts]
+    pair_in = lax.ppermute(pair_out, "space", pairs)
+    next_in = lax.ppermute(next_out, "space", nexts)
 
     z_vec, y_vec, quads, dots = call(
         middle_kernel,
-        [
-            f32(3, depth, rows, cols),
-            f32(3, depth, rows, cols),
-            f32(3, depth, rows, cols),
-            f32(4, cols),
-        ],
+        [f32(3, depth, rows, cols)] * 3 + [f32(slabs, cols)],
+        inputs=7,
         scratch=[
             pltpu.VMEM((depth + 4, rows, cols), jnp.float32),
             pltpu.VMEM((depth + 3, 12, rows, cols), jnp.float32),
@@ -403,30 +410,17 @@
             pltpu.VMEM((depth + 1, 12, rows, cols), jnp.float32),
             pltpu.VMEM((depth + 1, rows, cols), jnp.float32),
         ],
-    )(
-        sums, here, low_other, high_other, low_same, high_same,
-        density, load_field, below, above, spread_y, spread_zx,
-    )
-
-    dots = ring_sum(dots, (8, 16, 24), 32, 0)
-    dots = ring_sum(dots, (2, 4, 6), 8, 0)
-    other_dots = lax.ppermute(dots, "space", [(at, at ^ 1) for at in range(slabs)])
-
-    share = rows // 4
-    displacement, compliance, keep, send1, send2, send3 = call(
+    )(sums, density, load_field, pair_in, next_in, spread_y, spread_zx)
+    dots = lax.all_to_all(dots, "space", 0, 0, tiled=True)
+
+    displacement, compliance, terms = call(
         last_kernel,
-        [f32(1, 3, depth, rows, cols), f32(1)] + [f32(depth, share, cols)] * 4,
-        out_specs=[vmem_spec(), pl.BlockSpec(memory_space=pltpu.SMEM)] + [vmem_spec()] * 4,
-    )(dots, other_dots, z_vec, y_vec, quads)
-
-    got = [along_chips(value, step + 1) for step, value in enumerate((send1, send2, send3))]
-    total = keep + got[0] + got[1] + got[2]
-    halves = total.reshape(depth, 2, share // 2, cols)
-    core = lax.axis_index("sample") % 2
-    own = lax.dynamic_index_in_dim(halves, core, 1, keepdims=False)
-    away = lax.dynamic_index_in_dim(halves, 1 - core, 1, keepdims=False)
-    gradient = own + neighbour(away, True, 0)
-    return displacement, gradient, compliance
+        [f32(1, 3, depth, rows, cols), f32(1), f32(samples, depth, rows // samples, cols)],
+        inputs=4,
+        out_specs=[vmem_spec(), pl.BlockSpec(memory_space=pltpu.SMEM), vmem_spec()],
+    )(dots, z_vec, y_vec, quads)
+    terms = lax.all_to_all(terms, "sample", 0, 0, tiled=True)
+    return displacement, jnp.sum(terms, axis=0), compliance
 
 
 def solution(mesh):

time: 75.1 us -> 62.8 us (0.84)
  starting transfers between devices: 50.7 us -> 2.39 us
  blocking collectives: 0 us -> 44 us
  waiting for transfers between devices: 12.4 us -> 5.29 us
  local copies, waits for them, and re-layouts: 4.95 us -> 4.04 us
    ppermute x21 -> x2, starting transfers between devices: 50.7 us -> 2.39 us  [the longest x1 1.72 us: per_device(): pair_in = lax.ppermute(pair_out, 'space', pairs)]
    all_to_all x0 -> x3, blocking collectives: none -> 44 us  [the longest x1 22.8 us: per_device(): dots = lax.all_to_all(dots, 'space', 0, 0, tiled=True)]
    ppermute x21 -> x2, waiting for transfers between devices: 12.4 us -> 5.29 us  [the longest x1 5.29 us: per_device(): pair_in = lax.ppermute(pair_out, 'space', pairs)]
    unnamed x16, local copies, waits for them, and re-layouts: 4.93 us -> 4.04 us
    pallas_call x3 -> x4, Pallas kernels: 5.16 us -> 5.34 us  [the longest x1 4.06 us: per_device(): call(middle_kernel, [f32(3, depth, rows, cols)] * 3 + [f32(slabs, cols)],...]
  transfers between devices with their start and end apart: 21 -> 2, of which waited for: 10 -> 1; matrix products, arithmetic and copies ran while one was open for 0% -> 0% of each run, Pallas kernels for 0% -> 0%
where the time goes in v2:
time: 62.8 us; the launch traced here: 62.4 us
  blocking collectives  44 us (70%)
  Pallas kernels  5.34 us (9%)
  waiting for transfers between devices  5.29 us (8%)
  local copies, waits for them, and re-layouts  4.04 us (6%)
  starting transfers between devices  2.39 us (4%)
  between operations  0.71 us (1%)
    all_to_all x1, blocking collectives, per_device(): dots = lax.all_to_all(dots, 'space', 0, 0, tiled=True)  22.8 us
    all_to_all x1, blocking collectives, per_device(): terms = lax.all_to_all(terms, 'sample', 0, 0, tiled=True)  11 us
    all_to_all x1, blocking collectives, per_device(): parts = lax.all_to_all(partial, 'sample', 0, 0, tiled=True)  10.3 us
    ppermute x1, waiting for transfers between devices, per_device(): pair_in = lax.ppermute(pair_out, 'space', pairs)  5.29 us
    pallas_call x1, Pallas kernels, per_device(): call(middle_kernel, [f32(3, depth, rows, cols)] * 3 + [f32(slabs, cols)],...  4.06 us
    unnamed x16, local copies, waits for them, and re-layouts  4.04 us
    ppermute x1, starting transfers between devices, per_device(): pair_in = lax.ppermute(pair_out, 'space', pairs)  1.72 us
  transfers between devices with their start and end apart: 2, of which 1 were waited for; matrix products, arithmetic and copies ran while one was open for 0% of the time, Pallas kernels for 0%

profile of v2, /device:TPU:1, one launch (start us, length us, event | category | flops | bytes accessed | tf_op | source)
XLA Modules:
  0.0 62.4 jit_solution(9437711498313769795)
XLA Ops:
  0.6 0.0 copy-start.7
  0.6 0.7 %copy-done.7 = f32[256]{0:T(256)S(1)} copy-done((f32[256]{0:T(256)S(1)}, f32[256]{0:T(256)}, u32[]{:S(2)}) %copy-start.7) | copy-done | bytes 1048
  1.3 0.0 copy-start.5
  1.3 0.8 %copy-done.5 = bf16[32,1,512]{2,0,1:T(8,128)(2,1)S(1)} copy-done((bf16[32,1,512]{2,0,1:T(8,128)(2,1)S(1)}, bf16[32,1,512]{2,0,1:T(8,128)(2,1)}, u32[]{:S(2)}) %copy-start.5) | copy-done | bytes 32792
  2.1 0.0 copy-start.6
  2.1 0.7 %copy-done.6 = f32[8,256]{1,0:T(8,128)S(1)} copy-done((f32[8,256]{1,0:T(8,128)S(1)}, f32[8,256]{1,0:T(8,128)}, u32[]{:S(2)}) %copy-start.6) | copy-done | bytes 8216
  2.8 0.3 shard_map.94
  3.1 0.0 copy-start.4
  3.1 10.3 %all_to_all.21.parts_ref = f32[8,4,128]{2,1,0:T(4,128)S(1)} all-to-all(f32[8,4,128]{2,1,0:T(4,128)S(1)} %shard_map.94), channel_id=1, replica_groups=mesh['sample'=8,'space'=32] {'sample'}, dimensions={0} | all-to-all | bytes 32768 | tf_op jit(solution)/shard_map/all_to_all | solution.py:390
  13.4 0.0 copy-start
  13.4 1.0 %copy-done = f32[3,4,64,128]{3,2,1,0:T(8,128)S(1)} copy-done((f32[3,4,64,128]{3,2,1,0:T(8,128)S(1)}, f32[3,4,64,128]{3,2,1,0:T(8,128)}, u32[]{:S(2)}) %copy-start) | copy-done | bytes 393240
  14.4 0.0 copy-start.2
  14.4 0.9 %copy-done.2 = f32[4,64,128]{2,1,0:T(8,128)S(1)} copy-done((f32[4,64,128]{2,1,0:T(8,128)S(1)}, f32[4,64,128]{2,1,0:T(8,128)}, u32[]{:S(2)}) %copy-start.2) | copy-done | bytes 131096
  15.3 0.0 copy-start.1
  15.3 0.0 copy-start.3
  15.3 1.7 %collective-permute-start = (f32[520,128]{1,0:T(8,128)S(1)}, f32[520,128]{1,0:T(8,128)S(1)}, u32[]{:S(2)}, u32[]{:S(2)}) collective-permute-start(f32[520,128]{1,0:T(8,128)S(1)} %get-tuple-element.14), channel_id=1, source_target_pairs={{0,1},{1,0},{2,3},{3,2},{4,5},{5,4},{6,7},{7,6},{8,9},{9,8},{10,11... | collective-permute-start | bytes 798728 | tf_op jit(solution)/shard_map/ppermute | solution.py:399
  17.1 0.7 %collective-permute-start.1 = (f32[520,128]{1,0:T(8,128)S(1)}, f32[520,128]{1,0:T(8,128)S(1)}, u32[]{:S(2)}, u32[]{:S(2)}) collective-permute-start(f32[520,128]{1,0:T(8,128)S(1)} %get-tuple-element.15), channel_id=1, source_target_pairs={{1,2},{3,4},{5,6},{7,8},{9,10},{11,12},{13,14},{15,16},{17,18},{19... | collective-permute-start | bytes 798728 | tf_op jit(solution)/shard_map/ppermute | solution.py:400
  17.7 5.3 %collective-permute-done.pair_ref = f32[520,128]{1,0:T(8,128)S(1)} collective-permute-done((f32[520,128]{1,0:T(8,128)S(1)}, f32[520,128]{1,0:T(8,128)S(1)}, u32[]{:S(2)}, u32[]{:S(2)}) %collective-permute-start) | collective-permute-done | bytes 266272 | tf_op jit(solution)/shard_map/ppermute | solution.py:399
  23.0 0.0 collective-permute-done.1.next_ref
  23.0 0.0 copy-done.4
  23.0 0.0 copy-done.1
  23.0 0.0 copy-done.3
  23.0 4.1 %shard_map.96 = (f32[3,4,64,128]{3,2,1,0:T(8,128)S(1)}, f32[3,4,64,128]{3,2,1,0:T(8,128)S(1)}, f32[3,4,64,128]{3,2,1,0:T(8,128)S(1)}, f32[32,128]{1,0:T(8,128)S(1)}) custom-call(f32[4,128]{1,0:T(4,128)S(1)} %get-tuple-element.13.sums_ref, f32[4,64,128]{2,1,0:T(8,128)S(1)} %copy-done.2, f32[3,4,64,128]{3,2,1,0:T(8,128)S(1)} %copy-done.1, ...), custom_call_target="tpu_custom_call" | custom-call | tf_op jit(solution)/shard_map/pallas_call | solution.py:402
  27.1 22.8 %all_to_all.22 = f32[32,1,128]{2,1,0:T(1,128)S(1)} all-to-all(f32[32,1,128]{2,1,0:T(1,128)S(1)} %bitcast.8), channel_id=1, replica_groups=mesh['sample'=8,'space'=32] {'space'}, dimensions={0} | all-to-all | bytes 32768 | tf_op jit(solution)/shard_map/all_to_all | solution.py:414
  49.9 0.9 %shard_map.97 = (f32[1,3,4,64,128]{4,3,2,1,0:T(8,128)}, f32[1]{0:T(128)}, f32[8,4,8,128]{3,2,1,0:T(8,128)S(1)}) custom-call(f32[32,128]{1,0:T(8,128)S(1)} %bitcast.6, f32[3,4,64,128]{3,2,1,0:T(8,128)S(1)} %get-tuple-element.17.z_ref, f32[3,4,64,128]{3,2,1,0:T(8,128)S(1)} %get-tuple-element.18.y_ref, f32[3,4,64,128]{3,2,1,0:T(8,128)S(1)} %get-tuple-element.19.quad_ref), custom_call_target="tpu_custom_call" | custom-call | tf_op jit(solution)/shard_map/pallas_call | solution.py:416
  50.8 11.0 %all_to_all.23 = f32[8,4,8,128]{3,2,1,0:T(8,128)S(1)} all-to-all(f32[8,4,8,128]{3,2,1,0:T(8,128)S(1)} %get-tuple-element.21), channel_id=1, replica_groups=mesh['sample'=8,'space'=32] {'sample'}, dimensions={0} | all-to-all | bytes 262144 | tf_op jit(solution)/shard_map/all_to_all | solution.py:422
  61.8 0.6 reduce_sum.9
  (1 shorter events, 0.0 us)
Async XLA Ops:
  0.6 0.7 %copy-start.7 = (f32[256]{0:T(256)S(1)}, f32[256]{0:T(256)}, u32[]{:S(2)}) copy-start(f32[256]{0:T(256)} %param.10) | copy-start | bytes 3076
  1.3 0.8 %copy-start.5 = (bf16[32,1,512]{2,0,1:T(8,128)(2,1)S(1)}, bf16[32,1,512]{2,0,1:T(8,128)(2,1)}, u32[]{:S(2)}) copy-start(bf16[32,1,512]{2,0,1:T(8,128)(2,1)} %param.9) | copy-start | bytes 98308
  2.1 0.7 %copy-start.6 = (f32[8,256]{1,0:T(8,128)S(1)}, f32[8,256]{1,0:T(8,128)}, u32[]{:S(2)}) copy-start(f32[8,256]{1,0:T(8,128)} %germs_hbm.1) | copy-start | bytes 24580
  3.1 19.9 %copy-start.4 = (bf16[128,128]{1,0:T(8,128)(2,1)S(1)}, bf16[128,128]{1,0:T(8,128)(2,1)}, u32[]{:S(2)}) copy-start(bf16[128,128]{1,0:T(8,128)(2,1)} %constant.6.clone.spread_y_ref) | copy-start | bytes 98308
  13.4 1.0 %copy-start = (f32[3,4,64,128]{3,2,1,0:T(8,128)S(1)}, f32[3,4,64,128]{3,2,1,0:T(8,128)}, u32[]{:S(2)}) copy-start(f32[3,4,64,128]{3,2,1,0:T(8,128)} %load_ref.3) | copy-start | bytes 1179652
  14.4 0.9 %copy-start.2 = (f32[4,64,128]{2,1,0:T(8,128)S(1)}, f32[4,64,128]{2,1,0:T(8,128)}, u32[]{:S(2)}) copy-start(f32[4,64,128]{2,1,0:T(8,128)} %density_ref.3) | copy-start | bytes 393220
  15.3 7.8 %copy-start.1 = (f32[3,4,64,128]{3,2,1,0:T(8,128)S(1)}, f32[3,4,64,128]{3,2,1,0:T(8,128)}, u32[]{:S(2)}) copy-start(f32[3,4,64,128]{3,2,1,0:T(8,128)} %load_ref.3) | copy-start | bytes 1179652
  15.3 7.8 %copy-start.3 = (bf16[512,48]{1,0:T(8,128)(2,1)S(1)}, bf16[512,48]{1,0:T(8,128)(2,1)}, u32[]{:S(2)}) copy-start(bf16[512,48]{1,0:T(8,128)(2,1)} %constant.7.clone.spread_zx_ref) | copy-start | bytes 147460
  15.3 7.7 %collective-permute-start = (f32[520,128]{1,0:T(8,128)S(1)}, f32[520,128]{1,0:T(8,128)S(1)}, u32[]{:S(2)}, u32[]{:S(2)}) collective-permute-start(f32[520,128]{1,0:T(8,128)S(1)} %get-tuple-element.14), channel_id=1, source_target_pairs={{0,1},{1,0},{2,3},{3,2},{4,5},{5,4},{6,7},{7,6},{8,9},{9,8},{10,11... | collective-permute-start | bytes 798728 | tf_op jit(solution)/shard_map/ppermute | solution.py:399
  17.1 6.0 %collective-permute-start.1 = (f32[520,128]{1,0:T(8,128)S(1)}, f32[520,128]{1,0:T(8,128)S(1)}, u32[]{:S(2)}, u32[]{:S(2)}) collective-permute-start(f32[520,128]{1,0:T(8,128)S(1)} %get-tuple-element.15), channel_id=1, source_target_pairs={{1,2},{3,4},{5,6},{7,8},{9,10},{11,12},{13,14},{15,16},{17,18},{19... | collective-permute-start | bytes 798728 | tf_op jit(solution)/shard_map/ppermute | solution.py:400

commit v3 on v2

v3 whole, which is shorter than its diff:
```python
import itertools

import jax
import jax.numpy as jnp
import numpy as np
from jax import lax
from jax.experimental import pallas as pl
from jax.experimental.pallas import tpu as pltpu
from jax.sharding import PartitionSpec as P

POISSON = 0.3
LAME = POISSON / ((1.0 + POISSON) * (1.0 - 2.0 * POISSON))
SHEAR = 1.0 / (2.0 * (1.0 + POISSON))
DIAGONAL = (LAME + 2.0 * SHEAR) / 9.0 + 2.0 * SHEAR / 9.0
RATIO = LAME / SHEAR
UNIT = SHEAR / 16.0
VMEM_LIMIT = 48 * 1024 * 1024


def vmem_spec():
    return pl.BlockSpec(memory_space=pltpu.VMEM)


def f32(*shape):
    return jax.ShapeDtypeStruct(shape, jnp.float32)


def split3(value):
    high = value.astype(jnp.bfloat16)
    rest = value - high.astype(jnp.float32)
    mid = rest.astype(jnp.bfloat16)
    low = (rest - mid.astype(jnp.float32)).astype(jnp.bfloat16)
    return high, mid, low


def dot32(left, right):
    return jnp.dot(left, right, preferred_element_type=jnp.float32)


def weight_tables(depth, rows, cols):
    def hat(positions, cells):
        return np.maximum(0.0, 1.0 - np.abs(positions[:, None] - cells[None, :]))

    along_x = hat((np.arange(rows) + 0.5) / 4.0 - 0.5, np.arange(rows // 4))
    along_y = hat((np.arange(cols) + 0.5) / 4.0 - 0.5, np.arange(cols // 4))
    along_z = hat((np.arange(depth + 4) - 2 + 0.5) / 4.0 - 0.5, np.arange(-1, 2))
    spread_y = np.tile(along_y.T, (4, 1))
    spread_zx = np.einsum("pc,xd->pxcd", along_z, along_x).reshape((depth + 4) * rows, -1)
    return spread_y.astype(jnp.bfloat16), spread_zx.astype(jnp.bfloat16)


def first_kernel(
    weight_hbm, germs_hbm, panels_hbm, density_hbm, load_hbm,
    partial_ref, density_ref, load_ref,
    weight, germs, panels, sems,
):
    sample = lax.axis_index("sample")
    copies = [
        pltpu.make_async_copy(source, target, sems.at[at])
        for at, (source, target) in enumerate(
            (
                (weight_hbm, weight),
                (germs_hbm, germs),
                (panels_hbm, panels),
                (density_hbm, density_ref),
                (load_hbm, load_ref),
            )
        )
    ]
    for copy in copies:
        copy.start()
    own_modes = panels.shape[0]
    modes = germs.shape[1]
    mode_at = lax.broadcasted_iota(jnp.int32, (modes, own_modes), 0)
    slot_at = lax.broadcasted_iota(jnp.int32, (modes, own_modes), 1)
    pick = jnp.where(mode_at == slot_at + sample * own_modes, 1.0, 0.0).astype(jnp.bfloat16)
    for copy in copies[:3]:
        copy.wait()
    coefficients = (weight[...] * germs[...]).astype(jnp.bfloat16)
    own_coeff = dot32(coefficients, pick).astype(jnp.bfloat16)
    partial = dot32(own_coeff, panels[...])
    for at in range(partial_ref.shape[1]):
        partial_ref[:, at] = partial[:, at * 128 : (at + 1) * 128]
    for copy in copies[3:]:
        copy.wait()


def pack_kernel(parts_ref, density_ref, load_ref, sums_ref, pair_ref, next_ref):
    slab = lax.axis_index("space")
    planes = (pair_ref.shape[0] - 8) // density_ref.shape[1]
    rows = density_ref.shape[1]
    depth = density_ref.shape[0]
    cells = parts_ref.shape[1]
    sums = jnp.sum(parts_ref[...], axis=0)
    sums_ref[...] = sums

    def fill(up_ref, down_ref):
        up = [density_ref[depth - 2], density_ref[depth - 1]]
        up += [load_ref[comp, depth - 1] for comp in range(3)]
        down = [density_ref[0], density_ref[1]]
        down += [load_ref[comp, place] for comp in range(3) for place in range(2)]
        for ref, parts in ((up_ref, up), (down_ref, down)):
            for at in range(planes):
                ref[at * rows : (at + 1) * rows] = parts[at] if at < len(parts) else jnp.zeros_like(up[0])
            ref[planes * rows : planes * rows + cells] = sums
            ref[planes * rows + cells :] = jnp.zeros((8 - cells, sums.shape[1]), jnp.float32)

    @pl.when(slab % 2 == 0)
    def _():
        fill(pair_ref, next_ref)

    @pl.when(slab % 2 == 1)
    def _():
        fill(next_ref, pair_ref)


def shift_ahead(value, axis, mask):
    return jnp.where(mask, 0.0, pltpu.roll(value, value.shape[axis] - 1, axis))


def shift_back(value, axis, mask):
    return jnp.where(mask, 0.0, pltpu.roll(value, 1, axis))


def store_along_y(target, place, comp, value, last_col):
    ahead = shift_ahead(value, 1, last_col)
    target[place, 2 * comp, 0 : value.shape[0]] = value + ahead
    target[place, 2 * comp + 1, 0 : value.shape[0]] = ahead - value


def load_spread(source, place, chunk):
    parts = []
    for comp in range(3):
        here = [source[place, 2 * comp + mode, pl.ds(chunk * 8, 8)] for mode in range(2)]
        ahead = [source[place, 2 * comp + mode, pl.ds(chunk * 8 + 1, 8)] for mode in range(2)]
        parts += [one + two for one, two in zip(here, ahead)]
        parts += [two - one for one, two in zip(here, ahead)]
    return parts


def element_modes(lower, upper):
    hat = {}
    for comp in range(3):
        for mode_x, mode_y in itertools.product((0, 1), repeat=2):
            at = 4 * comp + 2 * mode_x + mode_y
            if mode_x or mode_y:
                hat[comp, (0, mode_x, mode_y)] = lower[at] + upper[at]
            hat[comp, (1, mode_x, mode_y)] = upper[at] - lower[at]
    return hat


def mode(*axes):
    return tuple(int(axis in axes) for axis in range(3))


def modal_parts(hat):
    shear = {
        (one, two): hat[one, mode(two)] + hat[two, mode(one)] for one, two in ((0, 1), (0, 2), (1, 2))
    }
    trace = hat[0, mode(0)] + hat[1, mode(1)] + hat[2, mode(2)]
    twist = [hat[axis, mode(*(other for other in range(3) if other != axis))] for axis in range(3)]
    bends = {}
    for across in range(3):
        one, two = (axis for axis in range(3) if axis != across)
        bends[across] = (one, two, hat[one, mode(one, across)] + hat[two, mode(two, across)])
    return shear, trace, twist, bends


def modal_forces(hat, weight):
    shear, trace, twist, bends = modal_parts(hat)
    forces = {}
    for (one, two), value in shear.items():
        forces[one, mode(two)] = forces[two, mode(one)] = value * weight
    level = RATIO * trace
    for axis in range(3):
        forces[axis, mode(axis)] = (2.0 * hat[axis, mode(axis)] + level) * weight
    third = (1.0 / 3.0) * weight
    both = twist[0] + twist[1] + twist[2]
    for axis in range(3):
        place = mode(*(other for other in range(3) if other != axis))
        forces[axis, place] = (twist[axis] + both) * third
    for across, (one, two, total) in bends.items():
        extra = (RATIO / 3.0) * total
        for axis in (one, two):
            place = mode(axis, across)
            forces[axis, place] = (hat[axis, place] + extra) * weight
    last = ((RATIO + 4.0) / 9.0) * weight
    for axis in range(3):
        forces[axis, (1, 1, 1)] = hat[axis, (1, 1, 1)] * last
    return forces


def total_of(values):
    values = list(values)
    while len(values) > 1:
        paired = [one + two for one, two in zip(values[::2], values[1::2])]
        values = paired + ([values[-1]] if len(values) % 2 else [])
    return values[0]


def modal_product(left, right):
    return total_of(left[key] * value for key, value in right.items())


def modal_energy(hat):
    shear, trace, twist, bends = modal_parts(hat)

    def squares(values):
        return total_of(value * value for value in values)

    both = twist[0] + twist[1] + twist[2]
    whole = list(shear.values())
    for across, (one, two, _) in bends.items():
        whole += [hat[one, mode(one, across)], hat[two, mode(two, across)]]
    return total_of(
        [
            squares(whole),
            2.0 * squares(hat[axis, mode(axis)] for axis in range(3)),
            RATIO * (trace * trace),
            (1.0 / 3.0) * squares(twist + [both]),
            (RATIO / 3.0) * squares(total for _, _, total in bends.values()),
            ((RATIO + 4.0) / 9.0) * squares(hat[axis, (1, 1, 1)] for axis in range(3)),
        ]
    )


def fold(plane):
    return jnp.sum(plane.reshape(-1, 8, plane.shape[-1]), axis=0)


def middle_kernel(
    sums_ref, density_ref, load_ref, pair_ref, next_ref, spread_y_ref, spread_zx_ref,
    z_ref, y_ref, growth_ref, dots_ref,
    elastic, dense_all, loads, around, inverse, fields, fields_y, near_at, far_at,
):
    slab = lax.axis_index("space")
    slabs = lax.axis_size("space")
    even = slab % 2 == 0
    depth, rows, cols = density_ref.shape
    row_at = lax.broadcasted_iota(jnp.int32, (rows, cols), 0)
    col_at = lax.broadcasted_iota(jnp.int32, (rows, cols), 1)
    first_row = row_at == 0
    first_col, last_col = col_at == 0, col_at == cols - 1
    cells = sums_ref.shape[0]
    extra = pl.ds(pair_ref.shape[0] - 8, cells)

    def from_below(span):
        return jnp.where(even, next_ref[span], pair_ref[span])

    def from_above(span):
        return jnp.where(even, pair_ref[span], next_ref[span])

    def plane(place):
        return pl.ds(place * rows, rows)

    coarse_x, coarse_y = rows // 4, cols // 4
    fold_x = coarse_x // cells
    line_at = lax.broadcasted_iota(jnp.int32, (coarse_x, cols), 0)
    cell_at = lax.broadcasted_iota(jnp.int32, (coarse_x, cols), 1)
    on_line = cell_at // coarse_y == line_at % fold_x
    lines = []
    for coarse in (from_below(extra), sums_ref[...], from_above(extra)):
        tall = jnp.zeros((coarse_x, cols), jnp.float32)
        for at in range(cells):
            tall = jnp.where(line_at // fold_x == at, coarse[at : at + 1], tall)
        lines.append(jnp.where(on_line, tall, 0.0))
    lines = jnp.concatenate(lines, axis=0)
    spread_y = spread_y_ref[...]
    high, mid, low = (dot32(part, spread_y) for part in split3(lines))
    along_y = high + (mid + low)
    spread_zx = spread_zx_ref[...]
    high, mid, low = (dot32(spread_zx, part) for part in split3(along_y))
    growth_ref[...] = jnp.exp(high + (mid + low)).reshape(depth + 4, rows, cols)

    for place in range(2):
        dense_all[place] = from_below(plane(place))
        dense_all[place + depth + 2] = from_above(plane(place))
    dense_all[2 : depth + 2] = density_ref[...]
    for comp in range(3):
        loads[comp, 1] = from_below(plane(2 + comp))
        loads[comp, 2 : depth + 2] = load_ref[comp]
        for place in range(2):
            loads[comp, place + depth + 2] = from_above(plane(2 + 2 * comp + place))
    zero_rows = jnp.zeros((8, cols), jnp.float32)
    for target, first in ((fields, rows), (fields_y, rows), (far_at, 0)):
        for place, at in itertools.product(range(target.shape[0]), range(6)):
            target[place, at, first : first + 8] = zero_rows

    def stiffen(place, carry):
        dense = dense_all[place]
        missing = ((slab == 0) & (place < 2)) | ((slab == slabs - 1) & (place >= depth + 2))
        scale = jnp.where(missing, 0.0, UNIT)
        modulus = growth_ref[place] * (0.001 + dense * dense * dense) * scale
        elastic[place] = modulus
        along = modulus + shift_back(modulus, 1, first_col)
        around[place] = along + shift_back(along, 0, first_row)
        return carry

    lax.fori_loop(0, depth + 4, stiffen, 0, unroll=True)

    def start(place, carry):
        diagonal = (DIAGONAL / UNIT) * (around[place - 1] + around[place])
        missing = ((slab == 0) & (place == 1)) | ((slab == slabs - 1) & (place == depth + 3))
        inverse_here = 1.0 / jnp.where(missing, 1.0, diagonal)
        inverse[place - 1] = inverse_here
        for comp in range(3):
            value = loads[comp, place] * inverse_here
            z_ref[comp, place - 1] = value
            store_along_y(fields, place - 1, comp, value, last_col)
        return carry

    lax.fori_loop(1, depth + 4, start, 0, unroll=True)

    def first_product(chunk, carry):
        lower = load_spread(fields, 0, chunk)
        carried = None
        for place in range(1, depth + 3):
            upper = load_spread(fields, place, chunk)
            forces = modal_forces(element_modes(lower, upper), elastic[place, pl.ds(chunk * 8, 8)])
            passed = []
            for comp in range(3):
                sums = []
                for mode_x, mode_y in itertools.product((0, 1), repeat=2):
                    rise = forces[comp, (1, mode_x, mode_y)]
                    if mode_x or mode_y:
                        level = forces[comp, (0, mode_x, mode_y)]
                        near, far = level - rise, level + rise
                    else:
                        near, far = -rise, rise
                    if carried is not None:
                        sums.append(near + carried[4 * comp + 2 * mode_x + mode_y])
                    passed.append(far)
                if carried is not None:
                    for mode_y in range(2):
                        level, rise = sums[mode_y], sums[2 + mode_y]
                        near_at[place - 2, 2 * comp + mode_y, pl.ds(chunk * 8, 8)] = level - rise
                        far_at[place - 2, 2 * comp + mode_y, pl.ds(chunk * 8 + 8, 8)] = level + rise
            carried = passed
            lower = upper
        return carry

    lax.fori_loop(0, rows // 8, first_product, 0, unroll=True)

    def image_at(place, dots, own):
        dot_load, dot_zz, dot_zy = dots
        scale = inverse[place + 1]
        if not own:
            scale = jnp.where(slab < slabs - 1, scale, 0.0)
        for comp in range(3):
            along = [
                near_at[place, 2 * comp + mode_y] + far_at[place, 2 * comp + mode_y, 7 : rows + 7]
                for mode_y in range(2)
            ]
            image = (along[0] - along[1]) + shift_back(along[0] + along[1], 1, first_col)
            scaled = image * scale
            y_ref[comp, place] = scaled
            if own:
                value = z_ref[comp, place + 1]
                dot_load = dot_load + fold(loads[comp, place + 2] * value)
                dot_zz = dot_zz + fold(value * image)
                dot_zy = dot_zy + fold(scaled * image)
            store_along_y(fields_y, place, comp, scaled, last_col)
        return dot_load, dot_zz, dot_zy

    zeros = jnp.zeros((8, cols), jnp.float32)
    dot_load, dot_zz, dot_zy = lax.fori_loop(
        0, depth, lambda place, dots: image_at(place, dots, True), (zeros,) * 3, unroll=True
    )
    image_at(depth, (zeros,) * 3, False)

    def second_product(chunk, dot_yy):
        lower = load_spread(fields_y, 0, chunk)
        for place in range(depth):
            upper = load_spread(fields_y, place + 1, chunk)
            weight = elastic[place + 2, pl.ds(chunk * 8, 8)]
            dot_yy = dot_yy + weight * modal_energy(element_modes(lower, upper))
            lower = upper
        return dot_yy

    dot_yy = lax.fori_loop(0, rows // 8, second_product, zeros, unroll=True)
    lane_at = lax.broadcasted_iota(jnp.int32, (1, cols), 1)
    packed = jnp.zeros((1, cols), jnp.float32)
    for at, part in enumerate((dot_load, dot_zz, dot_zy, dot_yy)):
        packed = jnp.where(lane_at == at, jnp.sum(part, keepdims=True), packed)
    dots_ref[...] = jnp.broadcast_to(packed, dots_ref.shape)


def energy_kernel(z_ref, y_ref, growth_ref, density_ref, quad_ref, fields, fields_y):
    depth, rows, cols = density_ref.shape
    last_col = lax.broadcasted_iota(jnp.int32, (rows, cols), 1) == cols - 1
    zero_rows = jnp.zeros((8, cols), jnp.float32)

    def spread(place, carry):
        for source, first, target in ((z_ref, 1, fields), (y_ref, 0, fields_y)):
            for comp in range(3):
                store_along_y(target, place, comp, source[comp, place + first], last_col)
            for at in range(6):
                target[place, at, rows : rows + 8] = zero_rows
        return carry

    lax.fori_loop(0, depth + 1, spread, 0)

    def products(chunk, carry):
        span = pl.ds(chunk * 8, 8)
        lower, lower_y = load_spread(fields, 0, chunk), load_spread(fields_y, 0, chunk)
        for place in range(depth):
            upper, upper_y = load_spread(fields, place + 1, chunk), load_spread(fields_y, place + 1, chunk)
            hat, hat_y = element_modes(lower, upper), element_modes(lower_y, upper_y)
            dense = density_ref[place, span]
            weight = (-3.0 / 8.0 * UNIT) * dense * dense * growth_ref[place + 2, span]
            forces = modal_forces(hat, weight)
            quad_ref[0, place, span] = modal_product(hat, forces)
            quad_ref[1, place, span] = 2.0 * modal_product(hat_y, forces)
            quad_ref[2, place, span] = weight * modal_energy(hat_y)
            lower, lower_y = upper, upper_y
        return carry

    lax.fori_loop(0, rows // 8, products, 0)


def solve(dots_ref):
    dots = jnp.sum(dots_ref[...], axis=0, keepdims=True)
    lane_at = lax.broadcasted_iota(jnp.int32, dots.shape, 1)
    dot_load, dot_zz, dot_zy, dot_yy = (
        jnp.sum(jnp.where(lane_at == at, dots, 0.0), axis=1, keepdims=True) for at in range(4)
    )
    first = dot_zz / dot_load
    second = dot_zy / dot_load
    third = dot_yy / dot_load
    under = third * first - second * second
    along_z = (third - first * second) / under
    along_y = (first * first - second) / under
    return dot_load * (along_z + along_y * first), along_z, along_y


def terms_kernel(dots_ref, quad_ref, terms_ref):
    _, along_z, along_y = solve(dots_ref)
    squares = (along_z * along_z, along_z * along_y, along_y * along_y)
    samples, depth, share = terms_ref.shape[:3]
    for sample in range(samples):
        span = pl.ds(sample * share, share)
        for place in range(depth):
            terms_ref[sample, place] = sum(squares[at] * quad_ref[at, place, span] for at in range(3))


def displacement_kernel(dots_ref, z_ref, y_ref, displacement_ref, compliance_ref):
    compliance, along_z, along_y = solve(dots_ref)
    compliance_ref[0] = compliance[0, 0]
    for comp in range(3):
        for place in range(displacement_ref.shape[2]):
            displacement_ref[0, comp, place] = along_z * z_ref[comp, place + 1] + along_y * y_ref[comp, place]


def call(kernel, outs, inputs, scratch=(), in_memory=pltpu.VMEM, out_specs=None):
    return pl.pallas_call(
        kernel,
        out_shape=outs,
        in_specs=[pl.BlockSpec(memory_space=in_memory)] * inputs,
        out_specs=out_specs if out_specs is not None else [vmem_spec()] * len(outs),
        scratch_shapes=scratch,
        compiler_params=pltpu.CompilerParams(vmem_limit_bytes=VMEM_LIMIT),
    )


def per_device(load_field, density, mode_panels, mode_weight, mode_germs):
    depth, rows, cols = density.shape
    slabs = lax.axis_size("space")
    samples = lax.axis_size("sample")
    own_modes, _, cells = mode_panels.shape
    spread_y, spread_zx = weight_tables(depth, rows, cols)

    held_density, held_load = f32(depth, rows, cols), f32(3, depth, rows, cols)
    partial, density, load_field = call(
        first_kernel,
        [f32(samples, cells // 128, 128), held_density, held_load],
        inputs=5,
        scratch=[
            pltpu.VMEM((1, mode_weight.shape[0]), jnp.float32),
            pltpu.VMEM(mode_germs.shape, jnp.float32),
            pltpu.VMEM((own_modes, cells), jnp.bfloat16),
            pltpu.SemaphoreType.DMA((5,)),
        ],
        in_memory=pltpu.HBM,
    )(
        *(
            pltpu.with_memory_space_constraint(value, pltpu.HBM)
            for value in (
                mode_weight.reshape(1, -1),
                mode_germs,
                mode_panels.reshape(own_modes, cells),
                density,
                load_field,
            )
        )
    )
    parts = lax.all_to_all(partial, "sample", 0, 0, tiled=True)

    message = f32(8 * rows + 8, cols)
    sums, pair_out, next_out = call(pack_kernel, [f32(cells // 128, 128), message, message], inputs=3)(
        parts, density, load_field
    )
    pairs = [(at, at ^ 1) for at in range(slabs)]
    nexts = [(at, at + 1) for at in range(1, slabs - 1, 2)]
    nexts += [(target, source) for source, target in nexts]
    pair_in = lax.ppermute(pair_out, "space", pairs)
    next_in = lax.ppermute(next_out, "space", nexts)

    padded = pltpu.VMEM((depth + 1, 6, rows + 8, cols), jnp.float32)
    planes = pltpu.VMEM((depth + 4, rows, cols), jnp.float32)
    z_vec, y_vec, growth, dots = call(
        middle_kernel,
        [
            f32(3, depth + 3, rows, cols),
            f32(3, depth + 1, rows, cols),
            f32(depth + 4, rows, cols),
            f32(slabs, cols),
        ],
        inputs=7,
        scratch=[
            planes,
            planes,
            pltpu.VMEM((3, depth + 4, rows, cols), jnp.float32),
            planes,
            pltpu.VMEM((depth + 3, rows, cols), jnp.float32),
            pltpu.VMEM((depth + 3, 6, rows + 8, cols), jnp.float32),
            padded,
            pltpu.VMEM((depth + 1, 6, rows, cols), jnp.float32),
            padded,
        ],
    )(sums, density, load_field, pair_in, next_in, spread_y, spread_zx)
    dots = lax.all_to_all(dots, "space", 0, 0, tiled=True)
    (quads,) = call(energy_kernel, [f32(3, depth, rows, cols)], inputs=4, scratch=[padded, padded])(
        z_vec, y_vec, growth, density
    )
    (terms,) = call(terms_kernel, [f32(samples, depth, rows // samples, cols)], inputs=2)(dots, quads)
    terms = lax.all_to_all(terms, "sample", 0, 0, tiled=True)
    displacement, compliance = call(
        displacement_kernel,
        [f32(1, 3, depth, rows, cols), f32(1)],
        inputs=3,
        out_specs=[vmem_spec(), pl.BlockSpec(memory_space=pltpu.SMEM)],
    )(dots, z_vec, y_vec)
    return displacement, jnp.sum(terms, axis=0), compliance


def solution(mesh):
    placed = (
        P(None, "space", None, None),
        P("space", None, None),
        P("sample", "space", None),
        P(),
        P(),
    )
    return jax.shard_map(
        per_device,
        mesh=mesh,
        in_specs=placed,
        out_specs=(P("sample", None, "space", None, None), P("space", "sample", None), P("sample")),
        check_vma=False,
    )
```

time: 62.8 us -> 59.6 us (0.949)
  blocking collectives: 44 us -> 10.3 us
  starting transfers between devices: 2.39 us -> 23.3 us
  waiting for transfers between devices: 5.29 us -> 16.4 us
  local copies, waits for them, and re-layouts: 4.04 us -> 0.01 us
  Pallas kernels: 5.34 us -> 8 us
    all_to_all x2 -> x0, blocking collectives: 33.8 us -> none  [the longest x1 22.8 us: per_device(): dots = lax.all_to_all(dots, 'space', 0, 0, tiled=True)]
    all_to_all x0 -> x2, starting transfers between devices: none -> 20.9 us  [the longest x1 14.3 us: per_device(): dots = lax.all_to_all(dots, 'space', 0, 0, tiled=True)]
    all_to_all x0 -> x2, waiting for transfers between devices: none -> 11.1 us  [the longest x1 6.73 us: per_device(): dots = lax.all_to_all(dots, 'space', 0, 0, tiled=True)]
    unnamed x16 -> x4, local copies, waits for them, and re-layouts: 4.04 us -> 0.01 us
    pallas_call x3 -> x5, Pallas kernels: 5.3 us -> 7.96 us  [the longest x1 3.3 us: per_device(): call(middle_kernel, [f32(3, depth + 3, rows, cols), f32(3, depth + 1, row...]
  transfers between devices with their start and end apart: 2 -> 4, of which waited for: 1 -> 3; matrix products, arithmetic and copies ran while one was open for 0% -> 0% of each run, Pallas kernels for 0% -> 5%
where the time goes in v3:
time: 59.6 us; the launch traced here: 59.3 us
  starting transfers between devices  23.3 us (39%)
  waiting for transfers between devices  16.4 us (28%)
  blocking collectives  10.3 us (17%)
  Pallas kernels  8 us (13%)
  between operations  0.69 us (1%)
  other arithmetic  0.62 us (1%)
    all_to_all x1, starting transfers between devices, per_device(): dots = lax.all_to_all(dots, 'space', 0, 0, tiled=True)  14.3 us
    all_to_all x1, blocking collectives, per_device(): parts = lax.all_to_all(partial, 'sample', 0, 0, tiled=True)  10.3 us
    all_to_all x1, waiting for transfers between devices, per_device(): dots = lax.all_to_all(dots, 'space', 0, 0, tiled=True)  6.73 us
    all_to_all x1, starting transfers between devices, per_device(): terms = lax.all_to_all(terms, 'sample', 0, 0, tiled=True)  6.61 us
    ppermute x1, waiting for transfers between devices, per_device(): pair_in = lax.ppermute(pair_out, 'space', pairs)  5.29 us
    all_to_all x1, waiting for transfers between devices, per_device(): terms = lax.all_to_all(terms, 'sample', 0, 0, tiled=True)  4.38 us
    pallas_call x1, Pallas kernels, per_device(): call(middle_kernel, [f32(3, depth + 3, rows, cols), f32(3, depth + 1, row...  3.3 us
    pallas_call x1, Pallas kernels, per_device(): call(energy_kernel, [f32(3, depth, rows, cols)], inputs=4, scratch=[padde...  1.83 us
  transfers between devices with their start and end apart: 4, of which 3 were waited for; matrix products, arithmetic and copies ran while one was open for 0% of the time, Pallas kernels for 5%

profile of v3, /device:TPU:1, one launch (start us, length us, event | category | flops | bytes accessed | tf_op | source)
XLA Modules:
  0.0 59.3 jit_solution(1547059080028639646)
XLA Ops:
  0.6 1.2 %shard_map.94 = (f32[8,4,128]{2,1,0:T(4,128)S(1)}, f32[4,64,128]{2,1,0:T(8,128)S(1)}, f32[3,4,64,128]{3,2,1,0:T(8,128)S(1)}) custom-call(f32[1,256]{1,0:T(1,128)} %bitcast.9, f32[8,256]{1,0:T(8,128)} %germs_hbm.1, bf16[32,512]{1,0:T(8,128)(2,1)} %bitcast.8, f32[4,64,128]{2,1,0:T(8,128)} %density_hbm.1, f32[3,4,64,128]{3,2,1,0:T(8,128)} %load_hbm.1), custom_call_target="tpu_custom_call" | custom-call | tf_op jit(solution)/shard_map/pallas_call | solution.py:473
  1.8 10.3 %all_to_all.21.parts_ref = f32[8,4,128]{2,1,0:T(4,128)S(1)} all-to-all(f32[8,4,128]{2,1,0:T(4,128)S(1)} %get-tuple-element.15), channel_id=1, replica_groups=mesh['sample'=8,'space'=32] {'sample'}, dimensions={0} | all-to-all | bytes 32768 | tf_op jit(solution)/shard_map/all_to_all | solution.py:496
  12.0 0.0 copy-start
  12.0 0.0 copy-start.1
  12.1 1.7 %collective-permute-start = (f32[520,128]{1,0:T(8,128)S(1)}, f32[520,128]{1,0:T(8,128)S(1)}, u32[]{:S(2)}, u32[]{:S(2)}) collective-permute-start(f32[520,128]{1,0:T(8,128)S(1)} %get-tuple-element.19), channel_id=1, source_target_pairs={{0,1},{1,0},{2,3},{3,2},{4,5},{5,4},{6,7},{7,6},{8,9},{9,8},{10,11... | collective-permute-start | bytes 798728 | tf_op jit(solution)/shard_map/ppermute | solution.py:505
  13.8 0.7 %collective-permute-start.1 = (f32[520,128]{1,0:T(8,128)S(1)}, f32[520,128]{1,0:T(8,128)S(1)}, u32[]{:S(2)}, u32[]{:S(2)}) collective-permute-start(f32[520,128]{1,0:T(8,128)S(1)} %get-tuple-element.20), channel_id=1, source_target_pairs={{1,2},{3,4},{5,6},{7,8},{9,10},{11,12},{13,14},{15,16},{17,18},{19... | collective-permute-start | bytes 798728 | tf_op jit(solution)/shard_map/ppermute | solution.py:506
  14.5 5.3 %collective-permute-done.pair_ref = f32[520,128]{1,0:T(8,128)S(1)} collective-permute-done((f32[520,128]{1,0:T(8,128)S(1)}, f32[520,128]{1,0:T(8,128)S(1)}, u32[]{:S(2)}, u32[]{:S(2)}) %collective-permute-start) | collective-permute-done | bytes 266272 | tf_op jit(solution)/shard_map/ppermute | solution.py:505
  19.8 0.0 collective-permute-done.1.next_ref
  19.8 0.0 copy-done
  19.8 0.0 copy-done.1
  19.8 3.3 %shard_map.96 = (f32[3,7,64,128]{3,2,1,0:T(8,128)S(1)}, f32[3,5,64,128]{3,2,1,0:T(8,128)S(1)}, f32[8,64,128]{2,1,0:T(8,128)S(1)}, f32[32,128]{1,0:T(8,128)}) custom-call(f32[4,128]{1,0:T(4,128)S(1)} %get-tuple-element.18.sums_ref, f32[4,64,128]{2,1,0:T(8,128)S(1)} %get-tuple-element.16.density_ref, f32[3,4,64,128]{3,2,1,0:T(8,128)S(1)} %get-tuple-element.17.load_ref, ...), custom_call_target="tpu_custom_call" | custom-call | tf_op jit(solution)/shard_map/pallas_call | solution.py:510
  23.1 14.3 %all-to-all-start.1 = ((f32[32,1,128]{2,1,0:T(1,128)}), f32[32,1,128]{2,1,0:T(1,128)S(1)}, u32[]{:S(2)}, u32[]{:S(2)}) async-start(f32[32,1,128]{2,1,0:T(1,128)} %bitcast.3), calls=%async_computation.1 | async-start | bytes 32768 | tf_op jit(solution)/shard_map/all_to_all | solution.py:531
  37.4 1.8 %shard_map.98.quad_ref = f32[3,4,64,128]{3,2,1,0:T(8,128)S(1)} custom-call(f32[3,7,64,128]{3,2,1,0:T(8,128)S(1)} %get-tuple-element.22.z_ref, f32[3,5,64,128]{3,2,1,0:T(8,128)S(1)} %get-tuple-element.23.y_ref, f32[8,64,128]{2,1,0:T(8,128)S(1)} %get-tuple-element.25.growth_ref, f32[4,64,128]{2,1,0:T(8,128)S(1)} %get-tuple-element.16.density_ref), custom_call_target="tpu_custom_call" | custom-call | tf_op jit(solution)/shard_map/pallas_call | solution.py:532
  39.3 6.7 %all-to-all-done.1 = f32[32,1,128]{2,1,0:T(1,128)S(1)} async-done(((f32[32,1,128]{2,1,0:T(1,128)}), f32[32,1,128]{2,1,0:T(1,128)S(1)}, u32[]{:S(2)}, u32[]{:S(2)}) %all-to-all-start.1) | async-done | bytes 16416 | tf_op jit(solution)/shard_map/all_to_all | solution.py:531
  46.0 0.8 %shard_map.99 = f32[8,4,8,128]{3,2,1,0:T(8,128)} custom-call(f32[32,128]{1,0:T(8,128)S(1)} %bitcast.6, f32[3,4,64,128]{3,2,1,0:T(8,128)S(1)} %shard_map.98.quad_ref), custom_call_target="tpu_custom_call" | custom-call | tf_op jit(solution)/shard_map/pallas_call | solution.py:535
  46.8 6.6 %all-to-all-start.2 = ((f32[8,4,8,128]{3,2,1,0:T(8,128)}), f32[8,4,8,128]{3,2,1,0:T(8,128)S(1)}, u32[]{:S(2)}, u32[]{:S(2)}) async-start(f32[8,4,8,128]{3,2,1,0:T(8,128)} %shard_map.99), calls=%async_computation.2 | async-start | bytes 262144 | tf_op jit(solution)/shard_map/all_to_all | solution.py:536
  53.4 0.9 %shard_map.97 = (f32[1,3,4,64,128]{4,3,2,1,0:T(8,128)}, f32[1]{0:T(128)}) custom-call(f32[32,128]{1,0:T(8,128)S(1)} %bitcast.7, f32[3,7,64,128]{3,2,1,0:T(8,128)S(1)} %get-tuple-element.22.z_ref, f32[3,5,64,128]{3,2,1,0:T(8,128)S(1)} %get-tuple-element.23.y_ref), custom_call_target="tpu_custom_call" | custom-call | tf_op jit(solution)/shard_map/pallas_call | solution.py:537
  54.3 4.4 %all-to-all-done.2 = f32[8,4,8,128]{3,2,1,0:T(8,128)S(1)} async-done(((f32[8,4,8,128]{3,2,1,0:T(8,128)}), f32[8,4,8,128]{3,2,1,0:T(8,128)S(1)}, u32[]{:S(2)}, u32[]{:S(2)}) %all-to-all-start.2) | async-done | bytes 131104 | tf_op jit(solution)/shard_map/all_to_all | solution.py:536
  58.7 0.6 %reduce_sum.9 = f32[4,8,128]{2,1,0:T(8,128)} reduce(f32[8,4,8,128]{3,2,1,0:T(8,128)S(1)} %all-to-all-done.2, f32[]{:T(128)} %constant.2.clone.1), dimensions={0}, to_apply=%region_0.0 | reduce | flops 28672 | bytes 147460 | tf_op jit(solution)/shard_map/reduce_sum | solution.py:543
  (1 shorter events, 0.0 us)
Async XLA Ops:
  12.0 7.8 %copy-start = (bf16[512,48]{1,0:T(8,128)(2,1)S(1)}, bf16[512,48]{1,0:T(8,128)(2,1)}, u32[]{:S(2)}) copy-start(bf16[512,48]{1,0:T(8,128)(2,1)} %constant.7.clone.spread_zx_ref) | copy-start | bytes 147460
  12.0 7.8 %copy-start.1 = (bf16[128,128]{1,0:T(8,128)(2,1)S(1)}, bf16[128,128]{1,0:T(8,128)(2,1)}, u32[]{:S(2)}) copy-start(bf16[128,128]{1,0:T(8,128)(2,1)} %constant.6.clone.spread_y_ref) | copy-start | bytes 98308
  12.1 7.7 %collective-permute-start = (f32[520,128]{1,0:T(8,128)S(1)}, f32[520,128]{1,0:T(8,128)S(1)}, u32[]{:S(2)}, u32[]{:S(2)}) collective-permute-start(f32[520,128]{1,0:T(8,128)S(1)} %get-tuple-element.19), channel_id=1, source_target_pairs={{0,1},{1,0},{2,3},{3,2},{4,5},{5,4},{6,7},{7,6},{8,9},{9,8},{10,11... | collective-permute-start | bytes 798728 | tf_op jit(solution)/shard_map/ppermute | solution.py:505
  13.8 6.0 %collective-permute-start.1 = (f32[520,128]{1,0:T(8,128)S(1)}, f32[520,128]{1,0:T(8,128)S(1)}, u32[]{:S(2)}, u32[]{:S(2)}) collective-permute-start(f32[520,128]{1,0:T(8,128)S(1)} %get-tuple-element.20), channel_id=1, source_target_pairs={{1,2},{3,4},{5,6},{7,8},{9,10},{11,12},{13,14},{15,16},{17,18},{19... | collective-permute-start | bytes 798728 | tf_op jit(solution)/shard_map/ppermute | solution.py:506
  23.1 22.9 %all-to-all-start.1 = ((f32[32,1,128]{2,1,0:T(1,128)}), f32[32,1,128]{2,1,0:T(1,128)S(1)}, u32[]{:S(2)}, u32[]{:S(2)}) async-start(f32[32,1,128]{2,1,0:T(1,128)} %bitcast.3), calls=%async_computation.1 | async-start | bytes 32768 | tf_op jit(solution)/shard_map/all_to_all | solution.py:531
  46.8 11.9 %all-to-all-start.2 = ((f32[8,4,8,128]{3,2,1,0:T(8,128)}), f32[8,4,8,128]{3,2,1,0:T(8,128)S(1)}, u32[]{:S(2)}, u32[]{:S(2)}) async-start(f32[8,4,8,128]{3,2,1,0:T(8,128)} %shard_map.99), calls=%async_computation.2 | async-start | bytes 262144 | tf_op jit(solution)/shard_map/all_to_all | solution.py:536

commit v4 on v3

--- a/solution.py
+++ b/solution.py
@@ -85,33 +85,22 @@
         copy.wait()
 
 
-def pack_kernel(parts_ref, density_ref, load_ref, sums_ref, pair_ref, next_ref):
-    slab = lax.axis_index("space")
-    planes = (pair_ref.shape[0] - 8) // density_ref.shape[1]
+def pack_kernel(parts_ref, density_ref, load_ref, sums_ref, up_ref, down_ref):
     rows = density_ref.shape[1]
     depth = density_ref.shape[0]
     cells = parts_ref.shape[1]
     sums = jnp.sum(parts_ref[...], axis=0)
     sums_ref[...] = sums
-
-    def fill(up_ref, down_ref):
-        up = [density_ref[depth - 2], density_ref[depth - 1]]
-        up += [load_ref[comp, depth - 1] for comp in range(3)]
-        down = [density_ref[0], density_ref[1]]
-        down += [load_ref[comp, place] for comp in range(3) for place in range(2)]
-        for ref, parts in ((up_ref, up), (down_ref, down)):
-            for at in range(planes):
-                ref[at * rows : (at + 1) * rows] = parts[at] if at < len(parts) else jnp.zeros_like(up[0])
-            ref[planes * rows : planes * rows + cells] = sums
-            ref[planes * rows + cells :] = jnp.zeros((8 - cells, sums.shape[1]), jnp.float32)
-
-    @pl.when(slab % 2 == 0)
-    def _():
-        fill(pair_ref, next_ref)
-
-    @pl.when(slab % 2 == 1)
-    def _():
-        fill(next_ref, pair_ref)
+    up = [density_ref[depth - 2], density_ref[depth - 1]]
+    up += [load_ref[comp, depth - 1] for comp in range(3)]
+    down = [density_ref[0], density_ref[1]]
+    down += [load_ref[comp, place] for comp in range(3) for place in range(2)]
+    for ref, parts in ((up_ref, up), (down_ref, down)):
+        for at, part in enumerate(parts):
+            ref[at * rows : (at + 1) * rows] = part
+        first = len(parts) * rows
+        ref[first : first + cells] = sums
+        ref[first + cells :] = jnp.zeros((8 - cells, sums.shape[1]), jnp.float32)
 
 
 def shift_ahead(value, axis, mask):
@@ -229,26 +218,23 @@
 
 
 def middle_kernel(
-    sums_ref, density_ref, load_ref, pair_ref, next_ref, spread_y_ref, spread_zx_ref,
+    sums_ref, density_ref, load_ref, below_ref, above_ref, spread_y_ref, spread_zx_ref,
     z_ref, y_ref, growth_ref, dots_ref,
     elastic, dense_all, loads, around, inverse, fields, fields_y, near_at, far_at,
 ):
     slab = lax.axis_index("space")
     slabs = lax.axis_size("space")
-    even = slab % 2 == 0
     depth, rows, cols = density_ref.shape
     row_at = lax.broadcasted_iota(jnp.int32, (rows, cols), 0)
     col_at = lax.broadcasted_iota(jnp.int32, (rows, cols), 1)
     first_row = row_at == 0
     first_col, last_col = col_at == 0, col_at == cols - 1
     cells = sums_ref.shape[0]
-    extra = pl.ds(pair_ref.shape[0] - 8, cells)
-
     def from_below(span):
-        return jnp.where(even, next_ref[span], pair_ref[span])
+        return below_ref[span]
 
     def from_above(span):
-        return jnp.where(even, pair_ref[span], next_ref[span])
+        return above_ref[span]
 
     def plane(place):
         return pl.ds(place * rows, rows)
@@ -259,7 +245,7 @@
     cell_at = lax.broadcasted_iota(jnp.int32, (coarse_x, cols), 1)
     on_line = cell_at // coarse_y == line_at % fold_x
     lines = []
-    for coarse in (from_below(extra), sums_ref[...], from_above(extra)):
+    for coarse in (from_below(pl.ds(5 * rows, cells)), sums_ref[...], from_above(pl.ds(8 * rows, cells))):
         tall = jnp.zeros((coarse_x, cols), jnp.float32)
         for at in range(cells):
             tall = jnp.where(line_at // fold_x == at, coarse[at : at + 1], tall)
@@ -443,9 +429,12 @@
             terms_ref[sample, place] = sum(squares[at] * quad_ref[at, place, span] for at in range(3))
 
 
-def displacement_kernel(dots_ref, z_ref, y_ref, displacement_ref, compliance_ref):
+def last_kernel(
+    terms_ref, dots_ref, z_ref, y_ref, displacement_ref, gradient_ref, compliance_ref
+):
     compliance, along_z, along_y = solve(dots_ref)
-    compliance_ref[0] = compliance[0, 0]
+    compliance_ref[...] = compliance
+    gradient_ref[...] = jnp.sum(terms_ref[...], axis=0)
     for comp in range(3):
         for place in range(displacement_ref.shape[2]):
             displacement_ref[0, comp, place] = along_z * z_ref[comp, place + 1] + along_y * y_ref[comp, place]
@@ -495,15 +484,13 @@
     )
     parts = lax.all_to_all(partial, "sample", 0, 0, tiled=True)
 
-    message = f32(8 * rows + 8, cols)
-    sums, pair_out, next_out = call(pack_kernel, [f32(cells // 128, 128), message, message], inputs=3)(
-        parts, density, load_field
-    )
-    pairs = [(at, at ^ 1) for at in range(slabs)]
-    nexts = [(at, at + 1) for at in range(1, slabs - 1, 2)]
-    nexts += [(target, source) for source, target in nexts]
-    pair_in = lax.ppermute(pair_out, "space", pairs)
-    next_in = lax.ppermute(next_out, "space", nexts)
+    sums, up, down = call(
+        pack_kernel,
+        [f32(cells // 128, 128), f32(5 * rows + 8, cols), f32(8 * rows + 8, cols)],
+        inputs=3,
+    )(parts, density, load_field)
+    below = lax.ppermute(up, "space", [(at, at + 1) for at in range(slabs - 1)])
+    above = lax.ppermute(down, "space", [(at + 1, at) for at in range(slabs - 1)])
 
     padded = pltpu.VMEM((depth + 1, 6, rows + 8, cols), jnp.float32)
     planes = pltpu.VMEM((depth + 4, rows, cols), jnp.float32)
@@ -527,20 +514,19 @@
             pltpu.VMEM((depth + 1, 6, rows, cols), jnp.float32),
             padded,
         ],
-    )(sums, density, load_field, pair_in, next_in, spread_y, spread_zx)
+    )(sums, density, load_field, below, above, spread_y, spread_zx)
     dots = lax.all_to_all(dots, "space", 0, 0, tiled=True)
     (quads,) = call(energy_kernel, [f32(3, depth, rows, cols)], inputs=4, scratch=[padded, padded])(
         z_vec, y_vec, growth, density
     )
     (terms,) = call(terms_kernel, [f32(samples, depth, rows // samples, cols)], inputs=2)(dots, quads)
     terms = lax.all_to_all(terms, "sample", 0, 0, tiled=True)
-    displacement, compliance = call(
-        displacement_kernel,
-        [f32(1, 3, depth, rows, cols), f32(1)],
-        inputs=3,
-        out_specs=[vmem_spec(), pl.BlockSpec(memory_space=pltpu.SMEM)],
-    )(dots, z_vec, y_vec)
-    return displacement, jnp.sum(terms, axis=0), compliance
+    displacement, gradient, compliance = call(
+        last_kernel,
+        [f32(1, 3, depth, rows, cols), f32(depth, rows // samples, cols), f32(1, 1)],
+        inputs=4,
+    )(terms, dots, z_vec, y_vec)
+    return displacement, gradient, compliance.reshape(1)
 
 
 def solution(mesh):

time: 59.6 us -> 57.4 us (0.963)
  blocking collectives: 10.3 us -> 21 us
  starting transfers between devices: 23.3 us -> 17.3 us
  waiting for transfers between devices: 16.4 us -> 10.8 us
  Pallas kernels: 8 us -> 7.29 us
  other arithmetic: 0.62 us -> 0 us
    all_to_all x0 -> x1, blocking collectives: none -> 10.8 us  [per_device(): terms = lax.all_to_all(terms, 'sample', 0, 0, tiled=True)]
    all_to_all x1 -> x0, starting transfers between devices: 6.61 us -> none  [per_device(): terms = lax.all_to_all(terms, 'sample', 0, 0, tiled=True)]
    all_to_all x1 -> x0, waiting for transfers between devices: 4.38 us -> none  [per_device(): terms = lax.all_to_all(terms, 'sample', 0, 0, tiled=True)]
    ppermute x2, starting transfers between devices: 2.39 us -> 5.6 us  [the longest x1 4.18 us: per_device(): below = lax.ppermute(up, 'space', [(at, at + 1) for at in range(slabs - 1)])]
    all_to_all x1, starting transfers between devices: 14.3 us -> 11.7 us  [per_device(): dots = lax.all_to_all(dots, 'space', 0, 0, tiled=True)]
    ppermute x2, waiting for transfers between devices: 5.29 us -> 4.02 us  [the longest x1 2.77 us: per_device(): below = lax.ppermute(up, 'space', [(at, at + 1) for at in range(slabs - 1)])]
    pallas_call x1, Pallas kernels: 0.77 us -> 0.12 us  [per_device(): call(terms_kernel, [f32(samples, depth, rows // samples, cols)], inputs=2)]
    reduce_sum x1 -> x0, other arithmetic: 0.62 us -> none  [per_device(): return (displacement, jnp.sum(terms, axis=0), compliance)]
  transfers between devices with their start and end apart: 4 -> 3, of which waited for: 3 -> 3; matrix products, arithmetic and copies ran while one was open for 0% -> 0% of each run, Pallas kernels for 5% -> 3%
where the time goes in v4:
time: 57.4 us; the launch traced here: 57.1 us
  blocking collectives  21 us (37%)
  starting transfers between devices  17.3 us (30%)
  waiting for transfers between devices  10.8 us (19%)
  Pallas kernels  7.29 us (13%)
  between operations  0.69 us (1%)
    all_to_all x1, starting transfers between devices, per_device(): dots = lax.all_to_all(dots, 'space', 0, 0, tiled=True)  11.7 us
    all_to_all x1, blocking collectives, per_device(): terms = lax.all_to_all(terms, 'sample', 0, 0, tiled=True)  10.8 us
    all_to_all x1, blocking collectives, per_device(): parts = lax.all_to_all(partial, 'sample', 0, 0, tiled=True)  10.3 us
    all_to_all x1, waiting for transfers between devices, per_device(): dots = lax.all_to_all(dots, 'space', 0, 0, tiled=True)  6.73 us
    ppermute x1, starting transfers between devices, per_device(): below = lax.ppermute(up, 'space', [(at, at + 1) for at in range(slabs - 1)])  4.18 us
    pallas_call x1, Pallas kernels, per_device(): call(middle_kernel, [f32(3, depth + 3, rows, cols), f32(3, depth + 1, row...  3.26 us
    ppermute x1, waiting for transfers between devices, per_device(): below = lax.ppermute(up, 'space', [(at, at + 1) for at in range(slabs - 1)])  2.77 us
    pallas_call x1, Pallas kernels, per_device(): call(energy_kernel, [f32(3, depth, rows, cols)], inputs=4, scratch=[padde...  1.83 us
  transfers between devices with their start and end apart: 3, of which 3 were waited for; matrix products, arithmetic and copies ran while one was open for 0% of the time, Pallas kernels for 3%

profile of v4, /device:TPU:1, one launch (start us, length us, event | category | flops | bytes accessed | tf_op | source)
XLA Modules:
  0.0 57.1 jit_solution(9237387309584058970)
XLA Ops:
  0.6 1.2 %shard_map.94 = (f32[8,4,128]{2,1,0:T(4,128)S(1)}, f32[4,64,128]{2,1,0:T(8,128)S(1)}, f32[3,4,64,128]{3,2,1,0:T(8,128)S(1)}) custom-call(f32[1,256]{1,0:T(1,128)} %bitcast.10, f32[8,256]{1,0:T(8,128)} %germs_hbm.1, bf16[32,512]{1,0:T(8,128)(2,1)} %bitcast.9, f32[4,64,128]{2,1,0:T(8,128)} %density_hbm.1, f32[3,4,64,128]{3,2,1,0:T(8,128)} %load_hbm.1), custom_call_target="tpu_custom_call" | custom-call | tf_op jit(solution)/shard_map/pallas_call | solution.py:462
  1.8 10.3 %all_to_all.21.parts_ref = f32[8,4,128]{2,1,0:T(4,128)S(1)} all-to-all(f32[8,4,128]{2,1,0:T(4,128)S(1)} %get-tuple-element.16), channel_id=1, replica_groups=mesh['sample'=8,'space'=32] {'sample'}, dimensions={0} | all-to-all | bytes 32768 | tf_op jit(solution)/shard_map/all_to_all | solution.py:485
  12.0 0.0 copy-start
  12.0 0.0 copy-start.1
  12.1 1.4 %collective-permute-start.1 = (f32[520,128]{1,0:T(8,128)S(1)}, f32[520,128]{1,0:T(8,128)S(1)}, u32[]{:S(2)}, u32[]{:S(2)}) collective-permute-start(f32[520,128]{1,0:T(8,128)S(1)} %get-tuple-element.21), channel_id=1, source_target_pairs={{1,0},{2,1},{3,2},{4,3},{5,4},{6,5},{7,6},{8,7},{9,8},{10,9},{11,1... | collective-permute-start | bytes 798728 | tf_op jit(solution)/shard_map/ppermute | solution.py:493
  13.5 4.2 %collective-permute-start = (f32[328,128]{1,0:T(8,128)S(1)}, f32[328,128]{1,0:T(8,128)S(1)}, u32[]{:S(2)}, u32[]{:S(2)}) collective-permute-start(f32[328,128]{1,0:T(8,128)S(1)} %get-tuple-element.20), channel_id=1, source_target_pairs={{0,1},{1,2},{2,3},{3,4},{4,5},{5,6},{6,7},{7,8},{8,9},{9,10},{10,1... | collective-permute-start | bytes 503816 | tf_op jit(solution)/shard_map/ppermute | solution.py:492
  17.7 2.8 %collective-permute-done.below_ref = f32[328,128]{1,0:T(8,128)S(1)} collective-permute-done((f32[328,128]{1,0:T(8,128)S(1)}, f32[328,128]{1,0:T(8,128)S(1)}, u32[]{:S(2)}, u32[]{:S(2)}) %collective-permute-start) | collective-permute-done | bytes 167968 | tf_op jit(solution)/shard_map/ppermute | solution.py:492
  20.5 1.2 %collective-permute-done.1.above_ref = f32[520,128]{1,0:T(8,128)S(1)} collective-permute-done((f32[520,128]{1,0:T(8,128)S(1)}, f32[520,128]{1,0:T(8,128)S(1)}, u32[]{:S(2)}, u32[]{:S(2)}) %collective-permute-start.1) | collective-permute-done | bytes 266272 | tf_op jit(solution)/shard_map/ppermute | solution.py:493
  21.7 0.0 copy-done
  21.7 0.0 copy-done.1
  21.7 3.3 %shard_map.96 = (f32[3,7,64,128]{3,2,1,0:T(8,128)S(1)}, f32[3,5,64,128]{3,2,1,0:T(8,128)S(1)}, f32[8,64,128]{2,1,0:T(8,128)S(1)}, f32[32,128]{1,0:T(8,128)}) custom-call(f32[4,128]{1,0:T(4,128)S(1)} %get-tuple-element.19.sums_ref, f32[4,64,128]{2,1,0:T(8,128)S(1)} %get-tuple-element.17.density_ref, f32[3,4,64,128]{3,2,1,0:T(8,128)S(1)} %get-tuple-element.18.load_ref, ...), custom_call_target="tpu_custom_call" | custom-call | tf_op jit(solution)/shard_map/pallas_call | solution.py:497
  25.0 11.7 %all-to-all-start.1 = ((f32[32,1,128]{2,1,0:T(1,128)}), f32[32,1,128]{2,1,0:T(1,128)S(1)}, u32[]{:S(2)}, u32[]{:S(2)}) async-start(f32[32,1,128]{2,1,0:T(1,128)} %bitcast.3), calls=%async_computation.1 | async-start | bytes 32768 | tf_op jit(solution)/shard_map/all_to_all | solution.py:518
  36.7 1.8 %shard_map.97.quad_ref = f32[3,4,64,128]{3,2,1,0:T(8,128)S(1)} custom-call(f32[3,7,64,128]{3,2,1,0:T(8,128)S(1)} %get-tuple-element.23.z_ref, f32[3,5,64,128]{3,2,1,0:T(8,128)S(1)} %get-tuple-element.24.y_ref, f32[8,64,128]{2,1,0:T(8,128)S(1)} %get-tuple-element.25.growth_ref, f32[4,64,128]{2,1,0:T(8,128)S(1)} %get-tuple-element.17.density_ref), custom_call_target="tpu_custom_call" | custom-call | tf_op jit(solution)/shard_map/pallas_call | solution.py:519
  38.6 6.7 %all-to-all-done.1 = f32[32,1,128]{2,1,0:T(1,128)S(1)} async-done(((f32[32,1,128]{2,1,0:T(1,128)}), f32[32,1,128]{2,1,0:T(1,128)S(1)}, u32[]{:S(2)}, u32[]{:S(2)}) %all-to-all-start.1) | async-done | bytes 16416 | tf_op jit(solution)/shard_map/all_to_all | solution.py:518
  45.3 0.1 shard_map.98
  45.4 10.8 %all_to_all.22.terms_ref = f32[8,4,8,128]{3,2,1,0:T(8,128)S(1)} all-to-all(f32[8,4,8,128]{3,2,1,0:T(8,128)S(1)} %shard_map.98), channel_id=1, replica_groups=mesh['sample'=8,'space'=32] {'sample'}, dimensions={0} | all-to-all | bytes 262144 | tf_op jit(solution)/shard_map/all_to_all | solution.py:523
  56.2 0.9 %shard_map.99 = (f32[1,3,4,64,128]{4,3,2,1,0:T(8,128)}, f32[4,8,128]{2,1,0:T(8,128)}, f32[1,1]{1,0:T(1,128)}) custom-call(f32[8,4,8,128]{3,2,1,0:T(8,128)S(1)} %all_to_all.22.terms_ref, f32[32,128]{1,0:T(8,128)S(1)} %bitcast.8, f32[3,7,64,128]{3,2,1,0:T(8,128)S(1)} %get-tuple-element.23.z_ref, f32[3,5,64,128]{3,2,1,0:T(8,128)S(1)} %get-tuple-element.24.y_ref), custom_call_target="tpu_custom_call" | custom-call | tf_op jit(solution)/shard_map/pallas_call | solution.py:524
  (1 shorter events, 0.0 us)
Async XLA Ops:
  12.0 9.7 %copy-start = (bf16[512,48]{1,0:T(8,128)(2,1)S(1)}, bf16[512,48]{1,0:T(8,128)(2,1)}, u32[]{:S(2)}) copy-start(bf16[512,48]{1,0:T(8,128)(2,1)} %constant.5.clone.spread_zx_ref) | copy-start | bytes 147460
  12.0 9.7 %copy-start.1 = (bf16[128,128]{1,0:T(8,128)(2,1)S(1)}, bf16[128,128]{1,0:T(8,128)(2,1)}, u32[]{:S(2)}) copy-start(bf16[128,128]{1,0:T(8,128)(2,1)} %constant.4.clone.spread_y_ref) | copy-start | bytes 98308
  12.1 9.6 %collective-permute-start.1 = (f32[520,128]{1,0:T(8,128)S(1)}, f32[520,128]{1,0:T(8,128)S(1)}, u32[]{:S(2)}, u32[]{:S(2)}) collective-permute-start(f32[520,128]{1,0:T(8,128)S(1)} %get-tuple-element.21), channel_id=1, source_target_pairs={{1,0},{2,1},{3,2},{4,3},{5,4},{6,5},{7,6},{8,7},{9,8},{10,9},{11,1... | collective-permute-start | bytes 798728 | tf_op jit(solution)/shard_map/ppermute | solution.py:493
  13.5 7.0 %collective-permute-start = (f32[328,128]{1,0:T(8,128)S(1)}, f32[328,128]{1,0:T(8,128)S(1)}, u32[]{:S(2)}, u32[]{:S(2)}) collective-permute-start(f32[328,128]{1,0:T(8,128)S(1)} %get-tuple-element.20), channel_id=1, source_target_pairs={{0,1},{1,2},{2,3},{3,4},{4,5},{5,6},{6,7},{7,8},{8,9},{9,10},{10,1... | collective-permute-start | bytes 503816 | tf_op jit(solution)/shard_map/ppermute | solution.py:492
  25.0 20.3 %all-to-all-start.1 = ((f32[32,1,128]{2,1,0:T(1,128)}), f32[32,1,128]{2,1,0:T(1,128)S(1)}, u32[]{:S(2)}, u32[]{:S(2)}) async-start(f32[32,1,128]{2,1,0:T(1,128)} %bitcast.3), calls=%async_computation.1 | async-start | bytes 32768 | tf_op jit(solution)/shard_map/all_to_all | solution.py:518

commit v5 on v4

--- a/solution.py
+++ b/solution.py
@@ -220,7 +220,7 @@
 def middle_kernel(
     sums_ref, density_ref, load_ref, below_ref, above_ref, spread_y_ref, spread_zx_ref,
     z_ref, y_ref, growth_ref, dots_ref,
-    elastic, dense_all, loads, around, inverse, fields, fields_y, near_at, far_at,
+    elastic, around, inverse, fields, fields_y, near_at, far_at,
 ):
     slab = lax.axis_index("space")
     slabs = lax.axis_size("space")
@@ -258,44 +258,48 @@
     high, mid, low = (dot32(spread_zx, part) for part in split3(along_y))
     growth_ref[...] = jnp.exp(high + (mid + low)).reshape(depth + 4, rows, cols)
 
-    for place in range(2):
-        dense_all[place] = from_below(plane(place))
-        dense_all[place + depth + 2] = from_above(plane(place))
-    dense_all[2 : depth + 2] = density_ref[...]
-    for comp in range(3):
-        loads[comp, 1] = from_below(plane(2 + comp))
-        loads[comp, 2 : depth + 2] = load_ref[comp]
-        for place in range(2):
-            loads[comp, place + depth + 2] = from_above(plane(2 + 2 * comp + place))
+    def dense_at(place):
+        if place < 2:
+            return from_below(plane(place))
+        return density_ref[place - 2] if place < depth + 2 else from_above(plane(place - depth - 2))
+
+    def load_at(comp, place):
+        if place < 2:
+            return from_below(plane(2 + comp))
+        if place < depth + 2:
+            return load_ref[comp, place - 2]
+        return from_above(plane(2 + 2 * comp + place - depth - 2))
+
     zero_rows = jnp.zeros((8, cols), jnp.float32)
     for target, first in ((fields, rows), (fields_y, rows), (far_at, 0)):
         for place, at in itertools.product(range(target.shape[0]), range(6)):
             target[place, at, first : first + 8] = zero_rows
 
-    def stiffen(place, carry):
-        dense = dense_all[place]
-        missing = ((slab == 0) & (place < 2)) | ((slab == slabs - 1) & (place >= depth + 2))
-        scale = jnp.where(missing, 0.0, UNIT)
-        modulus = growth_ref[place] * (0.001 + dense * dense * dense) * scale
+    for place in range(depth + 4):
+        dense = dense_at(place)
+        modulus = growth_ref[place] * (0.001 + dense * dense * dense)
+        if place < 2:
+            modulus = modulus * jnp.where(slab == 0, 0.0, UNIT)
+        elif place >= depth + 2:
+            modulus = modulus * jnp.where(slab == slabs - 1, 0.0, UNIT)
+        else:
+            modulus = modulus * UNIT
         elastic[place] = modulus
         along = modulus + shift_back(modulus, 1, first_col)
         around[place] = along + shift_back(along, 0, first_row)
-        return carry
-
-    lax.fori_loop(0, depth + 4, stiffen, 0, unroll=True)
-
-    def start(place, carry):
+
+    for place in range(1, depth + 4):
         diagonal = (DIAGONAL / UNIT) * (around[place - 1] + around[place])
-        missing = ((slab == 0) & (place == 1)) | ((slab == slabs - 1) & (place == depth + 3))
-        inverse_here = 1.0 / jnp.where(missing, 1.0, diagonal)
+        if place == 1:
+            diagonal = jnp.where(slab == 0, 1.0, diagonal)
+        if place == depth + 3:
+            diagonal = jnp.where(slab == slabs - 1, 1.0, diagonal)
+        inverse_here = 1.0 / diagonal
         inverse[place - 1] = inverse_here
         for comp in range(3):
-            value = loads[comp, place] * inverse_here
+            value = load_at(comp, place) * inverse_here
             z_ref[comp, place - 1] = value
             store_along_y(fields, place - 1, comp, value, last_col)
-        return carry
-
-    lax.fori_loop(1, depth + 4, start, 0, unroll=True)
 
     def first_product(chunk, carry):
         lower = load_spread(fields, 0, chunk)
@@ -325,7 +329,7 @@
             lower = upper
         return carry
 
-    lax.fori_loop(0, rows // 8, first_product, 0, unroll=True)
+    lax.fori_loop(0, rows // 8, first_product, 0, unroll=2)
 
     def image_at(place, dots, own):
         dot_load, dot_zz, dot_zy = dots
@@ -342,7 +346,7 @@
             y_ref[comp, place] = scaled
             if own:
                 value = z_ref[comp, place + 1]
-                dot_load = dot_load + fold(loads[comp, place + 2] * value)
+                dot_load = dot_load + fold(load_ref[comp, place] * value)
                 dot_zz = dot_zz + fold(value * image)
                 dot_zy = dot_zy + fold(scaled * image)
             store_along_y(fields_y, place, comp, scaled, last_col)
@@ -506,8 +510,6 @@
         scratch=[
             planes,
             planes,
-            pltpu.VMEM((3, depth + 4, rows, cols), jnp.float32),
-            planes,
             pltpu.VMEM((depth + 3, rows, cols), jnp.float32),
             pltpu.VMEM((depth + 3, 6, rows + 8, cols), jnp.float32),
             padded,

time: 57.4 us -> 57.3 us (level)
  no operation moved by 1% of the time
where the time goes in v5:
time: 57.3 us; the launch traced here: 57 us
  blocking collectives  21 us (37%)
  starting transfers between devices  17.3 us (30%)
  waiting for transfers between devices  10.8 us (19%)
  Pallas kernels  7.19 us (13%)
  between operations  0.69 us (1%)
    all_to_all x1, starting transfers between devices, per_device(): dots = lax.all_to_all(dots, 'space', 0, 0, tiled=True)  11.7 us
    all_to_all x1, blocking collectives, per_device(): terms = lax.all_to_all(terms, 'sample', 0, 0, tiled=True)  10.8 us
    all_to_all x1, blocking collectives, per_device(): parts = lax.all_to_all(partial, 'sample', 0, 0, tiled=True)  10.3 us
    all_to_all x1, waiting for transfers between devices, per_device(): dots = lax.all_to_all(dots, 'space', 0, 0, tiled=True)  6.73 us
    ppermute x1, starting transfers between devices, per_device(): below = lax.ppermute(up, 'space', [(at, at + 1) for at in range(slabs - 1)])  4.18 us
    pallas_call x1, Pallas kernels, per_device(): call(middle_kernel, [f32(3, depth + 3, rows, cols), f32(3, depth + 1, row...  3.16 us
    ppermute x1, waiting for transfers between devices, per_device(): below = lax.ppermute(up, 'space', [(at, at + 1) for at in range(slabs - 1)])  2.77 us
    pallas_call x1, Pallas kernels, per_device(): call(energy_kernel, [f32(3, depth, rows, cols)], inputs=4, scratch=[padde...  1.83 us
  transfers between devices with their start and end apart: 3, of which 3 were waited for; matrix products, arithmetic and copies ran while one was open for 0% of the time, Pallas kernels for 3%

profile of v5, /device:TPU:1, one launch (start us, length us, event | category | flops | bytes accessed | tf_op | source)
XLA Modules:
  0.0 57.0 jit_solution(1282138297297834133)
XLA Ops:
  0.6 1.2 %shard_map.94 = (f32[8,4,128]{2,1,0:T(4,128)S(1)}, f32[4,64,128]{2,1,0:T(8,128)S(1)}, f32[3,4,64,128]{3,2,1,0:T(8,128)S(1)}) custom-call(f32[1,256]{1,0:T(1,128)} %bitcast.10, f32[8,256]{1,0:T(8,128)} %germs_hbm.1, bf16[32,512]{1,0:T(8,128)(2,1)} %bitcast.9, f32[4,64,128]{2,1,0:T(8,128)} %density_hbm.1, f32[3,4,64,128]{3,2,1,0:T(8,128)} %load_hbm.1), custom_call_target="tpu_custom_call" | custom-call | tf_op jit(solution)/shard_map/pallas_call | solution.py:466
  1.8 10.3 %all_to_all.21.parts_ref = f32[8,4,128]{2,1,0:T(4,128)S(1)} all-to-all(f32[8,4,128]{2,1,0:T(4,128)S(1)} %get-tuple-element.16), channel_id=1, replica_groups=mesh['sample'=8,'space'=32] {'sample'}, dimensions={0} | all-to-all | bytes 32768 | tf_op jit(solution)/shard_map/all_to_all | solution.py:489
  12.0 0.0 copy-start
  12.0 0.0 copy-start.1
  12.1 1.4 %collective-permute-start.1 = (f32[520,128]{1,0:T(8,128)S(1)}, f32[520,128]{1,0:T(8,128)S(1)}, u32[]{:S(2)}, u32[]{:S(2)}) collective-permute-start(f32[520,128]{1,0:T(8,128)S(1)} %get-tuple-element.21), channel_id=1, source_target_pairs={{1,0},{2,1},{3,2},{4,3},{5,4},{6,5},{7,6},{8,7},{9,8},{10,9},{11,1... | collective-permute-start | bytes 798728 | tf_op jit(solution)/shard_map/ppermute | solution.py:497
  13.5 4.2 %collective-permute-start = (f32[328,128]{1,0:T(8,128)S(1)}, f32[328,128]{1,0:T(8,128)S(1)}, u32[]{:S(2)}, u32[]{:S(2)}) collective-permute-start(f32[328,128]{1,0:T(8,128)S(1)} %get-tuple-element.20), channel_id=1, source_target_pairs={{0,1},{1,2},{2,3},{3,4},{4,5},{5,6},{6,7},{7,8},{8,9},{9,10},{10,1... | collective-permute-start | bytes 503816 | tf_op jit(solution)/shard_map/ppermute | solution.py:496
  17.7 2.8 %collective-permute-done.below_ref = f32[328,128]{1,0:T(8,128)S(1)} collective-permute-done((f32[328,128]{1,0:T(8,128)S(1)}, f32[328,128]{1,0:T(8,128)S(1)}, u32[]{:S(2)}, u32[]{:S(2)}) %collective-permute-start) | collective-permute-done | bytes 167968 | tf_op jit(solution)/shard_map/ppermute | solution.py:496
  20.5 1.2 %collective-permute-done.1.above_ref = f32[520,128]{1,0:T(8,128)S(1)} collective-permute-done((f32[520,128]{1,0:T(8,128)S(1)}, f32[520,128]{1,0:T(8,128)S(1)}, u32[]{:S(2)}, u32[]{:S(2)}) %collective-permute-start.1) | collective-permute-done | bytes 266272 | tf_op jit(solution)/shard_map/ppermute | solution.py:497
  21.7 0.0 copy-done
  21.7 0.0 copy-done.1
  21.7 3.2 %shard_map.96 = (f32[3,7,64,128]{3,2,1,0:T(8,128)S(1)}, f32[3,5,64,128]{3,2,1,0:T(8,128)S(1)}, f32[8,64,128]{2,1,0:T(8,128)S(1)}, f32[32,128]{1,0:T(8,128)}) custom-call(f32[4,128]{1,0:T(4,128)S(1)} %get-tuple-element.19.sums_ref, f32[4,64,128]{2,1,0:T(8,128)S(1)} %get-tuple-element.17.density_ref, f32[3,4,64,128]{3,2,1,0:T(8,128)S(1)} %get-tuple-element.18.load_ref, ...), custom_call_target="tpu_custom_call" | custom-call | tf_op jit(solution)/shard_map/pallas_call | solution.py:501
  24.9 11.7 %all-to-all-start.1 = ((f32[32,1,128]{2,1,0:T(1,128)}), f32[32,1,128]{2,1,0:T(1,128)S(1)}, u32[]{:S(2)}, u32[]{:S(2)}) async-start(f32[32,1,128]{2,1,0:T(1,128)} %bitcast.3), calls=%async_computation.1 | async-start | bytes 32768 | tf_op jit(solution)/shard_map/all_to_all | solution.py:520
  36.6 1.8 %shard_map.97.quad_ref = f32[3,4,64,128]{3,2,1,0:T(8,128)S(1)} custom-call(f32[3,7,64,128]{3,2,1,0:T(8,128)S(1)} %get-tuple-element.23.z_ref, f32[3,5,64,128]{3,2,1,0:T(8,128)S(1)} %get-tuple-element.24.y_ref, f32[8,64,128]{2,1,0:T(8,128)S(1)} %get-tuple-element.25.growth_ref, f32[4,64,128]{2,1,0:T(8,128)S(1)} %get-tuple-element.17.density_ref), custom_call_target="tpu_custom_call" | custom-call | tf_op jit(solution)/shard_map/pallas_call | solution.py:521
  38.5 6.7 %all-to-all-done.1 = f32[32,1,128]{2,1,0:T(1,128)S(1)} async-done(((f32[32,1,128]{2,1,0:T(1,128)}), f32[32,1,128]{2,1,0:T(1,128)S(1)}, u32[]{:S(2)}, u32[]{:S(2)}) %all-to-all-start.1) | async-done | bytes 16416 | tf_op jit(solution)/shard_map/all_to_all | solution.py:520
  45.2 0.1 shard_map.98
  45.3 10.8 %all_to_all.22.terms_ref = f32[8,4,8,128]{3,2,1,0:T(8,128)S(1)} all-to-all(f32[8,4,8,128]{3,2,1,0:T(8,128)S(1)} %shard_map.98), channel_id=1, replica_groups=mesh['sample'=8,'space'=32] {'sample'}, dimensions={0} | all-to-all | bytes 262144 | tf_op jit(solution)/shard_map/all_to_all | solution.py:525
  56.1 0.9 %shard_map.99 = (f32[1,3,4,64,128]{4,3,2,1,0:T(8,128)}, f32[4,8,128]{2,1,0:T(8,128)}, f32[1,1]{1,0:T(1,128)}) custom-call(f32[8,4,8,128]{3,2,1,0:T(8,128)S(1)} %all_to_all.22.terms_ref, f32[32,128]{1,0:T(8,128)S(1)} %bitcast.8, f32[3,7,64,128]{3,2,1,0:T(8,128)S(1)} %get-tuple-element.23.z_ref, f32[3,5,64,128]{3,2,1,0:T(8,128)S(1)} %get-tuple-element.24.y_ref), custom_call_target="tpu_custom_call" | custom-call | tf_op jit(solution)/shard_map/pallas_call | solution.py:526
  (1 shorter events, 0.0 us)
Async XLA Ops:
  12.0 9.7 %copy-start = (bf16[512,48]{1,0:T(8,128)(2,1)S(1)}, bf16[512,48]{1,0:T(8,128)(2,1)}, u32[]{:S(2)}) copy-start(bf16[512,48]{1,0:T(8,128)(2,1)} %constant.5.clone.spread_zx_ref) | copy-start | bytes 147460
  12.0 9.7 %copy-start.1 = (bf16[128,128]{1,0:T(8,128)(2,1)S(1)}, bf16[128,128]{1,0:T(8,128)(2,1)}, u32[]{:S(2)}) copy-start(bf16[128,128]{1,0:T(8,128)(2,1)} %constant.4.clone.spread_y_ref) | copy-start | bytes 98308
  12.1 9.6 %collective-permute-start.1 = (f32[520,128]{1,0:T(8,128)S(1)}, f32[520,128]{1,0:T(8,128)S(1)}, u32[]{:S(2)}, u32[]{:S(2)}) collective-permute-start(f32[520,128]{1,0:T(8,128)S(1)} %get-tuple-element.21), channel_id=1, source_target_pairs={{1,0},{2,1},{3,2},{4,3},{5,4},{6,5},{7,6},{8,7},{9,8},{10,9},{11,1... | collective-permute-start | bytes 798728 | tf_op jit(solution)/shard_map/ppermute | solution.py:497
  13.5 7.0 %collective-permute-start = (f32[328,128]{1,0:T(8,128)S(1)}, f32[328,128]{1,0:T(8,128)S(1)}, u32[]{:S(2)}, u32[]{:S(2)}) collective-permute-start(f32[328,128]{1,0:T(8,128)S(1)} %get-tuple-element.20), channel_id=1, source_target_pairs={{0,1},{1,2},{2,3},{3,4},{4,5},{5,6},{6,7},{7,8},{8,9},{9,10},{10,1... | collective-permute-start | bytes 503816 | tf_op jit(solution)/shard_map/ppermute | solution.py:496
  24.9 20.3 %all-to-all-start.1 = ((f32[32,1,128]{2,1,0:T(1,128)}), f32[32,1,128]{2,1,0:T(1,128)S(1)}, u32[]{:S(2)}, u32[]{:S(2)}) async-start(f32[32,1,128]{2,1,0:T(1,128)} %bitcast.3), calls=%async_computation.1 | async-start | bytes 32768 | tf_op jit(solution)/shard_map/all_to_all | solution.py:520

commit v6 on v5

--- a/solution.py
+++ b/solution.py
@@ -79,28 +79,41 @@
     coefficients = (weight[...] * germs[...]).astype(jnp.bfloat16)
     own_coeff = dot32(coefficients, pick).astype(jnp.bfloat16)
     partial = dot32(own_coeff, panels[...])
-    for at in range(partial_ref.shape[1]):
-        partial_ref[:, at] = partial[:, at * 128 : (at + 1) * 128]
+    lines = partial_ref.shape[1] // 2
+    for target in range(partial_ref.shape[0]):
+        for at in range(2 * lines):
+            row, line = target // 2 * 2 + at // lines, at % lines
+            partial_ref[target, at : at + 1] = partial[row : row + 1, line * 128 : (line + 1) * 128]
     for copy in copies[3:]:
         copy.wait()
 
 
-def pack_kernel(parts_ref, density_ref, load_ref, sums_ref, up_ref, down_ref):
+def towards_above():
+    core, slab = lax.axis_index("sample") % 2, lax.axis_index("space")
+    return core == slab % 2
+
+
+def pack_kernel(parts_ref, density_ref, load_ref, sums_ref, message_ref):
     rows = density_ref.shape[1]
     depth = density_ref.shape[0]
-    cells = parts_ref.shape[1]
     sums = jnp.sum(parts_ref[...], axis=0)
     sums_ref[...] = sums
-    up = [density_ref[depth - 2], density_ref[depth - 1]]
-    up += [load_ref[comp, depth - 1] for comp in range(3)]
-    down = [density_ref[0], density_ref[1]]
-    down += [load_ref[comp, place] for comp in range(3) for place in range(2)]
-    for ref, parts in ((up_ref, up), (down_ref, down)):
-        for at, part in enumerate(parts):
-            ref[at * rows : (at + 1) * rows] = part
-        first = len(parts) * rows
-        ref[first : first + cells] = sums
-        ref[first + cells :] = jnp.zeros((8 - cells, sums.shape[1]), jnp.float32)
+    message_ref[message_ref.shape[0] - sums.shape[0] :] = sums
+
+    def fill(parts):
+        for at in range(8):
+            part = parts[at] if at < len(parts) else jnp.zeros_like(parts[0])
+            message_ref[at * rows : (at + 1) * rows] = part
+
+    @pl.when(towards_above())
+    def _():
+        up = [density_ref[depth - 2], density_ref[depth - 1]]
+        fill(up + [load_ref[comp, depth - 1] for comp in range(3)])
+
+    @pl.when(jnp.logical_not(towards_above()))
+    def _():
+        down = [density_ref[0], density_ref[1]]
+        fill(down + [load_ref[comp, place] for comp in range(3) for place in range(2)])
 
 
 def shift_ahead(value, axis, mask):
@@ -218,7 +231,7 @@
 
 
 def middle_kernel(
-    sums_ref, density_ref, load_ref, below_ref, above_ref, spread_y_ref, spread_zx_ref,
+    sums_ref, density_ref, load_ref, own_ref, other_ref, spread_y_ref, spread_zx_ref,
     z_ref, y_ref, growth_ref, dots_ref,
     elastic, around, inverse, fields, fields_y, near_at, far_at,
 ):
@@ -229,12 +242,19 @@
     col_at = lax.broadcasted_iota(jnp.int32, (rows, cols), 1)
     first_row = row_at == 0
     first_col, last_col = col_at == 0, col_at == cols - 1
-    cells = sums_ref.shape[0]
+    cells = sums_ref.shape[0] // 2
+    core = lax.axis_index("sample") % 2
+    extra = own_ref.shape[0] - 2 * cells
+    own_above = towards_above()
+
     def from_below(span):
-        return below_ref[span]
+        return jnp.where(own_above, other_ref[span], own_ref[span])
 
     def from_above(span):
-        return above_ref[span]
+        return jnp.where(own_above, own_ref[span], other_ref[span])
+
+    def own_sample(lines):
+        return jnp.where(core == 0, lines[0:cells], lines[cells:])
 
     def plane(place):
         return pl.ds(place * rows, rows)
@@ -245,7 +265,9 @@
     cell_at = lax.broadcasted_iota(jnp.int32, (coarse_x, cols), 1)
     on_line = cell_at // coarse_y == line_at % fold_x
     lines = []
-    for coarse in (from_below(pl.ds(5 * rows, cells)), sums_ref[...], from_above(pl.ds(8 * rows, cells))):
+    last = pl.ds(extra, 2 * cells)
+    for both in (from_below(last), sums_ref[...], from_above(last)):
+        coarse = own_sample(both)
         tall = jnp.zeros((coarse_x, cols), jnp.float32)
         for at in range(cells):
             tall = jnp.where(line_at // fold_x == at, coarse[at : at + 1], tall)
@@ -465,7 +487,7 @@
     held_density, held_load = f32(depth, rows, cols), f32(3, depth, rows, cols)
     partial, density, load_field = call(
         first_kernel,
-        [f32(samples, cells // 128, 128), held_density, held_load],
+        [f32(samples, 2 * cells // 128, 128), held_density, held_load],
         inputs=5,
         scratch=[
             pltpu.VMEM((1, mode_weight.shape[0]), jnp.float32),
@@ -488,13 +510,18 @@
     )
     parts = lax.all_to_all(partial, "sample", 0, 0, tiled=True)
 
-    sums, up, down = call(
-        pack_kernel,
-        [f32(cells // 128, 128), f32(5 * rows + 8, cols), f32(8 * rows + 8, cols)],
-        inputs=3,
-    )(parts, density, load_field)
-    below = lax.ppermute(up, "space", [(at, at + 1) for at in range(slabs - 1)])
-    above = lax.ppermute(down, "space", [(at + 1, at) for at in range(slabs - 1)])
+    lines = 2 * cells // 128
+    sums, message = call(pack_kernel, [f32(lines, 128), f32(8 * rows + lines, cols)], inputs=3)(
+        parts, density, load_field
+    )
+    pairs = []
+    for sample in range(samples):
+        for slab in range(slabs):
+            target = slab + (1 if sample % 2 == slab % 2 else -1)
+            if 0 <= target < slabs:
+                pairs.append((sample * slabs + slab, sample * slabs + target))
+    own = lax.ppermute(message, ("sample", "space"), pairs)
+    other = lax.ppermute(own, "sample", [(at, at ^ 1) for at in range(samples)])
 
     padded = pltpu.VMEM((depth + 1, 6, rows + 8, cols), jnp.float32)
     planes = pltpu.VMEM((depth + 4, rows, cols), jnp.float32)
@@ -516,7 +543,7 @@
             pltpu.VMEM((depth + 1, 6, rows, cols), jnp.float32),
             padded,
         ],
-    )(sums, density, load_field, below, above, spread_y, spread_zx)
+    )(sums, density, load_field, own, other, spread_y, spread_zx)
     dots = lax.all_to_all(dots, "space", 0, 0, tiled=True)
     (quads,) = call(energy_kernel, [f32(3, depth, rows, cols)], inputs=4, scratch=[padded, padded])(
         z_vec, y_vec, growth, density

time: 57.3 us -> 56.2 us (0.981)
  starting transfers between devices: 17.3 us -> 20.4 us
  waiting for transfers between devices: 10.8 us -> 7.9 us
  blocking collectives: 21 us -> 19.8 us
    ppermute x2, starting transfers between devices: 5.6 us -> 9.16 us  [the longest x1 8.35 us: per_device(): other = lax.ppermute(own, 'sample', [(at, at ^ 1) for at in range(samples)])]
    ppermute x2, waiting for transfers between devices: 4.02 us -> 1.17 us  [the longest x1 1.17 us: per_device(): other = lax.ppermute(own, 'sample', [(at, at ^ 1) for at in range(samples)])]
    all_to_all x1, blocking collectives: 10.8 us -> 9.46 us  [per_device(): terms = lax.all_to_all(terms, 'sample', 0, 0, tiled=True)]
  transfers between devices with their start and end apart: 3 -> 3, of which waited for: 3 -> 2; matrix products, arithmetic and copies ran while one was open for 0% -> 0% of each run, Pallas kernels for 3% -> 3%
where the time goes in v6:
time: 56.2 us; the launch traced here: 56 us
  starting transfers between devices  20.4 us (36%)
  blocking collectives  19.8 us (35%)
  waiting for transfers between devices  7.9 us (14%)
  Pallas kernels  7.22 us (13%)
  between operations  0.69 us (1%)
    all_to_all x1, starting transfers between devices, per_device(): dots = lax.all_to_all(dots, 'space', 0, 0, tiled=True)  11.2 us
    all_to_all x1, blocking collectives, per_device(): parts = lax.all_to_all(partial, 'sample', 0, 0, tiled=True)  10.3 us
    all_to_all x1, blocking collectives, per_device(): terms = lax.all_to_all(terms, 'sample', 0, 0, tiled=True)  9.46 us
    ppermute x1, starting transfers between devices, per_device(): other = lax.ppermute(own, 'sample', [(at, at ^ 1) for at in range(samples)])  8.35 us
    all_to_all x1, waiting for transfers between devices, per_device(): dots = lax.all_to_all(dots, 'space', 0, 0, tiled=True)  6.73 us
    pallas_call x1, Pallas kernels, per_device(): call(middle_kernel, [f32(3, depth + 3, rows, cols), f32(3, depth + 1, row...  3.19 us
    pallas_call x1, Pallas kernels, per_device(): call(energy_kernel, [f32(3, depth, rows, cols)], inputs=4, scratch=[padde...  1.83 us
    ppermute x1, waiting for transfers between devices, per_device(): other = lax.ppermute(own, 'sample', [(at, at ^ 1) for at in range(samples)])  1.17 us
  transfers between devices with their start and end apart: 3, of which 2 were waited for; matrix products, arithmetic and copies ran while one was open for 0% of the time, Pallas kernels for 3%

profile of v6, /device:TPU:1, one launch (start us, length us, event | category | flops | bytes accessed | tf_op | source)
XLA Modules:
  0.0 56.0 jit_solution(13692292232812722891)
XLA Ops:
  0.6 1.2 %shard_map.94 = (f32[8,8,128]{2,1,0:T(8,128)S(1)}, f32[4,64,128]{2,1,0:T(8,128)S(1)}, f32[3,4,64,128]{3,2,1,0:T(8,128)S(1)}) custom-call(f32[1,256]{1,0:T(1,128)} %bitcast.10, f32[8,256]{1,0:T(8,128)} %germs_hbm.1, bf16[32,512]{1,0:T(8,128)(2,1)} %bitcast.9, f32[4,64,128]{2,1,0:T(8,128)} %density_hbm.1, f32[3,4,64,128]{3,2,1,0:T(8,128)} %load_hbm.1), custom_call_target="tpu_custom_call" | custom-call | tf_op jit(solution)/shard_map/pallas_call | solution.py:488
  1.8 10.3 %all_to_all.21.parts_ref = f32[8,8,128]{2,1,0:T(8,128)S(1)} all-to-all(f32[8,8,128]{2,1,0:T(8,128)S(1)} %get-tuple-element.15), channel_id=1, replica_groups=mesh['sample'=8,'space'=32] {'sample'}, dimensions={0} | all-to-all | bytes 65536 | tf_op jit(solution)/shard_map/all_to_all | solution.py:511
  12.1 0.0 copy-start
  12.1 0.0 copy-start.1
  12.2 0.8 %collective-permute-start = (f32[520,128]{1,0:T(8,128)S(1)}, f32[520,128]{1,0:T(8,128)S(1)}, u32[]{:S(2)}, u32[]{:S(2)}) collective-permute-start(f32[520,128]{1,0:T(8,128)S(1)} %get-tuple-element.19), channel_id=1, source_target_pairs={{0,1},{1,0},{2,3},{3,2},{4,5},{5,4},{6,7},{7,6},{8,9},{9,8},{10,11... | collective-permute-start | bytes 798728 | tf_op jit(solution)/shard_map/ppermute | solution.py:523
  13.0 0.0 collective-permute-done.own_ref
  13.0 8.3 %collective-permute-start.1 = (f32[520,128]{1,0:T(8,128)S(1)}, f32[520,128]{1,0:T(8,128)S(1)}, u32[]{:S(2)}, u32[]{:S(2)}) collective-permute-start(f32[520,128]{1,0:T(8,128)S(1)} %collective-permute-done.own_ref), channel_id=1, source_target_pairs={{0,32},{32,0},{64,96},{96,64},{128,160},{160,128},{192,224},{224,1... | collective-permute-start | bytes 798728 | tf_op jit(solution)/shard_map/ppermute | solution.py:524
  21.3 1.2 %collective-permute-done.1.other_ref = f32[520,128]{1,0:T(8,128)S(1)} collective-permute-done((f32[520,128]{1,0:T(8,128)S(1)}, f32[520,128]{1,0:T(8,128)S(1)}, u32[]{:S(2)}, u32[]{:S(2)}) %collective-permute-start.1) | collective-permute-done | bytes 266272 | tf_op jit(solution)/shard_map/ppermute | solution.py:524
  22.5 0.0 copy-done
  22.5 0.0 copy-done.1
  22.5 3.2 %shard_map.96 = (f32[3,7,64,128]{3,2,1,0:T(8,128)S(1)}, f32[3,5,64,128]{3,2,1,0:T(8,128)S(1)}, f32[8,64,128]{2,1,0:T(8,128)S(1)}, f32[32,128]{1,0:T(8,128)}) custom-call(f32[8,128]{1,0:T(8,128)S(1)} %get-tuple-element.18.sums_ref, f32[4,64,128]{2,1,0:T(8,128)S(1)} %get-tuple-element.16.density_ref, f32[3,4,64,128]{3,2,1,0:T(8,128)S(1)} %get-tuple-element.17.load_ref, ...), custom_call_target="tpu_custom_call" | custom-call | tf_op jit(solution)/shard_map/pallas_call | solution.py:528
  25.7 11.2 %all-to-all-start.1 = ((f32[32,1,128]{2,1,0:T(1,128)}), f32[32,1,128]{2,1,0:T(1,128)S(1)}, u32[]{:S(2)}, u32[]{:S(2)}) async-start(f32[32,1,128]{2,1,0:T(1,128)} %bitcast.3), calls=%async_computation.1 | async-start | bytes 32768 | tf_op jit(solution)/shard_map/all_to_all | solution.py:547
  36.9 1.8 %shard_map.97.quad_ref = f32[3,4,64,128]{3,2,1,0:T(8,128)S(1)} custom-call(f32[3,7,64,128]{3,2,1,0:T(8,128)S(1)} %get-tuple-element.21.z_ref, f32[3,5,64,128]{3,2,1,0:T(8,128)S(1)} %get-tuple-element.22.y_ref, f32[8,64,128]{2,1,0:T(8,128)S(1)} %get-tuple-element.23.growth_ref, f32[4,64,128]{2,1,0:T(8,128)S(1)} %get-tuple-element.16.density_ref), custom_call_target="tpu_custom_call" | custom-call | tf_op jit(solution)/shard_map/pallas_call | solution.py:548
  38.7 6.7 %all-to-all-done.1 = f32[32,1,128]{2,1,0:T(1,128)S(1)} async-done(((f32[32,1,128]{2,1,0:T(1,128)}), f32[32,1,128]{2,1,0:T(1,128)S(1)}, u32[]{:S(2)}, u32[]{:S(2)}) %all-to-all-start.1) | async-done | bytes 16416 | tf_op jit(solution)/shard_map/all_to_all | solution.py:547
  45.5 0.1 shard_map.98
  45.6 9.5 %all_to_all.22.terms_ref = f32[8,4,8,128]{3,2,1,0:T(8,128)S(1)} all-to-all(f32[8,4,8,128]{3,2,1,0:T(8,128)S(1)} %shard_map.98), channel_id=1, replica_groups=mesh['sample'=8,'space'=32] {'sample'}, dimensions={0} | all-to-all | bytes 262144 | tf_op jit(solution)/shard_map/all_to_all | solution.py:552
  55.1 0.9 %shard_map.99 = (f32[1,3,4,64,128]{4,3,2,1,0:T(8,128)}, f32[4,8,128]{2,1,0:T(8,128)}, f32[1,1]{1,0:T(1,128)}) custom-call(f32[8,4,8,128]{3,2,1,0:T(8,128)S(1)} %all_to_all.22.terms_ref, f32[32,128]{1,0:T(8,128)S(1)} %bitcast.8, f32[3,7,64,128]{3,2,1,0:T(8,128)S(1)} %get-tuple-element.21.z_ref, f32[3,5,64,128]{3,2,1,0:T(8,128)S(1)} %get-tuple-element.22.y_ref), custom_call_target="tpu_custom_call" | custom-call | tf_op jit(solution)/shard_map/pallas_call | solution.py:553
  (1 shorter events, 0.0 us)
Async XLA Ops:
  12.1 10.4 %copy-start = (bf16[512,48]{1,0:T(8,128)(2,1)S(1)}, bf16[512,48]{1,0:T(8,128)(2,1)}, u32[]{:S(2)}) copy-start(bf16[512,48]{1,0:T(8,128)(2,1)} %constant.5.clone.spread_zx_ref) | copy-start | bytes 147460
  12.1 10.4 %copy-start.1 = (bf16[128,128]{1,0:T(8,128)(2,1)S(1)}, bf16[128,128]{1,0:T(8,128)(2,1)}, u32[]{:S(2)}) copy-start(bf16[128,128]{1,0:T(8,128)(2,1)} %constant.4.clone.spread_y_ref) | copy-start | bytes 98308
  12.2 0.8 %collective-permute-start = (f32[520,128]{1,0:T(8,128)S(1)}, f32[520,128]{1,0:T(8,128)S(1)}, u32[]{:S(2)}, u32[]{:S(2)}) collective-permute-start(f32[520,128]{1,0:T(8,128)S(1)} %get-tuple-element.19), channel_id=1, source_target_pairs={{0,1},{1,0},{2,3},{3,2},{4,5},{5,4},{6,7},{7,6},{8,9},{9,8},{10,11... | collective-permute-start | bytes 798728 | tf_op jit(solution)/shard_map/ppermute | solution.py:523
  13.0 9.5 %collective-permute-start.1 = (f32[520,128]{1,0:T(8,128)S(1)}, f32[520,128]{1,0:T(8,128)S(1)}, u32[]{:S(2)}, u32[]{:S(2)}) collective-permute-start(f32[520,128]{1,0:T(8,128)S(1)} %collective-permute-done.own_ref), channel_id=1, source_target_pairs={{0,32},{32,0},{64,96},{96,64},{128,160},{160,128},{192,224},{224,1... | collective-permute-start | bytes 798728 | tf_op jit(solution)/shard_map/ppermute | solution.py:524
  25.7 19.8 %all-to-all-start.1 = ((f32[32,1,128]{2,1,0:T(1,128)}), f32[32,1,128]{2,1,0:T(1,128)S(1)}, u32[]{:S(2)}, u32[]{:S(2)}) async-start(f32[32,1,128]{2,1,0:T(1,128)} %bitcast.3), calls=%async_computation.1 | async-start | bytes 32768 | tf_op jit(solution)/shard_map/all_to_all | solution.py:547

commit v7 on v6

--- a/solution.py
+++ b/solution.py
@@ -397,39 +397,6 @@
     dots_ref[...] = jnp.broadcast_to(packed, dots_ref.shape)
 
 
-def energy_kernel(z_ref, y_ref, growth_ref, density_ref, quad_ref, fields, fields_y):
-    depth, rows, cols = density_ref.shape
-    last_col = lax.broadcasted_iota(jnp.int32, (rows, cols), 1) == cols - 1
-    zero_rows = jnp.zeros((8, cols), jnp.float32)
-
-    def spread(place, carry):
-        for source, first, target in ((z_ref, 1, fields), (y_ref, 0, fields_y)):
-            for comp in range(3):
-                store_along_y(target, place, comp, source[comp, place + first], last_col)
-            for at in range(6):
-                target[place, at, rows : rows + 8] = zero_rows
-        return carry
-
-    lax.fori_loop(0, depth + 1, spread, 0)
-
-    def products(chunk, carry):
-        span = pl.ds(chunk * 8, 8)
-        lower, lower_y = load_spread(fields, 0, chunk), load_spread(fields_y, 0, chunk)
-        for place in range(depth):
-            upper, upper_y = load_spread(fields, place + 1, chunk), load_spread(fields_y, place + 1, chunk)
-            hat, hat_y = element_modes(lower, upper), element_modes(lower_y, upper_y)
-            dense = density_ref[place, span]
-            weight = (-3.0 / 8.0 * UNIT) * dense * dense * growth_ref[place + 2, span]
-            forces = modal_forces(hat, weight)
-            quad_ref[0, place, span] = modal_product(hat, forces)
-            quad_ref[1, place, span] = 2.0 * modal_product(hat_y, forces)
-            quad_ref[2, place, span] = weight * modal_energy(hat_y)
-            lower, lower_y = upper, upper_y
-        return carry
-
-    lax.fori_loop(0, rows // 8, products, 0)
-
-
 def solve(dots_ref):
     dots = jnp.sum(dots_ref[...], axis=0, keepdims=True)
     lane_at = lax.broadcasted_iota(jnp.int32, dots.shape, 1)
@@ -445,14 +412,26 @@
     return dot_load * (along_z + along_y * first), along_z, along_y
 
 
-def terms_kernel(dots_ref, quad_ref, terms_ref):
+def terms_kernel(dots_ref, z_ref, y_ref, growth_ref, density_ref, terms_ref, fields):
     _, along_z, along_y = solve(dots_ref)
-    squares = (along_z * along_z, along_z * along_y, along_y * along_y)
-    samples, depth, share = terms_ref.shape[:3]
-    for sample in range(samples):
-        span = pl.ds(sample * share, share)
+    depth, rows, cols = density_ref.shape
+    last_col = lax.broadcasted_iota(jnp.int32, (rows, cols), 1) == cols - 1
+    zero_rows = jnp.zeros((8, cols), jnp.float32)
+    for place in range(depth + 1):
+        for comp in range(3):
+            value = along_z * z_ref[comp, place + 1] + along_y * y_ref[comp, place]
+            store_along_y(fields, place, comp, value, last_col)
+        for at in range(6):
+            fields[place, at, rows : rows + 8] = zero_rows
+    for chunk in range(rows // 8):
+        span = pl.ds(chunk * 8, 8)
+        lower = load_spread(fields, 0, chunk)
         for place in range(depth):
-            terms_ref[sample, place] = sum(squares[at] * quad_ref[at, place, span] for at in range(3))
+            upper = load_spread(fields, place + 1, chunk)
+            dense = density_ref[place, span]
+            share = (-3.0 / 8.0 * UNIT) * dense * dense * growth_ref[place + 2, span]
+            terms_ref[chunk, place] = share * modal_energy(element_modes(lower, upper))
+            lower = upper
 
 
 def last_kernel(
@@ -545,10 +524,9 @@
         ],
     )(sums, density, load_field, own, other, spread_y, spread_zx)
     dots = lax.all_to_all(dots, "space", 0, 0, tiled=True)
-    (quads,) = call(energy_kernel, [f32(3, depth, rows, cols)], inputs=4, scratch=[padded, padded])(
-        z_vec, y_vec, growth, density
-    )
-    (terms,) = call(terms_kernel, [f32(samples, depth, rows // samples, cols)], inputs=2)(dots, quads)
+    (terms,) = call(
+        terms_kernel, [f32(samples, depth, rows // samples, cols)], inputs=5, scratch=[padded]
+    )(dots, z_vec, y_vec, growth, density)
     terms = lax.all_to_all(terms, "sample", 0, 0, tiled=True)
     displacement, gradient, compliance = call(
         last_kernel,

time: 56.2 us -> 56.1 us (level)
  blocking collectives: 19.8 us -> 39.4 us
  starting transfers between devices: 20.4 us -> 9.16 us
  waiting for transfers between devices: 7.9 us -> 1.17 us
  Pallas kernels: 7.22 us -> 5.46 us
    all_to_all x0 -> x1, blocking collectives: none -> 19.6 us  [per_device(): dots = lax.all_to_all(dots, 'space', 0, 0, tiled=True)]
    all_to_all x1 -> x0, starting transfers between devices: 11.2 us -> none  [per_device(): dots = lax.all_to_all(dots, 'space', 0, 0, tiled=True)]
    all_to_all x1 -> x0, waiting for transfers between devices: 6.73 us -> none  [per_device(): dots = lax.all_to_all(dots, 'space', 0, 0, tiled=True)]
    pallas_call x2 -> x1, Pallas kernels: 1.95 us -> 0.77 us  [per_device(): call(terms_kernel, [f32(samples, depth, rows // samples, cols)], inputs=5...]
    pallas_call x1, Pallas kernels: 3.19 us -> 2.6 us  [per_device(): call(middle_kernel, [f32(3, depth + 3, rows, cols), f32(3, depth + 1, row...]
  transfers between devices with their start and end apart: 3 -> 2, of which waited for: 2 -> 1; matrix products, arithmetic and copies ran while one was open for 0% -> 0% of each run, Pallas kernels for 3% -> 0%
where the time goes in v7:
time: 56.1 us; the launch traced here: 55.9 us
  blocking collectives  39.4 us (70%)
  starting transfers between devices  9.16 us (16%)
  Pallas kernels  5.46 us (10%)
  waiting for transfers between devices  1.17 us (2%)
  between operations  0.68 us (1%)
    all_to_all x1, blocking collectives, per_device(): dots = lax.all_to_all(dots, 'space', 0, 0, tiled=True)  19.6 us
    all_to_all x1, blocking collectives, per_device(): parts = lax.all_to_all(partial, 'sample', 0, 0, tiled=True)  10.3 us
    all_to_all x1, blocking collectives, per_device(): terms = lax.all_to_all(terms, 'sample', 0, 0, tiled=True)  9.46 us
    ppermute x1, starting transfers between devices, per_device(): other = lax.ppermute(own, 'sample', [(at, at ^ 1) for at in range(samples)])  8.35 us
    pallas_call x1, Pallas kernels, per_device(): call(middle_kernel, [f32(3, depth + 3, rows, cols), f32(3, depth + 1, row...  2.6 us
    ppermute x1, waiting for transfers between devices, per_device(): other = lax.ppermute(own, 'sample', [(at, at ^ 1) for at in range(samples)])  1.17 us
    pallas_call x1, Pallas kernels, per_device(): call(first_kernel, [f32(samples, 2 * cells // 128, 128), held_density, he...  1.16 us
  transfers between devices with their start and end apart: 2, of which 1 were waited for; matrix products, arithmetic and copies ran while one was open for 0% of the time, Pallas kernels for 0%

profile of v7, /device:TPU:1, one launch (start us, length us, event | category | flops | bytes accessed | tf_op | source)
XLA Modules:
  0.0 55.9 jit_solution(12986114833035435746)
XLA Ops:
  0.6 1.2 %shard_map.94 = (f32[8,8,128]{2,1,0:T(8,128)S(1)}, f32[4,64,128]{2,1,0:T(8,128)S(1)}, f32[3,4,64,128]{3,2,1,0:T(8,128)S(1)}) custom-call(f32[1,256]{1,0:T(1,128)} %bitcast.11, f32[8,256]{1,0:T(8,128)} %germs_hbm.1, bf16[32,512]{1,0:T(8,128)(2,1)} %bitcast.10, f32[4,64,128]{2,1,0:T(8,128)} %density_hbm.1, f32[3,4,64,128]{3,2,1,0:T(8,128)} %load_hbm.1), custom_call_target="tpu_custom_call" | custom-call | tf_op jit(solution)/shard_map/pallas_call | solution.py:467
  1.8 10.3 %all_to_all.21.parts_ref = f32[8,8,128]{2,1,0:T(8,128)S(1)} all-to-all(f32[8,8,128]{2,1,0:T(8,128)S(1)} %get-tuple-element.15), channel_id=1, replica_groups=mesh['sample'=8,'space'=32] {'sample'}, dimensions={0} | all-to-all | bytes 65536 | tf_op jit(solution)/shard_map/all_to_all | solution.py:490
  12.1 0.0 copy-start
  12.1 0.0 copy-start.1
  12.2 0.8 %collective-permute-start = (f32[520,128]{1,0:T(8,128)S(1)}, f32[520,128]{1,0:T(8,128)S(1)}, u32[]{:S(2)}, u32[]{:S(2)}) collective-permute-start(f32[520,128]{1,0:T(8,128)S(1)} %get-tuple-element.19), channel_id=1, source_target_pairs={{0,1},{1,0},{2,3},{3,2},{4,5},{5,4},{6,7},{7,6},{8,9},{9,8},{10,11... | collective-permute-start | bytes 798728 | tf_op jit(solution)/shard_map/ppermute | solution.py:502
  13.0 0.0 collective-permute-done.own_ref
  13.0 8.3 %collective-permute-start.1 = (f32[520,128]{1,0:T(8,128)S(1)}, f32[520,128]{1,0:T(8,128)S(1)}, u32[]{:S(2)}, u32[]{:S(2)}) collective-permute-start(f32[520,128]{1,0:T(8,128)S(1)} %collective-permute-done.own_ref), channel_id=1, source_target_pairs={{0,32},{32,0},{64,96},{96,64},{128,160},{160,128},{192,224},{224,1... | collective-permute-start | bytes 798728 | tf_op jit(solution)/shard_map/ppermute | solution.py:503
  21.3 1.2 %collective-permute-done.1.other_ref = f32[520,128]{1,0:T(8,128)S(1)} collective-permute-done((f32[520,128]{1,0:T(8,128)S(1)}, f32[520,128]{1,0:T(8,128)S(1)}, u32[]{:S(2)}, u32[]{:S(2)}) %collective-permute-start.1) | collective-permute-done | bytes 266272 | tf_op jit(solution)/shard_map/ppermute | solution.py:503
  22.5 0.0 copy-done
  22.5 0.0 copy-done.1
  22.5 2.6 %shard_map.96 = (f32[3,7,64,128]{3,2,1,0:T(8,128)S(1)}, f32[3,5,64,128]{3,2,1,0:T(8,128)S(1)}, f32[8,64,128]{2,1,0:T(8,128)S(1)}, f32[32,128]{1,0:T(8,128)S(1)}) custom-call(f32[8,128]{1,0:T(8,128)S(1)} %get-tuple-element.18.sums_ref, f32[4,64,128]{2,1,0:T(8,128)S(1)} %get-tuple-element.16.density_ref, f32[3,4,64,128]{3,2,1,0:T(8,128)S(1)} %get-tuple-element.17.load_ref, ...), custom_call_target="tpu_custom_call" | custom-call | tf_op jit(solution)/shard_map/pallas_call | solution.py:507
  25.1 19.6 %all_to_all.22 = f32[32,1,128]{2,1,0:T(1,128)S(1)} all-to-all(f32[32,1,128]{2,1,0:T(1,128)S(1)} %bitcast.9), channel_id=1, replica_groups=mesh['sample'=8,'space'=32] {'space'}, dimensions={0} | all-to-all | bytes 32768 | tf_op jit(solution)/shard_map/all_to_all | solution.py:526
  44.8 0.8 %shard_map.97 = f32[8,4,8,128]{3,2,1,0:T(8,128)S(1)} custom-call(f32[32,128]{1,0:T(8,128)S(1)} %bitcast.7, f32[3,7,64,128]{3,2,1,0:T(8,128)S(1)} %get-tuple-element.21.z_ref, f32[3,5,64,128]{3,2,1,0:T(8,128)S(1)} %get-tuple-element.22.y_ref, f32[8,64,128]{2,1,0:T(8,128)S(1)} %get-tuple-element.23.growth_ref, f32[4,64,128]{2,1,0:T(8,128)S(1)} %get-tuple-element.16.density_ref), custom_call_target="tpu_custom_call" | custom-call | tf_op jit(solution)/shard_map/pallas_call | solution.py:527
  45.5 9.5 %all_to_all.23.terms_ref = f32[8,4,8,128]{3,2,1,0:T(8,128)S(1)} all-to-all(f32[8,4,8,128]{3,2,1,0:T(8,128)S(1)} %shard_map.97), channel_id=1, replica_groups=mesh['sample'=8,'space'=32] {'sample'}, dimensions={0} | all-to-all | bytes 262144 | tf_op jit(solution)/shard_map/all_to_all | solution.py:530
  55.0 0.9 %shard_map.98 = (f32[1,3,4,64,128]{4,3,2,1,0:T(8,128)}, f32[4,8,128]{2,1,0:T(8,128)}, f32[1,1]{1,0:T(1,128)}) custom-call(f32[8,4,8,128]{3,2,1,0:T(8,128)S(1)} %all_to_all.23.terms_ref, f32[32,128]{1,0:T(8,128)S(1)} %bitcast.8, f32[3,7,64,128]{3,2,1,0:T(8,128)S(1)} %get-tuple-element.21.z_ref, f32[3,5,64,128]{3,2,1,0:T(8,128)S(1)} %get-tuple-element.22.y_ref), custom_call_target="tpu_custom_call" | custom-call | tf_op jit(solution)/shard_map/pallas_call | solution.py:531
  (1 shorter events, 0.0 us)
Async XLA Ops:
  12.1 10.4 %copy-start = (bf16[512,48]{1,0:T(8,128)(2,1)S(1)}, bf16[512,48]{1,0:T(8,128)(2,1)}, u32[]{:S(2)}) copy-start(bf16[512,48]{1,0:T(8,128)(2,1)} %constant.5.clone.spread_zx_ref) | copy-start | bytes 147460
  12.1 10.4 %copy-start.1 = (bf16[128,128]{1,0:T(8,128)(2,1)S(1)}, bf16[128,128]{1,0:T(8,128)(2,1)}, u32[]{:S(2)}) copy-start(bf16[128,128]{1,0:T(8,128)(2,1)} %constant.4.clone.spread_y_ref) | copy-start | bytes 98308
  12.2 0.8 %collective-permute-start = (f32[520,128]{1,0:T(8,128)S(1)}, f32[520,128]{1,0:T(8,128)S(1)}, u32[]{:S(2)}, u32[]{:S(2)}) collective-permute-start(f32[520,128]{1,0:T(8,128)S(1)} %get-tuple-element.19), channel_id=1, source_target_pairs={{0,1},{1,0},{2,3},{3,2},{4,5},{5,4},{6,7},{7,6},{8,9},{9,8},{10,11... | collective-permute-start | bytes 798728 | tf_op jit(solution)/shard_map/ppermute | solution.py:502
  13.0 9.5 %collective-permute-start.1 = (f32[520,128]{1,0:T(8,128)S(1)}, f32[520,128]{1,0:T(8,128)S(1)}, u32[]{:S(2)}, u32[]{:S(2)}) collective-permute-start(f32[520,128]{1,0:T(8,128)S(1)} %collective-permute-done.own_ref), channel_id=1, source_target_pairs={{0,32},{32,0},{64,96},{96,64},{128,160},{160,128},{192,224},{224,1... | collective-permute-start | bytes 798728 | tf_op jit(solution)/shard_map/ppermute | solution.py:503

commit v8 on v7

--- a/solution.py
+++ b/solution.py
@@ -412,7 +412,9 @@
     return dot_load * (along_z + along_y * first), along_z, along_y
 
 
-def terms_kernel(dots_ref, z_ref, y_ref, growth_ref, density_ref, terms_ref, fields):
+def terms_kernel(
+    dots_ref, z_ref, y_ref, growth_ref, density_ref, terms_ref, displacement_hbm, fields, held, sem
+):
     _, along_z, along_y = solve(dots_ref)
     depth, rows, cols = density_ref.shape
     last_col = lax.broadcasted_iota(jnp.int32, (rows, cols), 1) == cols - 1
@@ -421,8 +423,12 @@
         for comp in range(3):
             value = along_z * z_ref[comp, place + 1] + along_y * y_ref[comp, place]
             store_along_y(fields, place, comp, value, last_col)
+            if place < depth:
+                held[comp, place] = value
         for at in range(6):
             fields[place, at, rows : rows + 8] = zero_rows
+    copy = pltpu.make_async_copy(held, displacement_hbm.at[0], sem)
+    copy.start()
     for chunk in range(rows // 8):
         span = pl.ds(chunk * 8, 8)
         lower = load_spread(fields, 0, chunk)
@@ -432,17 +438,12 @@
             share = (-3.0 / 8.0 * UNIT) * dense * dense * growth_ref[place + 2, span]
             terms_ref[chunk, place] = share * modal_energy(element_modes(lower, upper))
             lower = upper
-
-
-def last_kernel(
-    terms_ref, dots_ref, z_ref, y_ref, displacement_ref, gradient_ref, compliance_ref
-):
-    compliance, along_z, along_y = solve(dots_ref)
-    compliance_ref[...] = compliance
+    copy.wait()
+
+
+def last_kernel(terms_ref, dots_ref, gradient_ref, compliance_ref):
     gradient_ref[...] = jnp.sum(terms_ref[...], axis=0)
-    for comp in range(3):
-        for place in range(displacement_ref.shape[2]):
-            displacement_ref[0, comp, place] = along_z * z_ref[comp, place + 1] + along_y * y_ref[comp, place]
+    compliance_ref[...] = solve(dots_ref)[0]
 
 
 def call(kernel, outs, inputs, scratch=(), in_memory=pltpu.VMEM, out_specs=None):
@@ -524,15 +525,21 @@
         ],
     )(sums, density, load_field, own, other, spread_y, spread_zx)
     dots = lax.all_to_all(dots, "space", 0, 0, tiled=True)
-    (terms,) = call(
-        terms_kernel, [f32(samples, depth, rows // samples, cols)], inputs=5, scratch=[padded]
+    terms, displacement = call(
+        terms_kernel,
+        [f32(samples, depth, rows // samples, cols), f32(1, 3, depth, rows, cols)],
+        inputs=5,
+        scratch=[
+            padded,
+            pltpu.VMEM((3, depth, rows, cols), jnp.float32),
+            pltpu.SemaphoreType.DMA,
+        ],
+        out_specs=[vmem_spec(), pl.BlockSpec(memory_space=pl.ANY)],
     )(dots, z_vec, y_vec, growth, density)
     terms = lax.all_to_all(terms, "sample", 0, 0, tiled=True)
-    displacement, gradient, compliance = call(
-        last_kernel,
-        [f32(1, 3, depth, rows, cols), f32(depth, rows // samples, cols), f32(1, 1)],
-        inputs=4,
-    )(terms, dots, z_vec, y_vec)
+    gradient, compliance = call(
+        last_kernel, [f32(depth, rows // samples, cols), f32(1, 1)], inputs=2
+    )(terms, dots)
     return displacement, gradient, compliance.reshape(1)
 
 

time: 56.1 us -> 56 us (level)
  no operation moved by 1% of the time
where the time goes in v8:
time: 56 us; the launch traced here: 55.8 us
  blocking collectives  39.4 us (70%)
  starting transfers between devices  9.16 us (16%)
  Pallas kernels  5.32 us (10%)
  waiting for transfers between devices  1.17 us (2%)
  between operations  0.68 us (1%)
    all_to_all x1, blocking collectives, per_device(): dots = lax.all_to_all(dots, 'space', 0, 0, tiled=True)  19.6 us
    all_to_all x1, blocking collectives, per_device(): parts = lax.all_to_all(partial, 'sample', 0, 0, tiled=True)  10.3 us
    all_to_all x1, blocking collectives, per_device(): terms = lax.all_to_all(terms, 'sample', 0, 0, tiled=True)  9.46 us
    ppermute x1, starting transfers between devices, per_device(): other = lax.ppermute(own, 'sample', [(at, at ^ 1) for at in range(samples)])  8.35 us
    pallas_call x1, Pallas kernels, per_device(): call(middle_kernel, [f32(3, depth + 3, rows, cols), f32(3, depth + 1, row...  2.6 us
    ppermute x1, waiting for transfers between devices, per_device(): other = lax.ppermute(own, 'sample', [(at, at ^ 1) for at in range(samples)])  1.17 us
    pallas_call x1, Pallas kernels, per_device(): call(first_kernel, [f32(samples, 2 * cells // 128, 128), held_density, he...  1.16 us
  transfers between devices with their start and end apart: 2, of which 1 were waited for; matrix products, arithmetic and copies ran while one was open for 0% of the time, Pallas kernels for 0%

profile of v8, /device:TPU:1, one launch (start us, length us, event | category | flops | bytes accessed | tf_op | source)
XLA Modules:
  0.0 55.8 jit_solution(12655201435238919174)
XLA Ops:
  0.6 1.2 %shard_map.94 = (f32[8,8,128]{2,1,0:T(8,128)S(1)}, f32[4,64,128]{2,1,0:T(8,128)S(1)}, f32[3,4,64,128]{3,2,1,0:T(8,128)S(1)}) custom-call(f32[1,256]{1,0:T(1,128)} %bitcast.11, f32[8,256]{1,0:T(8,128)} %germs_hbm.1, bf16[32,512]{1,0:T(8,128)(2,1)} %bitcast.10, f32[4,64,128]{2,1,0:T(8,128)} %density_hbm.1, f32[3,4,64,128]{3,2,1,0:T(8,128)} %load_hbm.1), custom_call_target="tpu_custom_call" | custom-call | tf_op jit(solution)/shard_map/pallas_call | solution.py:468
  1.8 10.3 %all_to_all.21.parts_ref = f32[8,8,128]{2,1,0:T(8,128)S(1)} all-to-all(f32[8,8,128]{2,1,0:T(8,128)S(1)} %get-tuple-element.16), channel_id=1, replica_groups=mesh['sample'=8,'space'=32] {'sample'}, dimensions={0} | all-to-all | bytes 65536 | tf_op jit(solution)/shard_map/all_to_all | solution.py:491
  12.1 0.0 copy-start
  12.1 0.0 copy-start.1
  12.2 0.8 %collective-permute-start = (f32[520,128]{1,0:T(8,128)S(1)}, f32[520,128]{1,0:T(8,128)S(1)}, u32[]{:S(2)}, u32[]{:S(2)}) collective-permute-start(f32[520,128]{1,0:T(8,128)S(1)} %get-tuple-element.20), channel_id=1, source_target_pairs={{0,1},{1,0},{2,3},{3,2},{4,5},{5,4},{6,7},{7,6},{8,9},{9,8},{10,11... | collective-permute-start | bytes 798728 | tf_op jit(solution)/shard_map/ppermute | solution.py:503
  13.0 0.0 collective-permute-done.own_ref
  13.0 8.3 %collective-permute-start.1 = (f32[520,128]{1,0:T(8,128)S(1)}, f32[520,128]{1,0:T(8,128)S(1)}, u32[]{:S(2)}, u32[]{:S(2)}) collective-permute-start(f32[520,128]{1,0:T(8,128)S(1)} %collective-permute-done.own_ref), channel_id=1, source_target_pairs={{0,32},{32,0},{64,96},{96,64},{128,160},{160,128},{192,224},{224,1... | collective-permute-start | bytes 798728 | tf_op jit(solution)/shard_map/ppermute | solution.py:504
  21.3 1.2 %collective-permute-done.1.other_ref = f32[520,128]{1,0:T(8,128)S(1)} collective-permute-done((f32[520,128]{1,0:T(8,128)S(1)}, f32[520,128]{1,0:T(8,128)S(1)}, u32[]{:S(2)}, u32[]{:S(2)}) %collective-permute-start.1) | collective-permute-done | bytes 266272 | tf_op jit(solution)/shard_map/ppermute | solution.py:504
  22.5 0.0 copy-done
  22.5 0.0 copy-done.1
  22.5 2.6 %shard_map.96 = (f32[3,7,64,128]{3,2,1,0:T(8,128)S(1)}, f32[3,5,64,128]{3,2,1,0:T(8,128)S(1)}, f32[8,64,128]{2,1,0:T(8,128)S(1)}, f32[32,128]{1,0:T(8,128)S(1)}) custom-call(f32[8,128]{1,0:T(8,128)S(1)} %get-tuple-element.19.sums_ref, f32[4,64,128]{2,1,0:T(8,128)S(1)} %get-tuple-element.17.density_ref, f32[3,4,64,128]{3,2,1,0:T(8,128)S(1)} %get-tuple-element.18.load_ref, ...), custom_call_target="tpu_custom_call" | custom-call | tf_op jit(solution)/shard_map/pallas_call | solution.py:508
  25.1 19.6 %all_to_all.22 = f32[32,1,128]{2,1,0:T(1,128)S(1)} all-to-all(f32[32,1,128]{2,1,0:T(1,128)S(1)} %bitcast.9), channel_id=1, replica_groups=mesh['sample'=8,'space'=32] {'space'}, dimensions={0} | all-to-all | bytes 32768 | tf_op jit(solution)/shard_map/all_to_all | solution.py:527
  44.8 0.9 %shard_map.97 = (f32[8,4,8,128]{3,2,1,0:T(8,128)S(1)}, f32[1,3,4,64,128]{4,3,2,1,0:T(8,128)}) custom-call(f32[32,128]{1,0:T(8,128)S(1)} %bitcast.7, f32[3,7,64,128]{3,2,1,0:T(8,128)S(1)} %get-tuple-element.22.z_ref, f32[3,5,64,128]{3,2,1,0:T(8,128)S(1)} %get-tuple-element.23.y_ref, f32[8,64,128]{2,1,0:T(8,128)S(1)} %get-tuple-element.24.growth_ref, ...), custom_call_target="tpu_custom_call" | custom-call | tf_op jit(solution)/shard_map/pallas_call | solution.py:528
  45.7 9.5 %all_to_all.23.terms_ref = f32[8,4,8,128]{3,2,1,0:T(8,128)S(1)} all-to-all(f32[8,4,8,128]{3,2,1,0:T(8,128)S(1)} %get-tuple-element.26), channel_id=1, replica_groups=mesh['sample'=8,'space'=32] {'sample'}, dimensions={0} | all-to-all | bytes 262144 | tf_op jit(solution)/shard_map/all_to_all | solution.py:539
  55.1 0.6 %shard_map.98 = (f32[4,8,128]{2,1,0:T(8,128)}, f32[1,1]{1,0:T(1,128)}) custom-call(f32[8,4,8,128]{3,2,1,0:T(8,128)S(1)} %all_to_all.23.terms_ref, f32[32,128]{1,0:T(8,128)S(1)} %bitcast.8), custom_call_target="tpu_custom_call" | custom-call | tf_op jit(solution)/shard_map/pallas_call | solution.py:540
  (1 shorter events, 0.0 us)
Async XLA Ops:
  12.1 10.4 %copy-start = (bf16[512,48]{1,0:T(8,128)(2,1)S(1)}, bf16[512,48]{1,0:T(8,128)(2,1)}, u32[]{:S(2)}) copy-start(bf16[512,48]{1,0:T(8,128)(2,1)} %constant.5.clone.spread_zx_ref) | copy-start | bytes 147460
  12.1 10.4 %copy-start.1 = (bf16[128,128]{1,0:T(8,128)(2,1)S(1)}, bf16[128,128]{1,0:T(8,128)(2,1)}, u32[]{:S(2)}) copy-start(bf16[128,128]{1,0:T(8,128)(2,1)} %constant.4.clone.spread_y_ref) | copy-start | bytes 98308
  12.2 0.8 %collective-permute-start = (f32[520,128]{1,0:T(8,128)S(1)}, f32[520,128]{1,0:T(8,128)S(1)}, u32[]{:S(2)}, u32[]{:S(2)}) collective-permute-start(f32[520,128]{1,0:T(8,128)S(1)} %get-tuple-element.20), channel_id=1, source_target_pairs={{0,1},{1,0},{2,3},{3,2},{4,5},{5,4},{6,7},{7,6},{8,9},{9,8},{10,11... | collective-permute-start | bytes 798728 | tf_op jit(solution)/shard_map/ppermute | solution.py:503
  13.0 9.5 %collective-permute-start.1 = (f32[520,128]{1,0:T(8,128)S(1)}, f32[520,128]{1,0:T(8,128)S(1)}, u32[]{:S(2)}, u32[]{:S(2)}) collective-permute-start(f32[520,128]{1,0:T(8,128)S(1)} %collective-permute-done.own_ref), channel_id=1, source_target_pairs={{0,32},{32,0},{64,96},{96,64},{128,160},{160,128},{192,224},{224,1... | collective-permute-start | bytes 798728 | tf_op jit(solution)/shard_map/ppermute | solution.py:504

commit v9 on v8

--- a/solution.py
+++ b/solution.py
@@ -413,22 +413,26 @@
 
 
 def terms_kernel(
-    dots_ref, z_ref, y_ref, growth_ref, density_ref, terms_ref, displacement_hbm, fields, held, sem
+    dots_ref, z_ref, y_ref, growth_ref, density_ref, terms_ref, displacement_hbm, fields, held, sems
 ):
     _, along_z, along_y = solve(dots_ref)
     depth, rows, cols = density_ref.shape
     last_col = lax.broadcasted_iota(jnp.int32, (rows, cols), 1) == cols - 1
     zero_rows = jnp.zeros((8, cols), jnp.float32)
-    for place in range(depth + 1):
-        for comp in range(3):
+    copies = []
+    for comp in range(3):
+        for place in range(depth + 1):
             value = along_z * z_ref[comp, place + 1] + along_y * y_ref[comp, place]
             store_along_y(fields, place, comp, value, last_col)
             if place < depth:
                 held[comp, place] = value
+        copies.append(
+            pltpu.make_async_copy(held.at[comp], displacement_hbm.at[0, comp], sems.at[comp])
+        )
+        copies[-1].start()
+    for place in range(depth + 1):
         for at in range(6):
             fields[place, at, rows : rows + 8] = zero_rows
-    copy = pltpu.make_async_copy(held, displacement_hbm.at[0], sem)
-    copy.start()
     for chunk in range(rows // 8):
         span = pl.ds(chunk * 8, 8)
         lower = load_spread(fields, 0, chunk)
@@ -438,7 +442,8 @@
             share = (-3.0 / 8.0 * UNIT) * dense * dense * growth_ref[place + 2, span]
             terms_ref[chunk, place] = share * modal_energy(element_modes(lower, upper))
             lower = upper
-    copy.wait()
+    for copy in copies:
+        copy.wait()
 
 
 def last_kernel(terms_ref, dots_ref, gradient_ref, compliance_ref):
@@ -532,7 +537,7 @@
         scratch=[
             padded,
             pltpu.VMEM((3, depth, rows, cols), jnp.float32),
-            pltpu.SemaphoreType.DMA,
+            pltpu.SemaphoreType.DMA((3,)),
         ],
         out_specs=[vmem_spec(), pl.BlockSpec(memory_space=pl.ANY)],
     )(dots, z_vec, y_vec, growth, density)

time: 56 us -> 56 us (level)
  no operation moved by 1% of the time
where the time goes in v9:
time: 56 us; the launch traced here: 55.7 us
  blocking collectives  39.4 us (70%)
  starting transfers between devices  9.16 us (16%)
  Pallas kernels  5.3 us (9%)
  waiting for transfers between devices  1.17 us (2%)
  between operations  0.68 us (1%)
    all_to_all x1, blocking collectives, per_device(): dots = lax.all_to_all(dots, 'space', 0, 0, tiled=True)  19.6 us
    all_to_all x1, blocking collectives, per_device(): parts = lax.all_to_all(partial, 'sample', 0, 0, tiled=True)  10.3 us
    all_to_all x1, blocking collectives, per_device(): terms = lax.all_to_all(terms, 'sample', 0, 0, tiled=True)  9.46 us
    ppermute x1, starting transfers between devices, per_device(): other = lax.ppermute(own, 'sample', [(at, at ^ 1) for at in range(samples)])  8.35 us
    pallas_call x1, Pallas kernels, per_device(): call(middle_kernel, [f32(3, depth + 3, rows, cols), f32(3, depth + 1, row...  2.6 us
    ppermute x1, waiting for transfers between devices, per_device(): other = lax.ppermute(own, 'sample', [(at, at ^ 1) for at in range(samples)])  1.17 us
    pallas_call x1, Pallas kernels, per_device(): call(first_kernel, [f32(samples, 2 * cells // 128, 128), held_density, he...  1.16 us
  transfers between devices with their start and end apart: 2, of which 1 were waited for; matrix products, arithmetic and copies ran while one was open for 0% of the time, Pallas kernels for 0%

profile of v9, /device:TPU:1, one launch (start us, length us, event | category | flops | bytes accessed | tf_op | source)
XLA Modules:
  0.0 55.7 jit_solution(13698871316737173508)
XLA Ops:
  0.6 1.2 %shard_map.94 = (f32[8,8,128]{2,1,0:T(8,128)S(1)}, f32[4,64,128]{2,1,0:T(8,128)S(1)}, f32[3,4,64,128]{3,2,1,0:T(8,128)S(1)}) custom-call(f32[1,256]{1,0:T(1,128)} %bitcast.11, f32[8,256]{1,0:T(8,128)} %germs_hbm.1, bf16[32,512]{1,0:T(8,128)(2,1)} %bitcast.10, f32[4,64,128]{2,1,0:T(8,128)} %density_hbm.1, f32[3,4,64,128]{3,2,1,0:T(8,128)} %load_hbm.1), custom_call_target="tpu_custom_call" | custom-call | tf_op jit(solution)/shard_map/pallas_call | solution.py:473
  1.8 10.3 %all_to_all.21.parts_ref = f32[8,8,128]{2,1,0:T(8,128)S(1)} all-to-all(f32[8,8,128]{2,1,0:T(8,128)S(1)} %get-tuple-element.16), channel_id=1, replica_groups=mesh['sample'=8,'space'=32] {'sample'}, dimensions={0} | all-to-all | bytes 65536 | tf_op jit(solution)/shard_map/all_to_all | solution.py:496
  12.1 0.0 copy-start
  12.1 0.0 copy-start.1
  12.2 0.8 %collective-permute-start = (f32[520,128]{1,0:T(8,128)S(1)}, f32[520,128]{1,0:T(8,128)S(1)}, u32[]{:S(2)}, u32[]{:S(2)}) collective-permute-start(f32[520,128]{1,0:T(8,128)S(1)} %get-tuple-element.20), channel_id=1, source_target_pairs={{0,1},{1,0},{2,3},{3,2},{4,5},{5,4},{6,7},{7,6},{8,9},{9,8},{10,11... | collective-permute-start | bytes 798728 | tf_op jit(solution)/shard_map/ppermute | solution.py:508
  13.0 0.0 collective-permute-done.own_ref
  13.0 8.3 %collective-permute-start.1 = (f32[520,128]{1,0:T(8,128)S(1)}, f32[520,128]{1,0:T(8,128)S(1)}, u32[]{:S(2)}, u32[]{:S(2)}) collective-permute-start(f32[520,128]{1,0:T(8,128)S(1)} %collective-permute-done.own_ref), channel_id=1, source_target_pairs={{0,32},{32,0},{64,96},{96,64},{128,160},{160,128},{192,224},{224,1... | collective-permute-start | bytes 798728 | tf_op jit(solution)/shard_map/ppermute | solution.py:509
  21.3 1.2 %collective-permute-done.1.other_ref = f32[520,128]{1,0:T(8,128)S(1)} collective-permute-done((f32[520,128]{1,0:T(8,128)S(1)}, f32[520,128]{1,0:T(8,128)S(1)}, u32[]{:S(2)}, u32[]{:S(2)}) %collective-permute-start.1) | collective-permute-done | bytes 266272 | tf_op jit(solution)/shard_map/ppermute | solution.py:509
  22.5 0.0 copy-done
  22.5 0.0 copy-done.1
  22.5 2.6 %shard_map.96 = (f32[3,7,64,128]{3,2,1,0:T(8,128)S(1)}, f32[3,5,64,128]{3,2,1,0:T(8,128)S(1)}, f32[8,64,128]{2,1,0:T(8,128)S(1)}, f32[32,128]{1,0:T(8,128)S(1)}) custom-call(f32[8,128]{1,0:T(8,128)S(1)} %get-tuple-element.19.sums_ref, f32[4,64,128]{2,1,0:T(8,128)S(1)} %get-tuple-element.17.density_ref, f32[3,4,64,128]{3,2,1,0:T(8,128)S(1)} %get-tuple-element.18.load_ref, ...), custom_call_target="tpu_custom_call" | custom-call | tf_op jit(solution)/shard_map/pallas_call | solution.py:513
  25.1 19.6 %all_to_all.22 = f32[32,1,128]{2,1,0:T(1,128)S(1)} all-to-all(f32[32,1,128]{2,1,0:T(1,128)S(1)} %bitcast.9), channel_id=1, replica_groups=mesh['sample'=8,'space'=32] {'space'}, dimensions={0} | all-to-all | bytes 32768 | tf_op jit(solution)/shard_map/all_to_all | solution.py:532
  44.8 0.9 %shard_map.97 = (f32[8,4,8,128]{3,2,1,0:T(8,128)S(1)}, f32[1,3,4,64,128]{4,3,2,1,0:T(8,128)}) custom-call(f32[32,128]{1,0:T(8,128)S(1)} %bitcast.7, f32[3,7,64,128]{3,2,1,0:T(8,128)S(1)} %get-tuple-element.22.z_ref, f32[3,5,64,128]{3,2,1,0:T(8,128)S(1)} %get-tuple-element.23.y_ref, f32[8,64,128]{2,1,0:T(8,128)S(1)} %get-tuple-element.24.growth_ref, ...), custom_call_target="tpu_custom_call" | custom-call | tf_op jit(solution)/shard_map/pallas_call | solution.py:533
  45.7 9.5 %all_to_all.23.terms_ref = f32[8,4,8,128]{3,2,1,0:T(8,128)S(1)} all-to-all(f32[8,4,8,128]{3,2,1,0:T(8,128)S(1)} %get-tuple-element.26), channel_id=1, replica_groups=mesh['sample'=8,'space'=32] {'sample'}, dimensions={0} | all-to-all | bytes 262144 | tf_op jit(solution)/shard_map/all_to_all | solution.py:544
  55.1 0.6 %shard_map.98 = (f32[4,8,128]{2,1,0:T(8,128)}, f32[1,1]{1,0:T(1,128)}) custom-call(f32[8,4,8,128]{3,2,1,0:T(8,128)S(1)} %all_to_all.23.terms_ref, f32[32,128]{1,0:T(8,128)S(1)} %bitcast.8), custom_call_target="tpu_custom_call" | custom-call | tf_op jit(solution)/shard_map/pallas_call | solution.py:545
  (1 shorter events, 0.0 us)
Async XLA Ops:
  12.1 10.4 %copy-start = (bf16[512,48]{1,0:T(8,128)(2,1)S(1)}, bf16[512,48]{1,0:T(8,128)(2,1)}, u32[]{:S(2)}) copy-start(bf16[512,48]{1,0:T(8,128)(2,1)} %constant.5.clone.spread_zx_ref) | copy-start | bytes 147460
  12.1 10.4 %copy-start.1 = (bf16[128,128]{1,0:T(8,128)(2,1)S(1)}, bf16[128,128]{1,0:T(8,128)(2,1)}, u32[]{:S(2)}) copy-start(bf16[128,128]{1,0:T(8,128)(2,1)} %constant.4.clone.spread_y_ref) | copy-start | bytes 98308
  12.2 0.8 %collective-permute-start = (f32[520,128]{1,0:T(8,128)S(1)}, f32[520,128]{1,0:T(8,128)S(1)}, u32[]{:S(2)}, u32[]{:S(2)}) collective-permute-start(f32[520,128]{1,0:T(8,128)S(1)} %get-tuple-element.20), channel_id=1, source_target_pairs={{0,1},{1,0},{2,3},{3,2},{4,5},{5,4},{6,7},{7,6},{8,9},{9,8},{10,11... | collective-permute-start | bytes 798728 | tf_op jit(solution)/shard_map/ppermute | solution.py:508
  13.0 9.5 %collective-permute-start.1 = (f32[520,128]{1,0:T(8,128)S(1)}, f32[520,128]{1,0:T(8,128)S(1)}, u32[]{:S(2)}, u32[]{:S(2)}) collective-permute-start(f32[520,128]{1,0:T(8,128)S(1)} %collective-permute-done.own_ref), channel_id=1, source_target_pairs={{0,32},{32,0},{64,96},{96,64},{128,160},{160,128},{192,224},{224,1... | collective-permute-start | bytes 798728 | tf_op jit(solution)/shard_map/ppermute | solution.py:509
